TPU v7x, 32 devices: a whole 2x2x4 slice. The times are simulated.
32 devices in a mesh: band: 16 (over z, x, core), dp: 2 (over y).
Axes of the slice: x: 2, y: 2, z: 4, core: 2. Of those that a mesh axis runs over, the one named last changes fastest.
Arguments:
- pixels: bfloat16 [2, 16, 128, 16, 256], P('dp', None, None, 'band'), may hold values from -6 to 6
- wavelengths: int32 [16], replicated, may hold values from 400 to 2499
- band_counts: int32 [2, 16], P('dp'), may hold values from 2 to 16, as said below
- band_mask: int32 [2, 16, 16], P('dp', None, 'band'), may hold values from 0 to 1, as said below
- hyper_qkv: bfloat16 [128, 384], replicated, may hold values from -1 to 1
- hyper_out: bfloat16 [128, 128], replicated, may hold values from -0.5 to 0.5
- hyper_gain1: bfloat16 [128], replicated, may hold values from 0.099609375 to 1.8984375
- hyper_up: bfloat16 [128, 2048], replicated, may hold values from -0.5 to 0.5
- hyper_down: bfloat16 [2048, 128], replicated, may hold values from -0.125 to 0.125
- hyper_gain2: bfloat16 [128], replicated, may hold values from 0.099609375 to 1.8984375
- kernel_gen: bfloat16 [128, 196608], P(None, 'band'), may hold values from -0.03125 to 0.03125
- bias_gen: bfloat16 [128, 768], replicated, may hold values from -0.5 to 0.5
- norm_gain1: bfloat16 [768], replicated, may hold values from 0.099609375 to 1.8984375
- attn_qkv: bfloat16 [768, 2304], P(('band', 'dp')), may hold values from -0.21875 to 0.21875
- attn_out: bfloat16 [768, 768], P(('band', 'dp')), may hold values from -0.625 to 0.625
- norm_gain2: bfloat16 [768], replicated, may hold values from 0.099609375 to 1.8984375
- mlp_up: bfloat16 [768, 3072], P(('band', 'dp')), may hold values from -0.21875 to 0.21875
- mlp_down: bfloat16 [3072, 768], P(('band', 'dp')), may hold values from -0.109375 to 0.109375
- out_grad: bfloat16 [2, 16, 128, 768], P('dp', 'band'), may hold values from -6 to 6
Outputs:
- block_out: bfloat16 [2, 16, 128, 768], P('dp', 'band')
- pixel_grad: bfloat16 [2, 16, 128, 16, 256], P('dp', None, None, 'band')
- grad_hyper_qkv: float32 [128, 384], replicated
- grad_hyper_out: float32 [128, 128], replicated
- grad_hyper_gain1: float32 [128], replicated
- grad_hyper_up: float32 [128, 2048], replicated
- grad_hyper_down: float32 [2048, 128], replicated
- grad_hyper_gain2: float32 [128], replicated
- grad_kernel_gen: float32 [128, 196608], P(None, 'band')
- grad_bias_gen: float32 [128, 768], replicated
- grad_norm_gain1: float32 [768], replicated
- grad_attn_qkv: float32 [768, 2304], P(('band', 'dp'))
- grad_attn_out: float32 [768, 768], P(('band', 'dp'))
- grad_norm_gain2: float32 [768], replicated
- grad_mlp_up: float32 [768, 3072], P(('band', 'dp'))
- grad_mlp_down: float32 [3072, 768], P(('band', 'dp'))
Inputs may be any that keep to these rules, and one draw needn't show every extreme that they name: `wavelengths`: wavelength of each band slot in nanometres. Image i of group g uses band slot b when b < band_counts[g, i] and band_mask[g, i, b] = 1; in every group some image has 16 bands. `band_mask`: in every group the image with 16 bands keeps all of them.
All inputs are finite; a program needn't handle non-finite values.
Results may differ from a plain program's by a relative error of at most 0.014.
Values may be sent and summed in bfloat16 or wider, within the bound.
A program may use at most 256 MiB of HBM per device.

v0:
```python
import math

import jax
import jax.numpy as jnp
from jax import lax
from jax.sharding import PartitionSpec as P

HEADS = 12
HEAD_DIM = 64
HW = 128
HHEADS = 4


PRECISE = lax.Precision.HIGHEST
EPS_BLOCK = 1e-06
EPS_HYPER = 1e-05
GELU_COEF = 0.7978845608028654


def gelu_tanh(tensor):
    return (
        0.5 * tensor * (1.0 + jnp.tanh(GELU_COEF * (tensor + 0.044715 * tensor * tensor * tensor)))
    )


def gelu_slope(tensor):
    tanh_val = jnp.tanh(GELU_COEF * (tensor + 0.044715 * tensor * tensor * tensor))
    return 0.5 * (1.0 + tanh_val) + 0.5 * tensor * (1.0 - tanh_val * tanh_val) * GELU_COEF * (
        1.0 + 3.0 * 0.044715 * tensor * tensor
    )


def layer_norm(tensor, gain_vec, epsilon):
    centred = tensor - jnp.mean(tensor, axis=-1, keepdims=True)
    return (
        centred
        * lax.rsqrt(jnp.mean(centred * centred, axis=-1, keepdims=True) + epsilon)
        * gain_vec
    )


def norm_parts(tensor, gain_vec):
    centred = tensor - jnp.mean(tensor, axis=-1, keepdims=True)
    inverse = lax.rsqrt(jnp.mean(centred * centred, axis=-1, keepdims=True) + EPS_BLOCK)
    unit_rows = centred * inverse
    return (unit_rows * gain_vec, unit_rows, inverse)


def norm_back(grad_rows, gain_vec, unit_rows, inverse):
    scaled = grad_rows * gain_vec
    return inverse * (
        scaled
        - jnp.mean(scaled, axis=-1, keepdims=True)
        - unit_rows * jnp.mean(scaled * unit_rows, axis=-1, keepdims=True)
    )


def wave_embed(wave_ints, token_width):
    half_width = token_width // 2
    frequency = jnp.power(10000.0, -jnp.arange(half_width, dtype=jnp.float32) / half_width)
    angles = wave_ints.astype(jnp.float32)[:, None] * frequency[None, :]
    return jnp.concatenate([jnp.sin(angles), jnp.cos(angles)], axis=1)


def hyper_net(wave_tokens, qkv_weight, out_weight, gain_one, up_weight, down_weight, gain_two):
    tokens, token_width = wave_tokens.shape
    head_size = token_width // HHEADS
    qkv_rows = jnp.dot(wave_tokens, qkv_weight, precision=PRECISE)
    queries = qkv_rows[:, :token_width].reshape(tokens, HHEADS, head_size)
    key_rows = qkv_rows[:, token_width : 2 * token_width].reshape(tokens, HHEADS, head_size)
    value_rows = qkv_rows[:, 2 * token_width :].reshape(tokens, HHEADS, head_size)
    scores = jnp.einsum("nhc,mhc->hnm", queries, key_rows, precision=PRECISE) / math.sqrt(head_size)
    weights_soft = jax.nn.softmax(scores, axis=-1)
    mixed_rows = jnp.einsum("hnm,mhc->nhc", weights_soft, value_rows, precision=PRECISE).reshape(
        tokens, token_width
    )
    first_norm = layer_norm(
        wave_tokens + jnp.dot(mixed_rows, out_weight, precision=PRECISE), gain_one, EPS_HYPER
    )
    inner_act = gelu_tanh(jnp.dot(first_norm, up_weight, precision=PRECISE))
    return layer_norm(
        first_norm + jnp.dot(inner_act, down_weight, precision=PRECISE), gain_two, EPS_HYPER
    )


def body(
    pixels,
    wavelengths,
    band_counts,
    band_mask,
    hyper_qkv,
    hyper_out,
    hyper_gain1,
    hyper_up,
    hyper_down,
    hyper_gain2,
    kernel_gen,
    bias_gen,
    norm_gain1,
    attn_qkv,
    attn_out,
    norm_gain2,
    mlp_up,
    mlp_down,
    out_grad,
):
    f32 = jnp.float32
    b16 = jnp.bfloat16
    band_local = pixels.shape[3]
    pixel_local = pixels[0]
    model_width = bias_gen.shape[1]
    hyper_params = tuple(
        (
            weight.astype(f32)
            for weight in (hyper_qkv, hyper_out, hyper_gain1, hyper_up, hyper_down, hyper_gain2)
        )
    )
    wave_tokens = wave_embed(wavelengths, HW)
    band_code, hyper_pull = jax.vjp(lambda *params: hyper_net(wave_tokens, *params), *hyper_params)
    code_low = band_code.astype(b16)
    column_part = jnp.dot(code_low, kernel_gen, preferred_element_type=f32).astype(b16)
    kernel_rows = lax.all_to_all(column_part, "band", split_axis=0, concat_axis=1, tiled=True)
    kernels = kernel_rows.reshape(band_local, -1, model_width)
    first_band = lax.axis_index("band") * band_local
    own_code = lax.dynamic_slice_in_dim(code_low, first_band, band_local, 0)
    count_row = band_counts[0]
    biases = jnp.dot(own_code, bias_gen, preferred_element_type=f32)
    slot_ids = first_band + jnp.arange(band_local, dtype=jnp.int32)
    active = (slot_ids[None, :] < count_row[:, None]) & (band_mask[0] == 1)
    band_weight = jnp.where(active, lax.rsqrt(count_row.astype(f32))[:, None], f32(0.0))
    pixel_rows = pixel_local
    weight_rows = band_weight
    conv_out = jnp.einsum("inbp,bpd->inbd", pixel_rows, kernels, preferred_element_type=f32)
    residual = lax.psum_scatter(
        jnp.sum((conv_out + biases[None, None]) * weight_rows[:, None, :, None], axis=2),
        "band",
        scatter_dimension=0,
        tiled=True,
    )
    gathered = (
        lax.all_gather(attn_qkv, ("band", "dp"), axis=0, tiled=True),
        lax.all_gather(attn_out, ("band", "dp"), axis=0, tiled=True),
        lax.all_gather(mlp_up, ("band", "dp"), axis=0, tiled=True),
        lax.all_gather(mlp_down, ("band", "dp"), axis=0, tiled=True),
    )
    qkv_full, out_full, up_full, down_full = gathered
    gain_one = norm_gain1.astype(f32)
    gain_two = norm_gain2.astype(f32)
    images, tokens = (residual.shape[0], residual.shape[1])
    score_scale = 1.0 / math.sqrt(HEAD_DIM)
    normed_full, unit_one, inverse_one = norm_parts(residual, gain_one)
    normed_one = normed_full.astype(b16)
    joint_rows = jnp.einsum("ind,de->ine", normed_one, qkv_full, preferred_element_type=f32).astype(
        b16
    )
    queries = joint_rows[..., :model_width].reshape(images, tokens, HEADS, HEAD_DIM)
    key_rows = joint_rows[..., model_width : 2 * model_width].reshape(
        images, tokens, HEADS, HEAD_DIM
    )
    value_rows = joint_rows[..., 2 * model_width :].reshape(images, tokens, HEADS, HEAD_DIM)
    scores = (
        jnp.einsum("inhc,imhc->ihnm", queries, key_rows, preferred_element_type=f32) * score_scale
    )
    row_top = jnp.max(scores, axis=-1, keepdims=True)
    log_total = row_top + jnp.log(jnp.sum(jnp.exp(scores - row_top), axis=-1, keepdims=True))
    probs_full = jnp.exp(scores - log_total)
    probs_low = probs_full.astype(b16)
    mixed_low = (
        jnp.einsum("ihnm,imhc->inhc", probs_low, value_rows, preferred_element_type=f32)
        .reshape(images, tokens, model_width)
        .astype(b16)
    )
    middle = residual + jnp.einsum("ind,de->ine", mixed_low, out_full, preferred_element_type=f32)
    normed_two_full, unit_two, inverse_two = norm_parts(middle, gain_two)
    normed_two = normed_two_full.astype(b16)
    pre_act = jnp.einsum("ind,df->inf", normed_two, up_full, preferred_element_type=f32)
    act_low = gelu_tanh(pre_act).astype(b16)
    result = middle + jnp.einsum("inf,fd->ind", act_low, down_full, preferred_element_type=f32)
    block_out = result.astype(b16)[None]
    qkv_back, out_back, up_back, down_back = (
        lax.all_gather(attn_qkv, ("band", "dp"), axis=0, tiled=True),
        lax.all_gather(attn_out, ("band", "dp"), axis=0, tiled=True),
        lax.all_gather(mlp_up, ("band", "dp"), axis=0, tiled=True),
        lax.all_gather(mlp_down, ("band", "dp"), axis=0, tiled=True),
    )
    grad_top = out_grad[0]
    grad_down = jnp.einsum("inf,ind->fd", act_low, grad_top, preferred_element_type=f32)
    grad_act = jnp.einsum("ind,fd->inf", grad_top, down_back, preferred_element_type=f32)
    grad_pre = (grad_act * gelu_slope(pre_act)).astype(b16)
    grad_up = jnp.einsum("ind,inf->df", normed_two, grad_pre, preferred_element_type=f32)
    grad_normed_two = jnp.einsum("inf,df->ind", grad_pre, up_back, preferred_element_type=f32)
    grad_gain_two = jnp.sum(grad_normed_two * unit_two, axis=(0, 1))
    grad_middle = grad_top.astype(f32) + norm_back(grad_normed_two, gain_two, unit_two, inverse_two)
    grad_branch = grad_middle.astype(b16)
    grad_out_proj = jnp.einsum("ind,ine->de", mixed_low, grad_branch, preferred_element_type=f32)
    grad_mixed = (
        jnp.einsum("ine,de->ind", grad_branch, out_back, preferred_element_type=f32)
        .astype(b16)
        .reshape(images, tokens, HEADS, HEAD_DIM)
    )
    grad_values = jnp.einsum("ihnm,inhc->imhc", probs_low, grad_mixed, preferred_element_type=f32)
    grad_probs = jnp.einsum("inhc,imhc->ihnm", grad_mixed, value_rows, preferred_element_type=f32)
    grad_scores = (
        probs_full * (grad_probs - jnp.sum(grad_probs * probs_full, axis=-1, keepdims=True))
    ).astype(b16)
    grad_queries = (
        jnp.einsum("ihnm,imhc->inhc", grad_scores, key_rows, preferred_element_type=f32)
        * score_scale
    )
    grad_keys = (
        jnp.einsum("ihnm,inhc->imhc", grad_scores, queries, preferred_element_type=f32)
        * score_scale
    )
    grad_joint = jnp.concatenate(
        [
            grad_queries.reshape(images, tokens, model_width),
            grad_keys.reshape(images, tokens, model_width),
            grad_values.reshape(images, tokens, model_width),
        ],
        axis=-1,
    ).astype(b16)
    grad_qkv = jnp.einsum("ind,ine->de", normed_one, grad_joint, preferred_element_type=f32)
    grad_normed_one = jnp.einsum("ine,de->ind", grad_joint, qkv_back, preferred_element_type=f32)
    grad_gain_one = jnp.sum(grad_normed_one * unit_one, axis=(0, 1))
    grad_embed = grad_middle + norm_back(grad_normed_one, gain_one, unit_one, inverse_one)
    grad_embed_low = grad_embed.astype(b16)[None]
    grad_rows = lax.all_gather(grad_embed_low, "band", axis=1, tiled=True)[0].astype(f32)
    weight_rows = band_weight
    pixel_rows = pixel_local
    scaled = grad_rows[:, :, None, :] * weight_rows[:, None, :, None]
    bias_total = jnp.sum(scaled, axis=(0, 1))
    scaled_low = scaled.astype(b16)
    kernel_total = jnp.einsum("inbp,inbd->bpd", pixel_rows, scaled_low, preferred_element_type=f32)
    pixel_part = jnp.einsum(
        "inbd,bpd->inbp", scaled_low, kernels, preferred_element_type=f32
    ).astype(b16)
    pixel_total = pixel_part
    kernel_grad, bias_grad, pixel_total = (kernel_total, bias_total, pixel_total)
    pixel_out = pixel_total[None]
    kernel_grad_low = kernel_grad.reshape(band_local, -1).astype(b16)
    grad_columns = lax.all_to_all(kernel_grad_low, "band", split_axis=1, concat_axis=0, tiled=True)
    grad_kernel_part = jnp.einsum("nh,nc->hc", code_low, grad_columns, preferred_element_type=f32)
    grad_code_part = jnp.einsum("nc,hc->nh", grad_columns, kernel_gen, preferred_element_type=f32)
    bias_back = jnp.einsum("bd,hd->bh", bias_grad, bias_gen.astype(f32), precision=PRECISE)
    grad_code_part = grad_code_part + lax.dynamic_update_slice_in_dim(
        jnp.zeros_like(grad_code_part), bias_back, first_band, 0
    )
    grad_bias_part = jnp.einsum("bh,bd->hd", own_code.astype(f32), bias_grad, precision=PRECISE)
    grad_code, grad_bias_gen, grad_norm_gain1, grad_norm_gain2 = lax.psum(
        (grad_code_part, grad_bias_part, grad_gain_one, grad_gain_two), ("band", "dp")
    )
    grad_kernel_gen = lax.psum(grad_kernel_part.astype(jnp.bfloat16), "dp").astype(jnp.float32)
    hyper_grads = hyper_pull(grad_code)
    shares = (
        lax.psum_scatter(grad_qkv, ("band", "dp"), scatter_dimension=0, tiled=True),
        lax.psum_scatter(grad_out_proj, ("band", "dp"), scatter_dimension=0, tiled=True),
        lax.psum_scatter(grad_up, ("band", "dp"), scatter_dimension=0, tiled=True),
        lax.psum_scatter(grad_down, ("band", "dp"), scatter_dimension=0, tiled=True),
    )
    return (
        block_out,
        pixel_out,
        hyper_grads[0],
        hyper_grads[1],
        hyper_grads[2],
        hyper_grads[3],
        hyper_grads[4],
        hyper_grads[5],
        grad_kernel_gen,
        grad_bias_gen,
        grad_norm_gain1,
        shares[0],
        shares[1],
        grad_norm_gain2,
        shares[2],
        shares[3],
    )


def solution(mesh):
    placed = (
        P("dp", None, None, "band", None),
        P(),
        P("dp", None),
        P("dp", None, "band"),
        P(),
        P(),
        P(),
        P(),
        P(),
        P(),
        P(None, "band"),
        P(),
        P(),
        P(("band", "dp"), None),
        P(("band", "dp"), None),
        P(),
        P(("band", "dp"), None),
        P(("band", "dp"), None),
        P("dp", "band", None, None),
    )
    return jax.shard_map(
        body,
        mesh=mesh,
        in_specs=placed,
        out_specs=(
            P("dp", "band", None, None),
            P("dp", None, None, "band", None),
            P(),
            P(),
            P(),
            P(),
            P(),
            P(),
            P(None, "band"),
            P(),
            P(),
            P(("band", "dp"), None),
            P(("band", "dp"), None),
            P(),
            P(("band", "dp"), None),
            P(("band", "dp"), None),
        ),
        check_vma=False,
    )
```

profile of v0, /device:TPU:0, one launch (start us, length us, event | category | flops | bytes accessed | tf_op | source)
XLA Modules:
  0.0 975.2 jit_solution(1993503164514235203)
XLA Ops:
  23.7 7.4 all-to-all-start
  32.9 10.3 %all-to-all-done = bf16[16,2,6144]{2,1,0:T(2,128)(2,1)S(1)} async-done(((bf16[16,2,6144]{2,1,0:T(2,128)(2,1)}), bf16[16,2,6144]{2,1,0:T(2,128)(2,1)S(1)}, u32[]{:S(2)}, u32[]{:S(2)}) %all-to-all-start) | async-done | bytes 393248 | tf_op jit(solution)/shard_map/all_to_all | solution.py:122
  48.7 5.7 fusion.6
  58.1 86.3 %reduce-scatter.6.cloned.1.call-done = f32[1,128,768]{1,2,0:T(8,128)} async-done(((f32[16,128,768]{1,2,0:T(8,128)}), f32[1,128,768]{1,2,0:T(8,128)}) %reduce-scatter.6.cloned.1.call-update) | async-done | bytes 393232 | tf_op jit(solution)/shard_map/reduce_scatter | solution.py:134
  157.4 30.1 %all-gather.9.cloned.1.call-done = bf16[768,768]{1,0:T(8,128)(2,1)} async-done(((bf16[24,768]{1,0:T(8,128)(2,1)}), bf16[768,768]{1,0:T(8,128)(2,1)}) %all-gather.9.cloned.1.call-update) | async-done | bytes 1179664 | tf_op jit(solution)/shard_map/all_gather | solution.py:142
  190.8 62.7 %all-gather.11.cloned.1.call-done = bf16[768,3072]{1,0:T(8,128)(2,1)} async-done(((bf16[24,3072]{1,0:T(8,128)(2,1)}), bf16[768,3072]{1,0:T(8,128)(2,1)}) %all-gather.11.cloned.1.call-update) | async-done | bytes 4718608 | tf_op jit(solution)/shard_map/all_gather | solution.py:143
  253.5 4.5 fusion.125
  258.0 60.9 %all-gather.13.cloned.1.call-done = bf16[3072,768]{1,0:T(8,128)(2,1)} async-done(((bf16[96,768]{1,0:T(8,128)(2,1)}), bf16[3072,768]{1,0:T(8,128)(2,1)}) %all-gather.13.cloned.1.call-update) | async-done | bytes 4718608 | tf_op jit(solution)/shard_map/all_gather | solution.py:144
  319.0 4.8 fusion.7
  340.3 43.6 %all-gather.15.cloned.1.call-done = bf16[16,128,768]{2,1,0:T(8,128)(2,1)} async-done(((bf16[1,128,768]{2,1,0:T(8,128)(2,1)}), bf16[16,128,768]{2,1,0:T(8,128)(2,1)}) %all-gather.15.cloned.1.call-update) | async-done | bytes 3145744 | tf_op jit(solution)/shard_map/all_gather | solution.py:227
  383.8 4.2 fusion.17
  393.2 4.8 reduce.22
  400.1 16.4 %all_to_all.26 = bf16[16,2,6144]{2,1,0:T(2,128)(2,1)} all-to-all(bf16[16,2,6144]{2,1,0:T(2,128)(2,1)} %reshape.586), channel_id=1, replica_groups=mesh['band'=16,'dp'=2] {'band'}, dimensions={0} | all-to-all | bytes 786432 | tf_op jit(solution)/shard_map/all_to_all | solution.py:241
  432.6 5.2 fusion.41
  438.7 6.6 fusion.48
  446.4 6.3 fusion.123
  455.9 5.8 fusion.23
  472.5 39.1 %all-reduce.3 = (f32[16,128]{1,0:T(8,128)S(1)}, f32[768]{0:T(1024)}, f32[768]{0:T(1024)}) all-reduce(f32[16,128]{1,0:T(8,128)S(1)} %add.150, f32[768]{0:T(1024)S(1)} %copy-done.71, f32[768]{0:T(1024)S(1)} %copy-done.53), channel_id=1, replica_groups=mesh['band'=16,'dp'=2] {'band','dp'}, use_global_device_ids=true, to_apply=%region_19.20 | all-reduce | flops 3584 | bytes 28672 | tf_op jit(solution)/shard_map/psum | solution.py:249
  536.4 5.3 convert_element_type.217
  541.7 16.8 %reduce-scatter.10.cloned.1.call-done = f32[24,768]{1,0:T(8,128)} async-done(((f32[768,768]{1,0:T(8,128)}), f32[24,768]{1,0:T(8,128)}) %reduce-scatter.10.cloned.1.call-update) | async-done | bytes 73744 | tf_op jit(solution)/shard_map/reduce_scatter | solution.py:256
  558.5 97.5 %all-reduce.9.cloned.1.call-done = f32[128,768]{1,0:T(8,128)} async-done(((f32[128,768]{1,0:T(8,128)}), f32[128,768]{1,0:T(8,128)}) %all-reduce.9.cloned.1.call-update) | async-done | bytes 393232 | tf_op jit(solution)/shard_map/psum | solution.py:249
  656.1 26.8 %reduce-scatter.8.cloned.1.call-done = f32[24,2304]{1,0:T(8,128)} async-done(((f32[768,2304]{1,0:T(8,128)}), f32[24,2304]{1,0:T(8,128)}) %reduce-scatter.8.cloned.1.call-update) | async-done | bytes 221200 | tf_op jit(solution)/shard_map/reduce_scatter | solution.py:255
  682.8 142.2 %reduce-scatter.14.cloned.1.call-done = f32[96,768]{1,0:T(8,128)} async-done(((f32[3072,768]{1,0:T(8,128)}), f32[96,768]{1,0:T(8,128)}) %reduce-scatter.14.cloned.1.call-update) | async-done | bytes 294928 | tf_op jit(solution)/shard_map/reduce_scatter | solution.py:258
  825.0 140.9 %reduce-scatter.12.cloned.1.call-done = f32[24,3072]{1,0:T(8,128)} async-done(((f32[768,3072]{1,0:T(8,128)}), f32[24,3072]{1,0:T(8,128)}) %reduce-scatter.12.cloned.1.call-update) | async-done | bytes 294928 | tf_op jit(solution)/shard_map/reduce_scatter | solution.py:257
  (305 shorter events, 124.4 us)
Async XLA Ops:
  23.7 19.6 %all-to-all-start = ((bf16[16,2,6144]{2,1,0:T(2,128)(2,1)}), bf16[16,2,6144]{2,1,0:T(2,128)(2,1)S(1)}, u32[]{:S(2)}, u32[]{:S(2)}) async-start(bf16[16,2,6144]{2,1,0:T(2,128)(2,1)} %reshape.584), calls=%async_computation | async-start | bytes 786432 | tf_op jit(solution)/shard_map/all_to_all | solution.py:122
  31.0 113.3 %reduce-scatter.6.cloned.1.call-start = ((), (), s32[]{:S(2)}) async-start(), calls=%async_computation.7 | async-start | bytes 6684672 | tf_op jit(solution)/shard_map/reduce_scatter | solution.py:134
  54.5 92.2 %all-gather.7.cloned.1.call-start = ((), (), s32[]{:S(2)}) async-start(), calls=%async_computation.8 | async-start | bytes 3649536 | tf_op jit(solution)/shard_map/all_gather | solution.py:141
  55.1 132.4 %all-gather.9.cloned.1.call-start = ((), (), s32[]{:S(2)}) async-start(), calls=%async_computation.9 | async-start | bytes 1216512 | tf_op jit(solution)/shard_map/all_gather | solution.py:142
  55.7 197.8 %all-gather.11.cloned.1.call-start = ((), (), s32[]{:S(2)}) async-start(), calls=%async_computation.10 | async-start | bytes 4866048 | tf_op jit(solution)/shard_map/all_gather | solution.py:143
  56.2 262.7 %all-gather.13.cloned.1.call-start = ((), (), s32[]{:S(2)}) async-start(), calls=%async_computation.11 | async-start | bytes 4866048 | tf_op jit(solution)/shard_map/all_gather | solution.py:144
  57.0 326.9 %all-gather.15.cloned.1.call-start = ((), (), s32[]{:S(2)}) async-start(), calls=%async_computation.18 | async-start | bytes 3342336 | tf_op jit(solution)/shard_map/all_gather | solution.py:227
  340.0 196.4 %all-reduce.7.cloned.1.call-start = ((), (), s32[]{:S(2)}) async-start(), calls=%async_computation.12 | async-start | bytes 6291456 | tf_op jit(solution)/shard_map/psum | solution.py:252
  423.8 134.8 %reduce-scatter.10.cloned.1.call-start = ((), (), s32[]{:S(2)}) async-start(), calls=%async_computation.15 | async-start | bytes 2433024 | tf_op jit(solution)/shard_map/reduce_scatter | solution.py:256
  426.8 229.3 %all-reduce.9.cloned.1.call-start = ((), (), s32[]{:S(2)}) async-start(), calls=%async_computation.13 | async-start | bytes 786432 | tf_op jit(solution)/shard_map/psum | solution.py:249
  432.6 250.3 %reduce-scatter.8.cloned.1.call-start = ((), (), s32[]{:S(2)}) async-start(), calls=%async_computation.14 | async-start | bytes 7299072 | tf_op jit(solution)/shard_map/reduce_scatter | solution.py:255
  437.8 387.2 %reduce-scatter.14.cloned.1.call-start = ((), (), s32[]{:S(2)}) async-start(), calls=%async_computation.17 | async-start | bytes 9732096 | tf_op jit(solution)/shard_map/reduce_scatter | solution.py:258
  445.4 520.5 %reduce-scatter.12.cloned.1.call-start = ((), (), s32[]{:S(2)}) async-start(), calls=%async_computation.16 | async-start | bytes 9732096 | tf_op jit(solution)/shard_map/reduce_scatter | solution.py:257
  469.8 41.8 %copy-start.31 = (f32[16,128]{1,0:T(8,128)S(1)}, f32[16,128]{1,0:T(8,128)}, u32[]{:S(2)}) copy-start(f32[16,128]{1,0:T(8,128)} %copy-done.30) | copy-start | bytes 24580
  469.8 41.8 %copy-start.64 = (f32[16]{0:T(128)S(1)}, f32[16]{0:T(128)}, u32[]{:S(2)}) copy-start(f32[16]{0:T(128)} %copy-done.63) | copy-start | bytes 196
  469.8 41.8 %copy-start.68 = (f32[128]{0:T(128)S(1)}, f32[128]{0:T(128)}, u32[]{:S(2)}) copy-start(f32[128]{0:T(128)} %copy-done.67) | copy-start | bytes 1540
  469.9 42.5 %copy-start.80 = (f32[16]{0:T(128)S(1)}, f32[16]{0:T(128)}, u32[]{:S(2)}) copy-start(f32[16]{0:T(128)} %copy-done.79) | copy-start | bytes 196
  469.9 42.7 %copy-start.18 = (f32[16,2048]{1,0:T(8,128)S(1)}, f32[16,2048]{1,0:T(8,128)}, u32[]{:S(2)}) copy-start(f32[16,2048]{1,0:T(8,128)} %copy-done.17) | copy-start | bytes 393220
  472.1 48.0 %copy-start.27 = (f32[4,16,16]{1,2,0:T(8,128)S(1)}, f32[4,16,16]{1,2,0:T(8,128)}, u32[]{:S(2)}) copy-start(f32[4,16,16]{1,2,0:T(8,128)} %copy-done.26) | copy-start | bytes 12292
  472.1 52.5 %copy-start.35 = (f32[16,4,32]{2,1,0:T(4,128)S(1)}, f32[16,4,32]{2,1,0:T(4,128)}, u32[]{:S(2)}) copy-start(f32[16,4,32]{2,1,0:T(4,128)} %copy-done.34) | copy-start | bytes 24580
  472.1 54.2 %copy-start.33 = (f32[16,4,32]{2,1,0:T(4,128)S(1)}, f32[16,4,32]{2,1,0:T(4,128)}, u32[]{:S(2)}) copy-start(f32[16,4,32]{2,1,0:T(4,128)} %copy-done.32) | copy-start | bytes 24580
  472.1 55.3 %copy-start.38 = (f32[16,64]{1,0:T(8,128)S(1)}, f32[16,64]{1,0:T(8,128)}, u32[]{:S(2)}) copy-start(f32[16,64]{1,0:T(8,128)} %copy-done.37) | copy-start | bytes 12292
  472.2 55.3 %copy-start.40 = (f32[16,64]{1,0:T(8,128)S(1)}, f32[16,64]{1,0:T(8,128)}, u32[]{:S(2)}) copy-start(f32[16,64]{1,0:T(8,128)} %copy-done.39) | copy-start | bytes 12292
  472.4 56.9 %copy-start.42 = (f32[16,128]{1,0:T(8,128)S(1)}, f32[16,128]{1,0:T(8,128)}, u32[]{:S(2)}) copy-start(f32[16,128]{1,0:T(8,128)} %copy-done.41) | copy-start | bytes 24580
  (70 other events, 331.0 us)
Sparse Core Ops, SparseCore 0:
  54.6 89.7 reduce-scatter.5
  340.2 43.6 all-gather.14
  423.9 85.7 all-reduce.6
  514.9 141.1 all-reduce.8
Sparse Core Ops, SparseCore 1:
  58.3 72.9 all-gather.6
  134.5 52.9 all-gather.8
  190.7 62.7 all-gather.10
  256.8 62.1 all-gather.12
  431.3 127.2 reduce-scatter.9
  564.8 118.0 reduce-scatter.7
  690.2 134.8 reduce-scatter.13
  831.3 134.5 reduce-scatter.11
where the time goes:
time: 983 us; the launch traced here: 975 us
  waiting for transfers between devices  720 us (73%)
  matrix products  98.3 us (10%)
  blocking collectives  55.5 us (6%)
  local copies, waits for them, and re-layouts  43.5 us (4%)
  other arithmetic  32.3 us (3%)
  between operations  16.8 us (2%)
    reduce_scatter x1, waiting for transfers between devices, body(): lax.psum_scatter(grad_down, ('band', 'dp'), scatter_dimension=0, tiled=True)  142 us
    reduce_scatter x1, waiting for transfers between devices, body(): lax.psum_scatter(grad_up, ('band', 'dp'), scatter_dimension=0, tiled=True)  141 us
    psum x1, waiting for transfers between devices, body(): lax.psum((grad_code_part, grad_bias_part, grad_gain_one, grad_gain_two),...  97.5 us
    reduce_scatter x1, waiting for transfers between devices, body(): lax.psum_scatter(jnp.sum((conv_out + biases[None, None]) * weight_rows[:,...  86.3 us
    all_gather x1, waiting for transfers between devices, body(): lax.all_gather(mlp_up, ('band', 'dp'), axis=0, tiled=True)  62.7 us
    all_gather x1, waiting for transfers between devices, body(): lax.all_gather(mlp_down, ('band', 'dp'), axis=0, tiled=True)  60.9 us
    all_gather x1, waiting for transfers between devices, body(): lax.all_gather(grad_embed_low, 'band', axis=1, tiled=True)[0].astype(f32)  43.6 us
    psum x1, blocking collectives, body(): lax.psum((grad_code_part, grad_bias_part, grad_gain_one, grad_gain_two),...  39.1 us
  transfers between devices with their start and end apart: 13, of which 11 were waited for; matrix products, arithmetic and copies ran while one was open for 10% of the time, Pallas kernels for 0%

commit v1 on v0

--- a/solution.py
+++ b/solution.py
@@ -1,8 +1,11 @@
+import functools
 import math
 
 import jax
 import jax.numpy as jnp
 from jax import lax
+from jax.experimental import pallas as pl
+from jax.experimental.pallas import tpu as pltpu
 from jax.sharding import PartitionSpec as P
 
 HEADS = 12
@@ -81,6 +84,231 @@
     return layer_norm(
         first_norm + jnp.dot(inner_act, down_weight, precision=PRECISE), gain_two, EPS_HYPER
     )
+
+
+MESH = pl.DeviceIdType.MESH
+GATHER_ORDERS = ("zxy", "xzy", "yzx", "zyx", "xzy", "yzx")
+
+
+def place():
+    band = lax.axis_index("band")
+    return (band // 4, (band // 2) % 2, band % 2, lax.axis_index("dp"))
+
+
+def device(z, x, core, y):
+    return (z * 4 + x * 2 + core, y)
+
+
+def slot(z, x, core, y):
+    return (z * 4 + x * 2 + core) * 2 + y
+
+
+def when(cond, run):
+    if cond is True:
+        run()
+    else:
+        pl.when(cond)(run)
+
+
+def both(first, second):
+    return second if first is True else first & second
+
+
+def meet_neighbours():
+    z, x, core, y = place()
+    barrier = pltpu.get_barrier_semaphore()
+    near = [
+        (device(z, x, 1 - core, y), True),
+        (device(z, 1 - x, core, y), True),
+        (device(z, x, core, 1 - y), True),
+        (device(z + 1, x, core, y), z < 3),
+        (device(z - 1, x, core, y), z > 0),
+    ]
+    for target, cond in near:
+        when(
+            cond,
+            lambda target=target: pl.semaphore_signal(
+                barrier, inc=1, device_id=target, device_id_type=MESH
+            ),
+        )
+    pl.semaphore_wait(barrier, 5 - z // 3 - (3 - z) // 3)
+
+
+class Gather:
+    def __init__(self, held, rows, orders, send_sem, recv_sem, pair_send, pair_recv):
+        self.held, self.rows, self.orders = held, rows, orders
+        self.send_sem, self.recv_sem = send_sem, recv_sem
+        self.pair_send, self.pair_recv = pair_send, pair_recv
+        self.z, self.x, self.core, self.y = place()
+        self.sends = []
+        self.count = [0] * len(orders)
+
+    def view(self, chunk, where):
+        return self.held.at[where, pl.ds(chunk * self.rows, self.rows)]
+
+    def send(self, chunk, block, dim, cond, direction=0):
+        z, x, core, y = self.z, self.x, self.core, self.y
+        if dim == "x":
+            targets = [(device(z, 1 - x, core, y), cond)]
+        elif dim == "y":
+            targets = [(device(z, x, core, 1 - y), cond)]
+        else:
+            targets = []
+            if direction >= 0:
+                targets.append((device(z + 1, x, core, y), both(cond, z < 3)))
+            if direction <= 0:
+                targets.append((device(z - 1, x, core, y), both(cond, z > 0)))
+        src = self.view(chunk, slot(block[0], block[1], core, block[2]))
+        rail = block[0] * 4 + block[1] * 2 + block[2]
+        for target, needed in targets:
+            copy = pltpu.make_async_remote_copy(
+                src_ref=src,
+                dst_ref=src,
+                send_sem=self.send_sem.at[chunk, self.count[chunk]],
+                recv_sem=self.recv_sem.at[chunk, rail],
+                device_id=target,
+                device_id_type=MESH,
+            )
+            self.count[chunk] += 1
+            when(needed, copy.start)
+            self.sends.append((needed, copy))
+
+    def pair(self, chunk, block, core):
+        src = self.view(chunk, slot(block[0], block[1], core, block[2]))
+        rail = block[0] * 4 + block[1] * 2 + block[2]
+        return pltpu.make_async_remote_copy(
+            src_ref=src,
+            dst_ref=src,
+            send_sem=self.pair_send.at[chunk, rail],
+            recv_sem=self.pair_recv.at[chunk, rail],
+            device_id=device(self.z, self.x, 1 - self.core, self.y),
+            device_id_type=MESH,
+        )
+
+    def start(self, chunk):
+        own = (self.z, self.x, self.y)
+        for dim in self.orders[chunk]:
+            self.send(chunk, own, dim, True)
+        self.pair(chunk, own, self.core).start()
+
+    def events(self, chunk):
+        held, found = [(0, 0, 0, 0, 0.0)], []
+        for dim in self.orders[chunk]:
+            clock, new = 0.0, []
+            ordered = sorted(held, key=lambda item: item[4])
+            if dim == "z":
+                for dist in (1, 2, 3):
+                    for item in ordered:
+                        clock = max(clock, item[4]) + 1.0
+                        new += [(dist, way, item[2], item[3], clock) for way in (1, -1)]
+            else:
+                for item in ordered:
+                    clock = max(clock, item[4]) + 1.0
+                    flip = (1, item[3]) if dim == "x" else (item[2], 1)
+                    new.append((item[0], item[1], *flip, clock))
+            found += [(item[4], chunk, dim, item) for item in new]
+            held = held + new
+        return found
+
+    def arrive(self, chunk, dim, item):
+        dist, way, flip_x, flip_y, _ = item
+        cond = True
+        if way == 1:
+            cond = self.z >= dist
+        elif way == -1:
+            cond = self.z + dist <= 3
+        block = (
+            self.z - dist * way,
+            1 - self.x if flip_x else self.x,
+            1 - self.y if flip_y else self.y,
+        )
+        src = self.view(chunk, slot(block[0], block[1], self.core, block[2]))
+        rail = block[0] * 4 + block[1] * 2 + block[2]
+        arriving = pltpu.make_async_remote_copy(
+            src_ref=src,
+            dst_ref=src,
+            send_sem=self.send_sem.at[chunk, 0],
+            recv_sem=self.recv_sem.at[chunk, rail],
+            device_id=device(self.z, self.x, 1 - self.core, self.y),
+            device_id_type=MESH,
+        )
+        when(cond, arriving.wait_recv)
+        if dim == "z":
+            self.send(chunk, block, "z", cond, way)
+        order = self.orders[chunk]
+        for later in order[order.index(dim) + 1 :]:
+            self.send(chunk, block, later, cond)
+        when(cond, self.pair(chunk, block, self.core).start)
+
+    def finish(self):
+        for needed, copy in self.sends:
+            when(needed, copy.wait_send)
+        for chunk in range(len(self.orders)):
+            for rail in range(16):
+                block = (rail // 4, (rail // 2) % 2, rail % 2)
+                self.pair(chunk, block, self.core).wait_send()
+                self.pair(chunk, block, 1 - self.core).wait_recv()
+
+
+def gather_kernel(shard, whole, held, local_sem, *sems):
+    rows = held.shape[1] // len(GATHER_ORDERS)
+    own = pltpu.make_async_copy(shard, held.at[slot(*place())], local_sem)
+    own.start()
+    own.wait()
+    meet_neighbours()
+    gather = Gather(held, rows, GATHER_ORDERS, *sems)
+    events = []
+    for chunk in range(len(GATHER_ORDERS)):
+        gather.start(chunk)
+        events += gather.events(chunk)
+    for _, chunk, dim, item in sorted(events, key=lambda event: event[:2]):
+        gather.arrive(chunk, dim, item)
+    gather.finish()
+    out = pltpu.make_async_copy(held, whole, local_sem)
+    out.start()
+    out.wait()
+
+
+def gather_weights(attn_qkv, attn_out, mlp_up, mlp_down):
+    if (lax.axis_size("band"), lax.axis_size("dp")) != (16, 2):
+        return tuple(
+            lax.all_gather(weight, ("band", "dp"), axis=0, tiled=True)
+            for weight in (attn_qkv, attn_out, mlp_up, mlp_down)
+        )
+    width = attn_out.shape[1]
+    devices = lax.axis_size("band") * lax.axis_size("dp")
+
+    def stack(weight):
+        parts = weight.shape[1] // width
+        return weight.reshape(weight.shape[0], parts, width).transpose(1, 0, 2).reshape(-1, width)
+
+    shard = jnp.concatenate([stack(w) for w in (attn_qkv, attn_out, mlp_up, mlp_down)], axis=0)
+    chunks = len(GATHER_ORDERS)
+    whole = pl.pallas_call(
+        gather_kernel,
+        out_shape=jax.ShapeDtypeStruct((devices, *shard.shape), shard.dtype),
+        in_specs=[pl.BlockSpec(memory_space=pl.ANY)],
+        out_specs=pl.BlockSpec(memory_space=pl.ANY),
+        scratch_shapes=[
+            pltpu.VMEM((devices, *shard.shape), shard.dtype),
+            pltpu.SemaphoreType.DMA,
+            pltpu.SemaphoreType.DMA((chunks, 40)),
+            pltpu.SemaphoreType.DMA((chunks, 16)),
+            pltpu.SemaphoreType.DMA((chunks, 16)),
+            pltpu.SemaphoreType.DMA((chunks, 16)),
+        ],
+        compiler_params=pltpu.CompilerParams(
+            collective_id=0, has_side_effects=True, vmem_limit_bytes=56 * 2**20
+        ),
+        name="gather_weights",
+    )(shard)
+    out, at = [], 0
+    for weight in (attn_qkv, attn_out, mlp_up, mlp_down):
+        rows, parts = weight.shape[0], weight.shape[1] // width
+        piece = whole[:, at : at + rows * parts].reshape(devices, parts, rows, width)
+        out.append(piece.transpose(0, 2, 1, 3).reshape(devices * rows, parts * width))
+        at += rows * parts
+    return tuple(out)
 
 
 def body(
@@ -137,12 +365,7 @@
         scatter_dimension=0,
         tiled=True,
     )
-    gathered = (
-        lax.all_gather(attn_qkv, ("band", "dp"), axis=0, tiled=True),
-        lax.all_gather(attn_out, ("band", "dp"), axis=0, tiled=True),
-        lax.all_gather(mlp_up, ("band", "dp"), axis=0, tiled=True),
-        lax.all_gather(mlp_down, ("band", "dp"), axis=0, tiled=True),
-    )
+    gathered = gather_weights(attn_qkv, attn_out, mlp_up, mlp_down)
     qkv_full, out_full, up_full, down_full = gathered
     gain_one = norm_gain1.astype(f32)
     gain_two = norm_gain2.astype(f32)
@@ -177,12 +400,7 @@
     act_low = gelu_tanh(pre_act).astype(b16)
     result = middle + jnp.einsum("inf,fd->ind", act_low, down_full, preferred_element_type=f32)
     block_out = result.astype(b16)[None]
-    qkv_back, out_back, up_back, down_back = (
-        lax.all_gather(attn_qkv, ("band", "dp"), axis=0, tiled=True),
-        lax.all_gather(attn_out, ("band", "dp"), axis=0, tiled=True),
-        lax.all_gather(mlp_up, ("band", "dp"), axis=0, tiled=True),
-        lax.all_gather(mlp_down, ("band", "dp"), axis=0, tiled=True),
-    )
+    qkv_back, out_back, up_back, down_back = gathered
     grad_top = out_grad[0]
     grad_down = jnp.einsum("inf,ind->fd", act_low, grad_top, preferred_element_type=f32)
     grad_act = jnp.einsum("ind,fd->inf", grad_top, down_back, preferred_element_type=f32)
@@ -237,26 +455,27 @@
     pixel_total = pixel_part
     kernel_grad, bias_grad, pixel_total = (kernel_total, bias_total, pixel_total)
     pixel_out = pixel_total[None]
-    kernel_grad_low = kernel_grad.reshape(band_local, -1).astype(b16)
+    kernel_grad_low = lax.psum(kernel_grad.astype(b16), "dp").reshape(band_local, -1)
     grad_columns = lax.all_to_all(kernel_grad_low, "band", split_axis=1, concat_axis=0, tiled=True)
     grad_kernel_part = jnp.einsum("nh,nc->hc", code_low, grad_columns, preferred_element_type=f32)
     grad_code_part = jnp.einsum("nc,hc->nh", grad_columns, kernel_gen, preferred_element_type=f32)
     bias_back = jnp.einsum("bd,hd->bh", bias_grad, bias_gen.astype(f32), precision=PRECISE)
-    grad_code_part = grad_code_part + lax.dynamic_update_slice_in_dim(
+    grad_code_part = 0.5 * grad_code_part + lax.dynamic_update_slice_in_dim(
         jnp.zeros_like(grad_code_part), bias_back, first_band, 0
     )
     grad_bias_part = jnp.einsum("bh,bd->hd", own_code.astype(f32), bias_grad, precision=PRECISE)
     grad_code, grad_bias_gen, grad_norm_gain1, grad_norm_gain2 = lax.psum(
         (grad_code_part, grad_bias_part, grad_gain_one, grad_gain_two), ("band", "dp")
     )
-    grad_kernel_gen = lax.psum(grad_kernel_part.astype(jnp.bfloat16), "dp").astype(jnp.float32)
+    grad_kernel_gen = grad_kernel_part
     hyper_grads = hyper_pull(grad_code)
     shares = (
-        lax.psum_scatter(grad_qkv, ("band", "dp"), scatter_dimension=0, tiled=True),
-        lax.psum_scatter(grad_out_proj, ("band", "dp"), scatter_dimension=0, tiled=True),
-        lax.psum_scatter(grad_up, ("band", "dp"), scatter_dimension=0, tiled=True),
-        lax.psum_scatter(grad_down, ("band", "dp"), scatter_dimension=0, tiled=True),
-    )
+        lax.psum_scatter(grad_qkv.astype(b16), ("band", "dp"), scatter_dimension=0, tiled=True),
+        lax.psum_scatter(grad_out_proj.astype(b16), ("band", "dp"), scatter_dimension=0, tiled=True),
+        lax.psum_scatter(grad_up.astype(b16), ("band", "dp"), scatter_dimension=0, tiled=True),
+        lax.psum_scatter(grad_down.astype(b16), ("band", "dp"), scatter_dimension=0, tiled=True),
+    )
+    shares = tuple(share.astype(f32) for share in shares)
     return (
         block_out,
         pixel_out,

time: 983 us -> 853 us (0.87)
  waiting for transfers between devices: 720 us -> 512 us
  Pallas kernels: 0 us -> 85.2 us
  blocking collectives: 55.5 us -> 40.4 us
  local copies, waits for them, and re-layouts: 43.5 us -> 58.4 us
  matrix products: 98.3 us -> 86.6 us
    all_gather x4 -> x0, waiting for transfers between devices: 154 us -> none  [the longest x1 62.7 us: body(): lax.all_gather(mlp_up, ('band', 'dp'), axis=0, tiled=True)]
    reduce_scatter x1, waiting for transfers between devices: 86.3 us -> 0.01 us  [body(): lax.psum_scatter(jnp.sum((conv_out + biases[None, None]) * weight_rows[:,...]
    pallas_call x0 -> x1, Pallas kernels: none -> 85.2 us  [gather_weights(): pl.pallas_call(gather_kernel, out_shape=jax.ShapeDtypeStruct((devices, *s...]
    reduce_scatter x4, waiting for transfers between devices: 327 us -> 377 us  [the longest x1 111 us: body(): lax.psum_scatter(grad_up.astype(b16), ('band', 'dp'), scatter_dimension=0...]
    psum x1, waiting for transfers between devices: 97.5 us -> 62.2 us  [body(): lax.psum((grad_code_part, grad_bias_part, grad_gain_one, grad_gain_two),...]
    psum x1, waiting for transfers between devices: 0.01 us -> 25.4 us  [body(): lax.psum(kernel_grad.astype(b16), 'dp').reshape(band_local, -1)]
    all_to_all x1 -> x0, blocking collectives: 16.4 us -> none  [body(): lax.all_to_all(kernel_grad_low, 'band', split_axis=1, concat_axis=0, tile...]
    unnamed x170 -> x190, local copies, waits for them, and re-layouts: 23.8 us -> 23.6 us
  transfers between devices with their start and end apart: 13 -> 10, of which waited for: 11 -> 8; matrix products, arithmetic and copies ran while one was open for 10% -> 13% of each run, Pallas kernels for 0% -> 10%
where the time goes in v1:
time: 853 us; the launch traced here: 845 us
  waiting for transfers between devices  512 us (60%)
  matrix products  86.6 us (10%)
  Pallas kernels  85.2 us (10%)
  local copies, waits for them, and re-layouts  58.4 us (7%)
  blocking collectives  40.4 us (5%)
  other arithmetic  32.4 us (4%)
  between operations  15.8 us (2%)
  starting transfers between devices  13.8 us (2%)
    reduce_scatter x1, waiting for transfers between devices, body(): lax.psum_scatter(grad_up.astype(b16), ('band', 'dp'), scatter_dimension=0...  111 us
    reduce_scatter x1, waiting for transfers between devices, body(): lax.psum_scatter(grad_qkv.astype(b16), ('band', 'dp'), scatter_dimension=...  107 us
    reduce_scatter x1, waiting for transfers between devices, body(): lax.psum_scatter(grad_down.astype(b16), ('band', 'dp'), scatter_dimension...  88.1 us
    pallas_call x1, Pallas kernels, gather_weights(): pl.pallas_call(gather_kernel, out_shape=jax.ShapeDtypeStruct((devices, *s...  85.2 us
    reduce_scatter x1, waiting for transfers between devices, body(): lax.psum_scatter(grad_out_proj.astype(b16), ('band', 'dp'), scatter_dimen...  71.1 us
    psum x1, waiting for transfers between devices, body(): lax.psum((grad_code_part, grad_bias_part, grad_gain_one, grad_gain_two),...  62.2 us
    psum x1, blocking collectives, body(): lax.psum((grad_code_part, grad_bias_part, grad_gain_one, grad_gain_two),...  40.4 us
    all_gather x1, waiting for transfers between devices, body(): lax.all_gather(grad_embed_low, 'band', axis=1, tiled=True)[0].astype(f32)  37 us
  transfers between devices with their start and end apart: 10, of which 8 were waited for; matrix products, arithmetic and copies ran while one was open for 13% of the time, Pallas kernels for 10%

profile of v1, /device:TPU:0, one launch (start us, length us, event | category | flops | bytes accessed | tf_op | source)
XLA Modules:
  0.0 845.0 jit_solution(16932539180308946151)
XLA Ops:
  22.8 7.4 all-to-all-start
  32.1 10.3 %all-to-all-done = bf16[16,2,6144]{2,1,0:T(2,128)(2,1)S(1)} async-done(((bf16[16,2,6144]{2,1,0:T(2,128)(2,1)}), bf16[16,2,6144]{2,1,0:T(2,128)(2,1)S(1)}, u32[]{:S(2)}, u32[]{:S(2)}) %all-to-all-start) | async-done | bytes 393248 | tf_op jit(solution)/shard_map/all_to_all | solution.py:350
  43.5 3.4 reduce.17
  47.9 5.7 fusion.6
  56.4 85.2 %gather_weights.1 = bf16[32,288,768]{2,1,0:T(8,128)(2,1)} custom-call(bf16[288,768]{1,0:T(8,128)(2,1)} %pad_maximum_fusion.1.shard), custom_call_target="tpu_custom_call" | custom-call | tf_op jit(solution)/shard_map/gather_weights/pallas_call | solution.py:287
  145.8 6.6 fusion.128
  174.5 3.4 fusion.122
  177.9 4.7 fusion.8
  200.7 4.1 convolution_convert_fusion.3
  204.9 37.0 %all-gather.3.cloned.1.call-done = bf16[16,128,768]{2,1,0:T(8,128)(2,1)} async-done(((bf16[1,128,768]{2,1,0:T(8,128)(2,1)}), bf16[16,128,768]{2,1,0:T(8,128)(2,1)}) %all-gather.3.cloned.1.call-update) | async-done | bytes 3145744 | tf_op jit(solution)/shard_map/all_gather | solution.py:445
  241.9 4.2 fusion.18
  250.2 5.2 convolution_convert_fusion.1
  256.0 4.8 convolution_convert_fusion.2
  264.4 5.6 fusion.24
  271.8 71.1 %reduce-scatter.10.cloned.1.call-done = bf16[24,768]{1,0:T(8,128)(2,1)} async-done(((bf16[768,768]{1,0:T(8,128)(2,1)}), bf16[24,768]{1,0:T(8,128)(2,1)}) %reduce-scatter.10.cloned.1.call-update) | async-done | bytes 36880 | tf_op jit(solution)/shard_map/reduce_scatter | solution.py:474
  344.3 106.8 %reduce-scatter.8.cloned.1.call-done = bf16[24,2304]{1,0:T(8,128)(2,1)} async-done(((bf16[768,2304]{1,0:T(8,128)(2,1)}), bf16[24,2304]{1,0:T(8,128)(2,1)}) %reduce-scatter.8.cloned.1.call-update) | async-done | bytes 110608 | tf_op jit(solution)/shard_map/reduce_scatter | solution.py:473
  452.7 25.4 %all-reduce.7.cloned.1.call-done = bf16[1,16,12288]{2,1,0:T(8,128)(2,1)} async-done(((bf16[1,16,12288]{2,1,0:T(8,128)(2,1)}), bf16[1,16,12288]{2,1,0:T(8,128)(2,1)}) %all-reduce.7.cloned.1.call-update) | async-done | bytes 393232 | tf_op jit(solution)/shard_map/psum | solution.py:458
  480.7 4.1 reduce.22
  485.8 5.6 all-to-all-start.1
  502.3 88.1 %reduce-scatter.14.cloned.1.call-done = bf16[96,768]{1,0:T(8,128)(2,1)} async-done(((bf16[3072,768]{1,0:T(8,128)(2,1)}), bf16[96,768]{1,0:T(8,128)(2,1)}) %reduce-scatter.14.cloned.1.call-update) | async-done | bytes 147472 | tf_op jit(solution)/shard_map/reduce_scatter | solution.py:476
  592.0 111.4 %reduce-scatter.12.cloned.1.call-done = bf16[24,3072]{1,0:T(8,128)(2,1)} async-done(((bf16[768,3072]{1,0:T(8,128)(2,1)}), bf16[24,3072]{1,0:T(8,128)(2,1)}) %reduce-scatter.12.cloned.1.call-update) | async-done | bytes 147472 | tf_op jit(solution)/shard_map/reduce_scatter | solution.py:475
  708.8 40.4 %all-reduce.3 = (f32[16,128]{1,0:T(8,128)S(1)}, f32[768]{0:T(1024)}, f32[768]{0:T(1024)}) all-reduce(f32[16,128]{1,0:T(8,128)S(1)} %add.150, f32[768]{0:T(1024)S(1)} %copy-done.75, f32[768]{0:T(1024)S(1)} %copy-done.57), channel_id=1, replica_groups=mesh['band'=16,'dp'=2] {'band','dp'}, use_global_device_ids=true, to_apply=%region_20.21 | all-reduce | flops 3584 | bytes 28672 | tf_op jit(solution)/shard_map/psum | solution.py:467
  767.6 3.7 fusion.30
  773.7 62.2 %all-reduce.9.cloned.1.call-done = f32[128,768]{1,0:T(8,128)} async-done(((f32[128,768]{1,0:T(8,128)}), f32[128,768]{1,0:T(8,128)}) %all-reduce.9.cloned.1.call-update) | async-done | bytes 393232 | tf_op jit(solution)/shard_map/psum | solution.py:467
  (330 shorter events, 122.9 us)
Async XLA Ops:
  22.8 19.6 %all-to-all-start = ((bf16[16,2,6144]{2,1,0:T(2,128)(2,1)}), bf16[16,2,6144]{2,1,0:T(2,128)(2,1)S(1)}, u32[]{:S(2)}, u32[]{:S(2)}) async-start(bf16[16,2,6144]{2,1,0:T(2,128)(2,1)} %reshape.603), calls=%async_computation | async-start | bytes 786432 | tf_op jit(solution)/shard_map/all_to_all | solution.py:350
  30.2 132.7 %reduce-scatter.6.cloned.1.call-start = ((), (), s32[]{:S(2)}) async-start(), calls=%async_computation.7 | async-start | bytes 6684672 | tf_op jit(solution)/shard_map/reduce_scatter | solution.py:362
  32.1 15.8 %copy-start.80 = (f32[16]{0:T(128)}, f32[16]{0:T(128)S(1)}, u32[]{:S(2)}) copy-start(f32[16]{0:T(128)S(1)} %fusion.105) | copy-start | bytes 196
  53.6 188.3 %all-gather.3.cloned.1.call-start = ((), (), s32[]{:S(2)}) async-start(), calls=%async_computation.14 | async-start | bytes 3342336 | tf_op jit(solution)/shard_map/all_gather | solution.py:445
  198.0 144.9 %reduce-scatter.10.cloned.1.call-start = ((), (), s32[]{:S(2)}) async-start(), calls=%async_computation.11 | async-start | bytes 1216512 | tf_op jit(solution)/shard_map/reduce_scatter | solution.py:474
  200.7 250.4 %reduce-scatter.8.cloned.1.call-start = ((), (), s32[]{:S(2)}) async-start(), calls=%async_computation.10 | async-start | bytes 3649536 | tf_op jit(solution)/shard_map/reduce_scatter | solution.py:473
  204.9 37.0 %copy-start.81 = (f32[16]{0:T(128)S(1)}, f32[16]{0:T(128)}, u32[]{:S(2)}) copy-start(f32[16]{0:T(128)} %copy-done.80) | copy-start | bytes 196
  204.9 273.2 %all-reduce.7.cloned.1.call-start = ((), (), s32[]{:S(2)}) async-start(), calls=%async_computation.8 | async-start | bytes 786432 | tf_op jit(solution)/shard_map/psum | solution.py:458
  249.9 340.4 %reduce-scatter.14.cloned.1.call-start = ((), (), s32[]{:S(2)}) async-start(), calls=%async_computation.13 | async-start | bytes 4866048 | tf_op jit(solution)/shard_map/reduce_scatter | solution.py:476
  255.4 447.9 %reduce-scatter.12.cloned.1.call-start = ((), (), s32[]{:S(2)}) async-start(), calls=%async_computation.12 | async-start | bytes 4866048 | tf_op jit(solution)/shard_map/reduce_scatter | solution.py:475
  485.8 219.2 %all-to-all-start.1 = ((bf16[16,2,6144]{2,1,0:T(2,128)(2,1)}), bf16[16,2,6144]{2,1,0:T(2,128)(2,1)S(1)}, u32[]{:S(2)}, u32[]{:S(2)}) async-start(bf16[16,2,6144]{2,1,0:T(2,128)(2,1)} %reshape.605), calls=%async_computation.2 | async-start | bytes 786432 | tf_op jit(solution)/shard_map/all_to_all | solution.py:459
  491.4 344.5 %all-reduce.9.cloned.1.call-start = ((), (), s32[]{:S(2)}) async-start(), calls=%async_computation.9 | async-start | bytes 786432 | tf_op jit(solution)/shard_map/psum | solution.py:467
  706.1 43.1 %copy-start.34 = (f32[16,128]{1,0:T(8,128)S(1)}, f32[16,128]{1,0:T(8,128)}, u32[]{:S(2)}) copy-start(f32[16,128]{1,0:T(8,128)} %copy-done.33) | copy-start | bytes 24580
  706.1 43.1 %copy-start.68 = (f32[16]{0:T(128)S(1)}, f32[16]{0:T(128)}, u32[]{:S(2)}) copy-start(f32[16]{0:T(128)} %copy-done.67) | copy-start | bytes 196
  706.1 43.1 %copy-start.72 = (f32[128]{0:T(128)S(1)}, f32[128]{0:T(128)}, u32[]{:S(2)}) copy-start(f32[128]{0:T(128)} %copy-done.71) | copy-start | bytes 1540
  706.1 43.1 %copy-start.74 = (f32[16]{0:T(128)S(1)}, f32[16]{0:T(128)}, u32[]{:S(2)}) copy-start(f32[16]{0:T(128)} %copy-done.73) | copy-start | bytes 196
  706.2 43.8 %copy-start.87 = (f32[16]{0:T(128)S(1)}, f32[16]{0:T(128)}, u32[]{:S(2)}) copy-start(f32[16]{0:T(128)} %copy-done.86) | copy-start | bytes 196
  706.2 44.0 %copy-start.21 = (f32[16,2048]{1,0:T(8,128)S(1)}, f32[16,2048]{1,0:T(8,128)}, u32[]{:S(2)}) copy-start(f32[16,2048]{1,0:T(8,128)} %copy-done.20) | copy-start | bytes 393220
  706.2 45.7 %copy-start.54 = (f32[16]{0:T(128)S(1)}, f32[16]{0:T(128)}, u32[]{:S(2)}) copy-start(f32[16]{0:T(128)} %copy-done.53) | copy-start | bytes 196
  706.2 45.7 %copy-start.62 = (f32[128]{0:T(128)S(1)}, f32[128]{0:T(128)}, u32[]{:S(2)}) copy-start(f32[128]{0:T(128)} %copy-done.61) | copy-start | bytes 1540
  708.4 49.3 %copy-start.30 = (f32[4,16,16]{1,2,0:T(8,128)S(1)}, f32[4,16,16]{1,2,0:T(8,128)}, u32[]{:S(2)}) copy-start(f32[4,16,16]{1,2,0:T(8,128)} %copy-done.29) | copy-start | bytes 12292
  708.4 49.3 %copy-start.56 = (f32[4,16]{1,0:T(4,128)S(1)}, f32[4,16]{1,0:T(4,128)}, u32[]{:S(2)}) copy-start(f32[4,16]{1,0:T(4,128)} %copy-done.55) | copy-start | bytes 772
  708.4 50.3 %copy-start.39 = (f32[16,4,32]{2,1,0:T(4,128)S(1)}, f32[16,4,32]{2,1,0:T(4,128)}, u32[]{:S(2)}) copy-start(f32[16,4,32]{2,1,0:T(4,128)} %copy-done.38) | copy-start | bytes 24580
  708.4 51.9 %copy-start.37 = (f32[16,4,32]{2,1,0:T(4,128)S(1)}, f32[16,4,32]{2,1,0:T(4,128)}, u32[]{:S(2)}) copy-start(f32[16,4,32]{2,1,0:T(4,128)} %copy-done.36) | copy-start | bytes 24580
  (77 other events, 284.6 us)
Sparse Core Ops, SparseCore 0:
  53.8 101.4 reduce-scatter.5
  198.1 43.7 all-gather.2
  247.8 95.0 reduce-scatter.9
  349.1 101.9 reduce-scatter.7
  453.3 24.6 all-reduce.6
  483.4 106.9 reduce-scatter.13
  597.3 106.0 reduce-scatter.11
  709.2 126.6 all-reduce.8

commit v2 on v1

--- a/solution.py
+++ b/solution.py
@@ -87,7 +87,11 @@
 
 
 MESH = pl.DeviceIdType.MESH
-GATHER_ORDERS = ("zxy", "xzy", "yzx", "zyx", "xzy", "yzx")
+B16 = jnp.bfloat16
+F32 = jnp.float32
+CHUNK = 48
+PART = 96
+ORDERS = ("zxy", "xzy", "yzx", "zyx", "xzy", "yzx")
 
 
 def place():
@@ -112,6 +116,10 @@
 
 def both(first, second):
     return second if first is True else first & second
+
+
+def aligned(rows):
+    return pl.multiple_of(rows, 16)
 
 
 def meet_neighbours():
@@ -135,16 +143,13 @@
 
 
 class Gather:
-    def __init__(self, held, rows, orders, send_sem, recv_sem, pair_send, pair_recv):
-        self.held, self.rows, self.orders = held, rows, orders
+    def __init__(self, view, orders, send_sem, recv_sem, pair_send, pair_recv):
+        self.view, self.orders = view, orders
         self.send_sem, self.recv_sem = send_sem, recv_sem
         self.pair_send, self.pair_recv = pair_send, pair_recv
         self.z, self.x, self.core, self.y = place()
         self.sends = []
         self.count = [0] * len(orders)
-
-    def view(self, chunk, where):
-        return self.held.at[where, pl.ds(chunk * self.rows, self.rows)]
 
     def send(self, chunk, block, dim, cond, direction=0):
         z, x, core, y = self.z, self.x, self.core, self.y
@@ -206,7 +211,9 @@
                     clock = max(clock, item[4]) + 1.0
                     flip = (1, item[3]) if dim == "x" else (item[2], 1)
                     new.append((item[0], item[1], *flip, clock))
-            found += [(item[4], chunk, dim, item) for item in new]
+            found += [
+                (item[4], chunk, functools.partial(self.arrive, chunk, dim, item)) for item in new
+            ]
             held = held + new
         return found
 
@@ -250,65 +257,543 @@
                 self.pair(chunk, block, 1 - self.core).wait_recv()
 
 
-def gather_kernel(shard, whole, held, local_sem, *sems):
-    rows = held.shape[1] // len(GATHER_ORDERS)
-    own = pltpu.make_async_copy(shard, held.at[slot(*place())], local_sem)
-    own.start()
-    own.wait()
+class Reduce:
+    def __init__(self, view, orders, pair_view, pair_buf, buf, pair_send, pair_recv, send, recv):
+        self.view, self.orders = view, tuple(order[::-1] for order in orders)
+        self.pair_view, self.pair_buf, self.buf = pair_view, pair_buf, buf
+        self.pair_send, self.pair_recv = pair_send, pair_recv
+        self.send_sem, self.recv_sem = send, recv
+        self.z, self.x, self.core, self.y = place()
+        self.sends = []
+        self.count = [0] * len(orders)
+        self.index = [{} for _ in orders]
+
+    def coords(self, block):
+        zz, flip_x, flip_y = block
+        return (zz, 1 - self.x if flip_x else self.x, 1 - self.y if flip_y else self.y)
+
+    def own(self, chunk, block):
+        zz, xx, yy = self.coords(block)
+        return self.view(chunk, slot(zz, xx, self.core, yy))
+
+    def add(self, target, source):
+        target[...] = target[...] + source[...]
+
+    def pair_copy(self, part, rail):
+        block = (rail // 4, (rail // 2) % 2, rail % 2)
+        return pltpu.make_async_remote_copy(
+            src_ref=self.pair_view(part, slot(block[0], block[1], 1 - self.core, block[2])),
+            dst_ref=self.pair_buf.at[part, rail],
+            send_sem=self.pair_send.at[part, rail],
+            recv_sem=self.pair_recv.at[part, rail],
+            device_id=device(self.z, self.x, 1 - self.core, self.y),
+            device_id_type=MESH,
+        )
+
+    def place_of(self, chunk, key):
+        return self.index[chunk].setdefault(key, len(self.index[chunk]))
+
+    def copy(self, chunk, block, key, target):
+        where = self.place_of(chunk, key)
+        number = self.count[chunk]
+        self.count[chunk] += 1
+        return pltpu.make_async_remote_copy(
+            src_ref=self.own(chunk, block),
+            dst_ref=self.buf.at[chunk, where],
+            send_sem=self.send_sem.at[chunk, number],
+            recv_sem=self.recv_sem.at[chunk, where],
+            device_id=target,
+            device_id_type=MESH,
+        )
+
+    def send(self, chunk, block, key, target, cond):
+        copy = self.copy(chunk, block, key, target)
+        when(cond, copy.start)
+        self.sends.append((cond, copy))
+
+    def wait_add(self, chunk, block, key):
+        where = self.place_of(chunk, key)
+        landed = self.buf.at[chunk, where]
+        pltpu.make_async_remote_copy(
+            src_ref=landed,
+            dst_ref=landed,
+            send_sem=self.send_sem.at[chunk, 0],
+            recv_sem=self.recv_sem.at[chunk, where],
+            device_id=device(self.z, self.x, 1 - self.core, self.y),
+            device_id_type=MESH,
+        ).wait_recv()
+        self.add(self.own(chunk, block), landed)
+
+    def flips(self, chunk, stage):
+        left = self.orders[chunk][stage:]
+        out = [(fx, fy) for fx in ((1, 0) if "x" in left else (0,)) for fy in ((1, 0) if "y" in left else (0,))]
+        return out
+
+    def pair_order(self, part):
+        return [8 * h + r for h in (0, 1) for r in range(8)]
+
+    def ready(self, chunk, stage, block, cond=True):
+        order = self.orders[chunk]
+        if stage == 3:
+            return
+        dim = order[stage]
+        zz, fx, fy = block
+        if dim == "x" and fx:
+            target = device(self.z, 1 - self.x, self.core, self.y)
+            self.send(chunk, block, (stage, zz if "z" in order[stage:] else "own", 0, fy), target, cond)
+        elif dim == "y" and fy:
+            target = device(self.z, self.x, self.core, 1 - self.y)
+            self.send(chunk, block, (stage, zz if "z" in order[stage:] else "own", fx, 0), target, cond)
+
+    def z_start(self, chunk, stage, step, flips):
+        up, down = (3 - step, *flips), (step, *flips)
+        self.send(chunk, up, (stage, step, 1, *flips), device(self.z + 1, self.x, self.core, self.y), self.z == 0)
+        self.send(chunk, down, (stage, step, -1, *flips), device(self.z - 1, self.x, self.core, self.y), self.z == 3)
+
+    def z_arrive(self, chunk, stage, step, flips, way):
+        z = self.z if way == 1 else 3 - self.z
+        cond = (z >= 1) & (z <= step + 1)
+        zz = 2 + z - step
+        zz = zz if way == 1 else 3 - zz
+        block = (zz, *flips)
+        key = (stage, step, way, *flips)
+        when(cond, lambda: self.wait_add(chunk, block, key))
+        if step < 2:
+            self.send(
+                chunk, block, (stage, step + 1, way, *flips),
+                device(self.z + way, self.x, self.core, self.y), cond,
+            )
+
+    def z_done(self, chunk, stage, flips):
+        self.ready(chunk, stage + 1, (self.z, *flips))
+
+    def xy_arrive(self, chunk, stage, zz, fx, fy):
+        key = (stage, zz, fx, fy)
+        block = (self.z if zz == "own" else zz, fx, fy)
+        self.wait_add(chunk, block, key)
+        self.ready(chunk, stage + 1, block)
+
+    def pair_arrive(self, part, block, chunks):
+        zz, xx, yy = self.coords(block)
+        rail = zz * 4 + xx * 2 + yy
+        copy = pltpu.make_async_remote_copy(
+            src_ref=self.pair_buf.at[part, rail],
+            dst_ref=self.pair_buf.at[part, rail],
+            send_sem=self.pair_send.at[part, rail],
+            recv_sem=self.pair_recv.at[part, rail],
+            device_id=device(self.z, self.x, 1 - self.core, self.y),
+            device_id_type=MESH,
+        )
+        copy.wait_recv()
+        self.add(self.pair_view(part, slot(zz, xx, self.core, yy)), self.pair_buf.at[part, rail])
+        for chunk in chunks:
+            self.ready(chunk, 0, block)
+
+    def events(self, part, chunks):
+        found, ready = [], {}
+        number = 0
+        clock = 0.0
+        for fx, fy in ((1, 1), (1, 0), (0, 1), (0, 0)):
+            for zz in (3, 0, 2, 1):
+                clock += 0.5
+                found.append((clock, 0, functools.partial(self.pair_arrive, part, (zz, fx, fy), chunks)))
+                ready[(zz, fx, fy)] = clock
+        for chunk in chunks:
+            times = dict(ready)
+            order = self.orders[chunk]
+            for stage, dim in enumerate(order):
+                clock = 0.0
+                nxt = {}
+                flips = self.flips(chunk, stage)
+                if dim == "z":
+                    for step in range(3):
+                        for fl in flips:
+                            needed = (0, 3) if step == 0 else (0, 1, 2, 3)
+                            clock = max(clock, *(times[(zz, *fl)] for zz in needed)) + 0.001
+                            found.append((clock, chunk, functools.partial(self.z_start, chunk, stage, step, fl)))
+                            clock += 1.0
+                            for way in (1, -1):
+                                found.append((clock, chunk, functools.partial(self.z_arrive, chunk, stage, step, fl, way)))
+                            nxt[("own", *fl)] = clock + 0.001
+                    for fl in flips:
+                        found.append((nxt[("own", *fl)], chunk, functools.partial(self.z_done, chunk, stage, fl)))
+                else:
+                    pick = 0 if dim == "x" else 1
+                    sent = [key for key in times if key[1 + pick] == 1]
+                    kept = {}
+                    for key in sorted(sent, key=lambda key: times[key]):
+                        clock = max(clock, times[key]) + 1.0
+                        mine = (key[0], 0, key[2]) if dim == "x" else (key[0], key[1], 0)
+                        clock = max(clock, times[mine] + 0.001)
+                        kept[mine] = clock
+                        found.append((clock, chunk, functools.partial(self.xy_arrive, chunk, stage, *mine)))
+                    nxt = kept
+                times = nxt
+        return sorted(found, key=lambda event: event[:2])
+
+    def finish(self):
+        for cond, copy in self.sends:
+            when(cond, copy.wait_send)
+        for part in range(self.pair_buf.shape[0]):
+            for rail in range(16):
+                self.pair_copy(part, rail).wait_send()
+
+
+def dot_nt(left, right):
+    return lax.dot_general(left, right, (((1,), (1,)), ((), ())), preferred_element_type=F32)
+
+
+def dot_tn(left, right):
+    return lax.dot_general(left, right, (((0,), (0,)), ((), ())), preferred_element_type=F32)
+
+
+def dot_nn(left, right):
+    return jnp.dot(left, right, preferred_element_type=F32)
+
+
+def unit_parts(rows):
+    centred = rows - jnp.mean(rows, axis=-1, keepdims=True)
+    inverse = lax.rsqrt(jnp.mean(centred * centred, axis=-1, keepdims=True) + EPS_BLOCK)
+    return centred * inverse, inverse
+
+
+class Block:
+    def __init__(self, weights, down, refs):
+        self.weights, self.down = weights, down
+        self.__dict__.update(refs)
+        self.width = weights.shape[1]
+        self.halves = weights.shape[1] // (2 * HEAD_DIM)
+
+    def masks(self):
+        tokens = self.joint.shape[1]
+        lane = lax.broadcasted_iota(jnp.int32, (tokens, 2 * HEAD_DIM), 1)
+        low = lane < HEAD_DIM
+        return low, low.astype(F32).astype(B16), (~low).astype(F32).astype(B16)
+
+    def pair_rows(self, rows, low, high):
+        return jnp.concatenate([rows * low, rows * high], axis=0)
+
+    def project(self):
+        unit, inverse = unit_parts(self.residual[...])
+        normed = (unit * self.gain_one[...]).astype(B16)
+        self.normed_one[...] = normed
+        self.unit_one[...] = unit
+        self.inverse_one[...] = jnp.broadcast_to(inverse, self.inverse_one.shape)
+
+        @pl.loop(0, 3)
+        def _(part):
+            self.joint[part] = dot_nn(self.normed_one[...], self.weights[part]).astype(B16)
+
+    def attend(self):
+        tokens = self.joint.shape[1]
+        scale = 1.0 / math.sqrt(HEAD_DIM)
+
+        @pl.loop(0, self.halves)
+        def _(pair):
+            where, low, high = self.masks()
+            lanes = pl.ds(pl.multiple_of(pair * 2 * HEAD_DIM, 2 * HEAD_DIM), 2 * HEAD_DIM)
+            query, key, value = (self.joint[part, :, lanes] for part in range(3))
+            scores = dot_nt(self.pair_rows(query, low, high), key) * scale
+            raised = jnp.exp(scores - jnp.max(scores, axis=-1, keepdims=True))
+            probs = raised / jnp.sum(raised, axis=-1, keepdims=True)
+            self.probs[pair] = probs
+            mixed = dot_nn(probs.astype(B16), value)
+            self.mixed[:, lanes] = jnp.where(where, mixed[:tokens], mixed[tokens:]).astype(B16)
+
+    def widen(self):
+        middle = self.residual[...] + dot_nn(self.mixed[...], self.weights[3])
+        unit, inverse = unit_parts(middle)
+        self.normed_two[...] = (unit * self.gain_two[...]).astype(B16)
+        self.unit_two[...] = unit
+        self.inverse_two[...] = jnp.broadcast_to(inverse, self.inverse_two.shape)
+        self.result[...] = middle
+
+        @pl.loop(0, 4)
+        def _(part):
+            pre = dot_nn(self.normed_two[...], self.weights[4 + part])
+            self.pre_act[part] = pre
+            self.act[part] = gelu_tanh(pre).astype(B16)
+
+    def narrow(self):
+        @pl.loop(0, 4)
+        def _(part):
+            rows = pl.ds(aligned(part * self.width), self.width)
+            self.result[...] += dot_nn(self.act[part], self.down[rows, :])
+
+        self.block_out[...] = self.result[...].astype(B16)
+
+    def back_narrow(self, part):
+        rows = pl.ds(aligned(part * self.width), self.width)
+        grad_act = dot_nt(self.out_grad[...], self.down[rows, :])
+        grad_pre = (grad_act * gelu_slope(self.pre_act[part])).astype(B16)
+        self.grad_pre[part] = grad_pre
+        self.grad_normed[...] += dot_nt(grad_pre, self.weights[4 + part])
+
+    def down_grad(self, part, store):
+        turned = self.act[part].T
+        for at in range(0, self.width, 256):
+            store[pl.ds(aligned(part * self.width), self.width), at : at + 256] = dot_nn(
+                turned, self.out_grad[:, at : at + 256]
+            ).astype(B16)
+
+    def pair_grad(self, first, second, first_grad, second_grad, store, offset):
+        @pl.loop(0, 4)
+        def _(group):
+            rows = pl.ds(aligned(group * 192), 192)
+            for at in range(0, self.width, 256):
+                cols = slice(at, at + 256)
+                one = dot_nn(first[rows, :], first_grad(cols))
+                two = dot_nn(second[rows, :], second_grad(cols))
+                for owner in range(8):
+                    piece = jnp.concatenate(
+                        [one[owner * 24 : owner * 24 + 24], two[owner * 24 : owner * 24 + 24]], axis=0
+                    )
+                    target = aligned((group * 8 + owner) * PART + offset)
+                    store[pl.ds(target, CHUNK), cols] = piece.astype(B16)
+
+    def back_wide(self):
+        grad_normed = self.grad_normed[...]
+        unit = self.unit_two[...]
+        self.gain_grads[1:2, :] = jnp.sum(grad_normed * unit, axis=0, keepdims=True)
+        scaled = grad_normed * self.gain_two[...]
+        back = self.inverse_two[:, :1] * (
+            scaled
+            - jnp.mean(scaled, axis=-1, keepdims=True)
+            - unit * jnp.mean(scaled * unit, axis=-1, keepdims=True)
+        )
+        grad_middle = self.out_grad[...].astype(F32) + back
+        self.grad_middle[...] = grad_middle
+        branch = grad_middle.astype(B16)
+        self.grad_branch[...] = branch
+        self.grad_mixed[...] = dot_nt(branch, self.weights[3]).astype(B16)
+        self.turned_mixed[...] = self.mixed[...].T
+
+    def back_attend(self):
+        tokens = self.joint.shape[1]
+        scale = 1.0 / math.sqrt(HEAD_DIM)
+
+        @pl.loop(0, self.halves)
+        def _(pair):
+            where, low, high = self.masks()
+            lanes = pl.ds(pl.multiple_of(pair * 2 * HEAD_DIM, 2 * HEAD_DIM), 2 * HEAD_DIM)
+            query, key, value = (self.joint[part, :, lanes] for part in range(3))
+            grads = self.pair_rows(self.grad_mixed[:, lanes], low, high)
+            probs = self.probs[pair]
+            self.grad_joint[2, :, lanes] = dot_tn(probs.astype(B16), grads).astype(B16)
+            grad_probs = dot_nt(grads, value)
+            total = jnp.sum(grad_probs * probs, axis=-1, keepdims=True)
+            grad_scores = (probs * (grad_probs - total)).astype(B16)
+            queries = dot_nn(grad_scores, key) * scale
+            self.grad_joint[0, :, lanes] = jnp.where(
+                where, queries[:tokens], queries[tokens:]
+            ).astype(B16)
+            keys = dot_tn(grad_scores, self.pair_rows(query, low, high)) * scale
+            self.grad_joint[1, :, lanes] = keys.astype(B16)
+
+    def back_project(self):
+        self.grad_normed[...] = jnp.zeros(self.grad_normed.shape, F32)
+
+        @pl.loop(0, 3)
+        def _(part):
+            self.grad_normed[...] += dot_nt(self.grad_joint[part], self.weights[part])
+
+        grad_normed = self.grad_normed[...]
+        unit = self.unit_one[...]
+        self.gain_grads[0:1, :] = jnp.sum(grad_normed * unit, axis=0, keepdims=True)
+        scaled = grad_normed * self.gain_one[...]
+        back = self.inverse_one[:, :1] * (
+            scaled
+            - jnp.mean(scaled, axis=-1, keepdims=True)
+            - unit * jnp.mean(scaled * unit, axis=-1, keepdims=True)
+        )
+        self.grad_embed[...] = (self.grad_middle[...] + back).astype(B16)
+
+
+def spread(gathered, weights, chunk):
+    part, offset = chunk // 2, (chunk % 2) * CHUNK
+
+    @pl.loop(0, 16)
+    def _(two):
+        one, other = (
+            gathered[part, pl.ds(aligned((two * 2 + k) * PART + offset), CHUNK), :].astype(F32)
+            for k in (0, 1)
+        )
+        rows = pl.ds(aligned(two * CHUNK), CHUNK)
+        half = CHUNK // 2
+        weights[2 * chunk, rows, :] = jnp.concatenate([one[:half], other[:half]], 0).astype(B16)
+        weights[2 * chunk + 1, rows, :] = jnp.concatenate([one[half:], other[half:]], 0).astype(B16)
+
+
+def middle_kernel(shard, residual, out_grad, gain_one, gain_two, block_out, grad_embed, shares, gain_grads, *scratch):
+    (gathered, weights, down_grads, pair_buf, buf, joint, probs, pre_act, act, grad_pre, mixed, normed_one, normed_two,
+     unit_one, unit_two, inverse_one, inverse_two, result, grad_normed, grad_middle, grad_branch, grad_mixed, grad_joint,
+     turned_mixed, turned_one, turned_two, local_sem, *sems) = scratch
+    names = dict(
+        residual=residual, out_grad=out_grad, gain_one=gain_one, gain_two=gain_two, block_out=block_out,
+        grad_embed=grad_embed, gain_grads=gain_grads, joint=joint, probs=probs, pre_act=pre_act, act=act,
+        grad_pre=grad_pre, mixed=mixed, normed_one=normed_one, normed_two=normed_two, unit_one=unit_one,
+        unit_two=unit_two, inverse_one=inverse_one, inverse_two=inverse_two, result=result, grad_normed=grad_normed,
+        grad_middle=grad_middle, grad_branch=grad_branch, grad_mixed=grad_mixed, grad_joint=grad_joint,
+        turned_mixed=turned_mixed,
+    )
+    me = slot(*place())
+    own = [
+        pltpu.make_async_copy(
+            shard.at[pl.ds(part * PART, PART)],
+            gathered.at[part, pl.ds(aligned(me * PART), PART)],
+            local_sem.at[part],
+        )
+        for part in range(3)
+    ]
+    for copy in own:
+        copy.start()
+    for copy in own:
+        copy.wait()
     meet_neighbours()
-    gather = Gather(held, rows, GATHER_ORDERS, *sems)
+
+    def weight_view(chunk, where):
+        return gathered.at[chunk // 2, pl.ds(aligned(where * PART + (chunk % 2) * CHUNK), CHUNK)]
+
+    gather = Gather(weight_view, ORDERS, *sems[:4])
     events = []
-    for chunk in range(len(GATHER_ORDERS)):
+    for chunk in range(len(ORDERS)):
         gather.start(chunk)
         events += gather.events(chunk)
-    for _, chunk, dim, item in sorted(events, key=lambda event: event[:2]):
-        gather.arrive(chunk, dim, item)
+    for _, _, run in sorted(events, key=lambda event: event[:2]):
+        run()
     gather.finish()
-    out = pltpu.make_async_copy(held, whole, local_sem)
-    out.start()
-    out.wait()
-
-
-def gather_weights(attn_qkv, attn_out, mlp_up, mlp_down):
-    if (lax.axis_size("band"), lax.axis_size("dp")) != (16, 2):
-        return tuple(
-            lax.all_gather(weight, ("band", "dp"), axis=0, tiled=True)
-            for weight in (attn_qkv, attn_out, mlp_up, mlp_down)
-        )
+    for chunk in range(4):
+        spread(gathered, weights, chunk)
+
+    block = Block(weights, gathered.at[2], names)
+    block.project()
+    block.attend()
+    block.widen()
+    block.narrow()
+
+    def part_ref(part):
+        return down_grads if part == 2 else gathered.at[part]
+
+    def grad_view(chunk, where):
+        return part_ref(chunk // 2).at[pl.ds(aligned(where * PART + (chunk % 2) * CHUNK), CHUNK)]
+
+    def part_view(part, where):
+        return part_ref(part).at[pl.ds(aligned(where * PART), PART)]
+
+    reduce = Reduce(grad_view, ORDERS, part_view, pair_buf, buf, *sems[4:])
+    grad_normed[...] = jnp.zeros(grad_normed.shape, F32)
+
+    @pl.loop(0, 4)
+    def _(part):
+        block.back_narrow(part)
+        block.down_grad(part, down_grads)
+
+    for rail in range(16):
+        reduce.pair_copy(2, rail).start()
+    turned_two[...] = normed_two[...].T
+    for part in (0, 2):
+        block.pair_grad(
+            turned_two, turned_two, lambda cols, part=part: grad_pre[part, :, cols],
+            lambda cols, part=part: grad_pre[part + 1, :, cols], part_ref(1), part // 2 * CHUNK,
+        )
+    for rail in range(16):
+        reduce.pair_copy(1, rail).start()
+    block.back_wide()
+    block.back_attend()
+    turned_one[...] = normed_one[...].T
+    block.pair_grad(
+        turned_one, turned_one, lambda cols: grad_joint[0, :, cols], lambda cols: grad_joint[1, :, cols], part_ref(0), 0
+    )
+    block.pair_grad(
+        turned_one, turned_mixed, lambda cols: grad_joint[2, :, cols], lambda cols: grad_branch[:, cols], part_ref(0), CHUNK
+    )
+    for rail in range(16):
+        reduce.pair_copy(0, rail).start()
+    block.back_project()
+    events = []
+    for part, chunks in ((2, (4, 5)), (1, (2, 3)), (0, (0, 1))):
+        events += reduce.events(part, chunks)
+    for _, _, run in sorted(events, key=lambda event: event[:2]):
+        run()
+    for part in range(3):
+        shares[part * PART : (part + 1) * PART, :] = part_view(part, me)[...].astype(F32)
+    reduce.finish()
+
+
+def middle(attn_qkv, attn_out, mlp_up, mlp_down, residual, out_grad, gain_one, gain_two):
     width = attn_out.shape[1]
     devices = lax.axis_size("band") * lax.axis_size("dp")
+    tokens = residual.shape[0]
 
     def stack(weight):
         parts = weight.shape[1] // width
         return weight.reshape(weight.shape[0], parts, width).transpose(1, 0, 2).reshape(-1, width)
 
     shard = jnp.concatenate([stack(w) for w in (attn_qkv, attn_out, mlp_up, mlp_down)], axis=0)
-    chunks = len(GATHER_ORDERS)
-    whole = pl.pallas_call(
-        gather_kernel,
-        out_shape=jax.ShapeDtypeStruct((devices, *shard.shape), shard.dtype),
-        in_specs=[pl.BlockSpec(memory_space=pl.ANY)],
-        out_specs=pl.BlockSpec(memory_space=pl.ANY),
+    chunks = len(ORDERS)
+    vmem = pl.BlockSpec(memory_space=pltpu.VMEM)
+    rows = lambda kind, *lead: pltpu.VMEM((*lead, tokens, width), kind)
+    dma = pltpu.SemaphoreType.DMA
+    outs = pl.pallas_call(
+        middle_kernel,
+        out_shape=[
+            jax.ShapeDtypeStruct((tokens, width), B16),
+            jax.ShapeDtypeStruct((tokens, width), B16),
+            jax.ShapeDtypeStruct((3 * PART, width), F32),
+            jax.ShapeDtypeStruct((2, width), F32),
+        ],
+        in_specs=[pl.BlockSpec(memory_space=pl.ANY)] + [vmem] * 4,
+        out_specs=[vmem] * 4,
         scratch_shapes=[
-            pltpu.VMEM((devices, *shard.shape), shard.dtype),
-            pltpu.SemaphoreType.DMA,
-            pltpu.SemaphoreType.DMA((chunks, 40)),
-            pltpu.SemaphoreType.DMA((chunks, 16)),
-            pltpu.SemaphoreType.DMA((chunks, 16)),
-            pltpu.SemaphoreType.DMA((chunks, 16)),
+            pltpu.VMEM((3, devices * PART, width), B16),
+            pltpu.VMEM((8, width, width), B16),
+            pltpu.VMEM((devices * PART, width), B16),
+            pltpu.VMEM((3, 16, PART, width), B16),
+            pltpu.VMEM((chunks, 21, CHUNK, width), B16),
+            rows(B16, 3),
+            pltpu.VMEM((HEADS // 2, 2 * tokens, tokens), F32),
+            rows(F32, 4),
+            rows(B16, 4),
+            rows(B16, 4),
+            rows(B16),
+            rows(B16),
+            rows(B16),
+            rows(F32),
+            rows(F32),
+            pltpu.VMEM((tokens, 128), F32),
+            pltpu.VMEM((tokens, 128), F32),
+            rows(F32),
+            rows(F32),
+            rows(F32),
+            rows(B16),
+            rows(B16),
+            rows(B16, 3),
+            pltpu.VMEM((width, tokens), B16),
+            pltpu.VMEM((width, tokens), B16),
+            pltpu.VMEM((width, tokens), B16),
+            dma((3,)),
+            dma((chunks, 40)),
+            dma((chunks, 16)),
+            dma((chunks, 16)),
+            dma((chunks, 16)),
+            dma((3, 16)),
+            dma((3, 16)),
+            dma((chunks, 48)),
+            dma((chunks, 24)),
         ],
         compiler_params=pltpu.CompilerParams(
-            collective_id=0, has_side_effects=True, vmem_limit_bytes=56 * 2**20
+            collective_id=0, has_side_effects=True, vmem_limit_bytes=62 * 2**20
         ),
-        name="gather_weights",
-    )(shard)
-    out, at = [], 0
+        name="gather_block_reduce",
+    )(shard, residual, out_grad, gain_one, gain_two)
+    block_out, grad_embed, shares, gain_grads = outs
+    grads, at = [], 0
     for weight in (attn_qkv, attn_out, mlp_up, mlp_down):
-        rows, parts = weight.shape[0], weight.shape[1] // width
-        piece = whole[:, at : at + rows * parts].reshape(devices, parts, rows, width)
-        out.append(piece.transpose(0, 2, 1, 3).reshape(devices * rows, parts * width))
-        at += rows * parts
-    return tuple(out)
+        own_rows, parts = weight.shape[0], weight.shape[1] // width
+        piece = shares[at : at + own_rows * parts].reshape(parts, own_rows, width)
+        grads.append(piece.transpose(1, 0, 2).reshape(own_rows, parts * width))
+        at += own_rows * parts
+    return block_out, grad_embed, grads, gain_grads
 
 
 def body(
@@ -365,7 +850,12 @@
         scatter_dimension=0,
         tiled=True,
     )
-    gathered = gather_weights(attn_qkv, attn_out, mlp_up, mlp_down)
+    gathered = (
+        lax.all_gather(attn_qkv, ("band", "dp"), axis=0, tiled=True),
+        lax.all_gather(attn_out, ("band", "dp"), axis=0, tiled=True),
+        lax.all_gather(mlp_up, ("band", "dp"), axis=0, tiled=True),
+        lax.all_gather(mlp_down, ("band", "dp"), axis=0, tiled=True),
+    )
     qkv_full, out_full, up_full, down_full = gathered
     gain_one = norm_gain1.astype(f32)
     gain_two = norm_gain2.astype(f32)
@@ -400,7 +890,12 @@
     act_low = gelu_tanh(pre_act).astype(b16)
     result = middle + jnp.einsum("inf,fd->ind", act_low, down_full, preferred_element_type=f32)
     block_out = result.astype(b16)[None]
-    qkv_back, out_back, up_back, down_back = gathered
+    qkv_back, out_back, up_back, down_back = (
+        lax.all_gather(attn_qkv, ("band", "dp"), axis=0, tiled=True),
+        lax.all_gather(attn_out, ("band", "dp"), axis=0, tiled=True),
+        lax.all_gather(mlp_up, ("band", "dp"), axis=0, tiled=True),
+        lax.all_gather(mlp_down, ("band", "dp"), axis=0, tiled=True),
+    )
     grad_top = out_grad[0]
     grad_down = jnp.einsum("inf,ind->fd", act_low, grad_top, preferred_element_type=f32)
     grad_act = jnp.einsum("ind,fd->inf", grad_top, down_back, preferred_element_type=f32)
@@ -455,6 +950,126 @@
     pixel_total = pixel_part
     kernel_grad, bias_grad, pixel_total = (kernel_total, bias_total, pixel_total)
     pixel_out = pixel_total[None]
+    kernel_grad_low = kernel_grad.reshape(band_local, -1).astype(b16)
+    grad_columns = lax.all_to_all(kernel_grad_low, "band", split_axis=1, concat_axis=0, tiled=True)
+    grad_kernel_part = jnp.einsum("nh,nc->hc", code_low, grad_columns, preferred_element_type=f32)
+    grad_code_part = jnp.einsum("nc,hc->nh", grad_columns, kernel_gen, preferred_element_type=f32)
+    bias_back = jnp.einsum("bd,hd->bh", bias_grad, bias_gen.astype(f32), precision=PRECISE)
+    grad_code_part = grad_code_part + lax.dynamic_update_slice_in_dim(
+        jnp.zeros_like(grad_code_part), bias_back, first_band, 0
+    )
+    grad_bias_part = jnp.einsum("bh,bd->hd", own_code.astype(f32), bias_grad, precision=PRECISE)
+    grad_code, grad_bias_gen, grad_norm_gain1, grad_norm_gain2 = lax.psum(
+        (grad_code_part, grad_bias_part, grad_gain_one, grad_gain_two), ("band", "dp")
+    )
+    grad_kernel_gen = lax.psum(grad_kernel_part.astype(jnp.bfloat16), "dp").astype(jnp.float32)
+    hyper_grads = hyper_pull(grad_code)
+    shares = (
+        lax.psum_scatter(grad_qkv, ("band", "dp"), scatter_dimension=0, tiled=True),
+        lax.psum_scatter(grad_out_proj, ("band", "dp"), scatter_dimension=0, tiled=True),
+        lax.psum_scatter(grad_up, ("band", "dp"), scatter_dimension=0, tiled=True),
+        lax.psum_scatter(grad_down, ("band", "dp"), scatter_dimension=0, tiled=True),
+    )
+    return (
+        block_out,
+        pixel_out,
+        hyper_grads[0],
+        hyper_grads[1],
+        hyper_grads[2],
+        hyper_grads[3],
+        hyper_grads[4],
+        hyper_grads[5],
+        grad_kernel_gen,
+        grad_bias_gen,
+        grad_norm_gain1,
+        shares[0],
+        shares[1],
+        grad_norm_gain2,
+        shares[2],
+        shares[3],
+    )
+
+
+def fast_body(
+    pixels,
+    wavelengths,
+    band_counts,
+    band_mask,
+    hyper_qkv,
+    hyper_out,
+    hyper_gain1,
+    hyper_up,
+    hyper_down,
+    hyper_gain2,
+    kernel_gen,
+    bias_gen,
+    norm_gain1,
+    attn_qkv,
+    attn_out,
+    norm_gain2,
+    mlp_up,
+    mlp_down,
+    out_grad,
+):
+    f32 = jnp.float32
+    b16 = jnp.bfloat16
+    band_local = pixels.shape[3]
+    pixel_local = pixels[0]
+    model_width = bias_gen.shape[1]
+    hyper_params = tuple(
+        (
+            weight.astype(f32)
+            for weight in (hyper_qkv, hyper_out, hyper_gain1, hyper_up, hyper_down, hyper_gain2)
+        )
+    )
+    wave_tokens = wave_embed(wavelengths, HW)
+    band_code, hyper_pull = jax.vjp(lambda *params: hyper_net(wave_tokens, *params), *hyper_params)
+    code_low = band_code.astype(b16)
+    column_part = jnp.dot(code_low, kernel_gen, preferred_element_type=f32).astype(b16)
+    kernel_rows = lax.all_to_all(column_part, "band", split_axis=0, concat_axis=1, tiled=True)
+    kernels = kernel_rows.reshape(band_local, -1, model_width)
+    first_band = lax.axis_index("band") * band_local
+    own_code = lax.dynamic_slice_in_dim(code_low, first_band, band_local, 0)
+    count_row = band_counts[0]
+    biases = jnp.dot(own_code, bias_gen, preferred_element_type=f32)
+    slot_ids = first_band + jnp.arange(band_local, dtype=jnp.int32)
+    active = (slot_ids[None, :] < count_row[:, None]) & (band_mask[0] == 1)
+    band_weight = jnp.where(active, lax.rsqrt(count_row.astype(f32))[:, None], f32(0.0))
+    pixel_rows = pixel_local
+    weight_rows = band_weight
+    conv_out = jnp.einsum("inbp,bpd->inbd", pixel_rows, kernels, preferred_element_type=f32)
+    residual = lax.psum_scatter(
+        jnp.sum((conv_out + biases[None, None]) * weight_rows[:, None, :, None], axis=2),
+        "band",
+        scatter_dimension=0,
+        tiled=True,
+    )
+    block_out, grad_embed_low, shares, gain_grads = middle(
+        attn_qkv,
+        attn_out,
+        mlp_up,
+        mlp_down,
+        residual[0],
+        out_grad[0, 0],
+        norm_gain1.astype(f32)[None],
+        norm_gain2.astype(f32)[None],
+    )
+    block_out = block_out[None, None]
+    grad_embed_low = grad_embed_low[None, None]
+    grad_gain_one, grad_gain_two = gain_grads[0], gain_grads[1]
+    grad_rows = lax.all_gather(grad_embed_low, "band", axis=1, tiled=True)[0].astype(f32)
+    weight_rows = band_weight
+    pixel_rows = pixel_local
+    scaled = grad_rows[:, :, None, :] * weight_rows[:, None, :, None]
+    bias_total = jnp.sum(scaled, axis=(0, 1))
+    scaled_low = scaled.astype(b16)
+    kernel_total = jnp.einsum("inbp,inbd->bpd", pixel_rows, scaled_low, preferred_element_type=f32)
+    pixel_part = jnp.einsum(
+        "inbd,bpd->inbp", scaled_low, kernels, preferred_element_type=f32
+    ).astype(b16)
+    pixel_total = pixel_part
+    kernel_grad, bias_grad, pixel_total = (kernel_total, bias_total, pixel_total)
+    pixel_out = pixel_total[None]
     kernel_grad_low = lax.psum(kernel_grad.astype(b16), "dp").reshape(band_local, -1)
     grad_columns = lax.all_to_all(kernel_grad_low, "band", split_axis=1, concat_axis=0, tiled=True)
     grad_kernel_part = jnp.einsum("nh,nc->hc", code_low, grad_columns, preferred_element_type=f32)
@@ -469,13 +1084,6 @@
     )
     grad_kernel_gen = grad_kernel_part
     hyper_grads = hyper_pull(grad_code)
-    shares = (
-        lax.psum_scatter(grad_qkv.astype(b16), ("band", "dp"), scatter_dimension=0, tiled=True),
-        lax.psum_scatter(grad_out_proj.astype(b16), ("band", "dp"), scatter_dimension=0, tiled=True),
-        lax.psum_scatter(grad_up.astype(b16), ("band", "dp"), scatter_dimension=0, tiled=True),
-        lax.psum_scatter(grad_down.astype(b16), ("band", "dp"), scatter_dimension=0, tiled=True),
-    )
-    shares = tuple(share.astype(f32) for share in shares)
     return (
         block_out,
         pixel_out,
@@ -518,8 +1126,9 @@
         P(("band", "dp"), None),
         P("dp", "band", None, None),
     )
+    whole_block = (mesh.shape["band"], mesh.shape["dp"]) == (16, 2)
     return jax.shard_map(
-        body,
+        fast_body if whole_block else body,
         mesh=mesh,
         in_specs=placed,
         out_specs=(

time: 853 us -> 550 us (0.64)
  waiting for transfers between devices: 512 us -> 218 us
  Pallas kernels: 85.2 us -> 174 us
  matrix products: 86.6 us -> 38.5 us
  local copies, waits for them, and re-layouts: 58.4 us -> 28.8 us
  other arithmetic: 32.4 us -> 17 us
    reduce_scatter x5 -> x1, waiting for transfers between devices: 377 us -> 82.1 us  [fast_body(): lax.psum_scatter(jnp.sum((conv_out + biases[None, None]) * weight_rows[:,...]
    pallas_call x1, Pallas kernels: 85.2 us -> 174 us  [middle(): pl.pallas_call(middle_kernel, out_shape=[jax.ShapeDtypeStruct((tokens, wi...]
    dot_general x26 -> x8, matrix products: 64.6 us -> 21.7 us  [the longest x1 3.91 us: fast_body(): jnp.einsum('inbd,bpd->inbp', scaled_low, kernels, preferred_element_type=...]
    psum x2, waiting for transfers between devices: 87.6 us -> 75 us  [the longest x1 57 us: fast_body(): lax.psum((grad_code_part, grad_bias_part, grad_gain_one, grad_gain_two),...]
    unnamed x190 -> x104, local copies, waits for them, and re-layouts: 23.6 us -> 11.2 us
    all_gather x1, waiting for transfers between devices: 37 us -> 46.8 us  [fast_body(): lax.all_gather(grad_embed_low, 'band', axis=1, tiled=True)[0].astype(f32)]
  transfers between devices with their start and end apart: 10 -> 6, of which waited for: 8 -> 6; matrix products, arithmetic and copies ran while one was open for 13% -> 8% of each run, Pallas kernels for 10% -> 0%
where the time goes in v2:
time: 550 us; the launch traced here: 544 us
  waiting for transfers between devices  218 us (40%)
  Pallas kernels  174 us (32%)
  blocking collectives  38.9 us (7%)
  matrix products  38.5 us (7%)
  local copies, waits for them, and re-layouts  28.8 us (5%)
  other arithmetic  17 us (3%)
  between operations  15.1 us (3%)
  starting transfers between devices  13.4 us (2%)
    pallas_call x1, Pallas kernels, middle(): pl.pallas_call(middle_kernel, out_shape=[jax.ShapeDtypeStruct((tokens, wi...  174 us
    reduce_scatter x1, waiting for transfers between devices, fast_body(): lax.psum_scatter(jnp.sum((conv_out + biases[None, None]) * weight_rows[:,...  82.1 us
    psum x1, waiting for transfers between devices, fast_body(): lax.psum((grad_code_part, grad_bias_part, grad_gain_one, grad_gain_two),...  57 us
    all_gather x1, waiting for transfers between devices, fast_body(): lax.all_gather(grad_embed_low, 'band', axis=1, tiled=True)[0].astype(f32)  46.8 us
    psum x1, blocking collectives, fast_body(): lax.psum((grad_code_part, grad_bias_part, grad_gain_one, grad_gain_two),...  38.9 us
    psum x1, waiting for transfers between devices, fast_body(): lax.psum(kernel_grad.astype(b16), 'dp').reshape(band_local, -1)  18 us
    all_to_all x1, waiting for transfers between devices, fast_body(): lax.all_to_all(column_part, 'band', split_axis=0, concat_axis=1, tiled=True)  11.9 us
    unnamed x104, local copies, waits for them, and re-layouts  11.2 us
  transfers between devices with their start and end apart: 6, of which 6 were waited for; matrix products, arithmetic and copies ran while one was open for 8% of the time, Pallas kernels for 0%

profile of v2, /device:TPU:0, one launch (start us, length us, event | category | flops | bytes accessed | tf_op | source)
XLA Modules:
  0.0 543.8 jit_solution(13502293152836260404)
XLA Ops:
  17.4 2.4 fusion
  22.3 7.4 %all-to-all-start = ((bf16[16,2,6144]{2,1,0:T(2,128)(2,1)}), bf16[16,2,6144]{2,1,0:T(2,128)(2,1)S(1)}, u32[]{:S(2)}, u32[]{:S(2)}) async-start(bf16[16,2,6144]{2,1,0:T(2,128)(2,1)} %reshape.306), calls=%async_computation | async-start | bytes 786432 | tf_op jit(solution)/shard_map/all_to_all | solution.py:1029
  29.9 11.9 %all-to-all-done = bf16[16,2,6144]{2,1,0:T(2,128)(2,1)S(1)} async-done(((bf16[16,2,6144]{2,1,0:T(2,128)(2,1)}), bf16[16,2,6144]{2,1,0:T(2,128)(2,1)S(1)}, u32[]{:S(2)}, u32[]{:S(2)}) %all-to-all-start) | async-done | bytes 393248 | tf_op jit(solution)/shard_map/all_to_all | solution.py:1029
  42.2 2.3 reduce.1
  44.9 3.7 fusion.2
  50.7 82.1 %reduce-scatter.2.cloned.1.call-done = f32[1,128,768]{2,1,0:T(8,128)} async-done(((f32[16,128,768]{2,1,0:T(8,128)}), f32[1,128,768]{2,1,0:T(8,128)}) %reduce-scatter.2.cloned.1.call-update) | async-done | bytes 393232 | tf_op jit(solution)/shard_map/reduce_scatter | solution.py:1041
  132.8 174.0 %gather_block_reduce.1 = (bf16[128,768]{1,0:T(8,128)(2,1)}, bf16[128,768]{1,0:T(8,128)(2,1)}, f32[288,768]{1,0:T(8,128)}, f32[2,768]{1,0:T(2,128)}) custom-call(bf16[288,768]{1,0:T(8,128)(2,1)} %pad_maximum_fusion.shard, f32[128,768]{1,0:T(8,128)} %bitcast.130, bf16[128,768]{1,0:T(8,128)(2,1)} %bitcast.134, f32[1,768]{1,0:T(1,128)} %reshape.286.gain_one, ...), custom_call_target="tpu_custom_call" | custom-call | tf_op jit(solution)/shard_map/gather_block_reduce/pallas_call | solution.py:737
  307.5 46.8 %all-gather.3.cloned.1.call-done = bf16[2048,768]{1,0:T(8,128)(2,1)} async-done(((bf16[128,768]{1,0:T(8,128)(2,1)}), bf16[2048,768]{1,0:T(8,128)(2,1)}) %all-gather.3.cloned.1.call-update) | async-done | bytes 3145744 | tf_op jit(solution)/shard_map/all_gather | solution.py:1060
  354.3 5.4 copy.111
  359.6 3.8 fusion.6
  367.3 1.8 fusion.83
  371.3 18.0 %all-reduce.7.cloned.1.call-done = bf16[1,16,12288]{2,1,0:T(8,128)(2,1)} async-done(((bf16[1,16,12288]{2,1,0:T(8,128)(2,1)}), bf16[1,16,12288]{2,1,0:T(8,128)(2,1)}) %all-reduce.7.cloned.1.call-update) | async-done | bytes 393232 | tf_op jit(solution)/shard_map/psum | solution.py:1073
  391.1 3.0 reduce.10
  395.1 5.7 %all-to-all-start.1 = ((bf16[16,2,6144]{2,1,0:T(2,128)(2,1)}), bf16[16,2,6144]{2,1,0:T(2,128)(2,1)}, u32[]{:S(2)}, u32[]{:S(2)}) async-start(bf16[16,2,6144]{2,1,0:T(2,128)(2,1)} %reshape.308), calls=%async_computation.2 | async-start | bytes 786432 | tf_op jit(solution)/shard_map/all_to_all | solution.py:1074
  401.0 2.8 multiply_reduce_fusion
  405.3 3.9 fusion.4
  410.7 2.3 all-to-all-done.1
  413.0 2.7 reshape.309
  415.7 2.8 convolution_multiply_fusion.1
  419.9 38.9 %all-reduce.3 = (f32[16,128]{1,0:T(8,128)S(1)}, f32[768]{0:T(1024)}, f32[768]{0:T(1024)}) all-reduce(f32[16,128]{1,0:T(8,128)S(1)} %add.77, f32[768]{0:T(1024)} %get-tuple-element.93, f32[768]{0:T(1024)} %get-tuple-element.92), channel_id=1, replica_groups=mesh['band'=16,'dp'=2] {'band','dp'}, use_global_device_ids=true, to_apply=%region_9.10 | all-reduce | flops 3584 | bytes 28672 | tf_op jit(solution)/shard_map/psum | solution.py:1082
  466.4 2.1 fusion.51
  468.5 2.8 fusion.20
  471.3 3.7 fusion.9
  477.4 57.0 %all-reduce.9.cloned.1.call-done = f32[128,768]{1,0:T(8,128)} async-done(((f32[128,768]{1,0:T(8,128)}), f32[128,768]{1,0:T(8,128)}) %all-reduce.9.cloned.1.call-update) | async-done | bytes 393232 | tf_op jit(solution)/shard_map/psum | solution.py:1082
  (186 shorter events, 41.4 us)
Async XLA Ops:
  11.5 295.4 %copy-start.36 = (f32[4,16]{1,0:T(4,128)}, f32[4,16]{1,0:T(4,128)S(1)}, u32[]{:S(2)}) copy-start(f32[4,16]{1,0:T(4,128)S(1)} %fusion.39) | copy-start | bytes 772
  17.4 347.2 %copy-start.21 = (bf16[16,128]{1,0:T(8,128)(2,1)}, bf16[16,128]{1,0:T(8,128)(2,1)S(1)}, u32[]{:S(2)}) copy-start(bf16[16,128]{1,0:T(8,128)(2,1)S(1)} %multiply_convert_fusion.1) | copy-start | bytes 12292
  22.3 19.6 %all-to-all-start = ((bf16[16,2,6144]{2,1,0:T(2,128)(2,1)}), bf16[16,2,6144]{2,1,0:T(2,128)(2,1)S(1)}, u32[]{:S(2)}, u32[]{:S(2)}) async-start(bf16[16,2,6144]{2,1,0:T(2,128)(2,1)} %reshape.306), calls=%async_computation | async-start | bytes 786432 | tf_op jit(solution)/shard_map/all_to_all | solution.py:1029
  29.7 103.1 %reduce-scatter.2.cloned.1.call-start = ((), (), s32[]{:S(2)}) async-start(), calls=%async_computation.3 | async-start | bytes 6684672 | tf_op jit(solution)/shard_map/reduce_scatter | solution.py:1041
  29.9 371.1 %copy-start.33 = (f32[16]{0:T(128)}, f32[16]{0:T(128)S(1)}, u32[]{:S(2)}) copy-start(f32[16]{0:T(128)S(1)} %fusion.65) | copy-start | bytes 196
  48.6 305.7 %all-gather.3.cloned.1.call-start = ((), (), s32[]{:S(2)}) async-start(), calls=%async_computation.6 | async-start | bytes 3342336 | tf_op jit(solution)/shard_map/all_gather | solution.py:1060
  306.8 82.5 %all-reduce.7.cloned.1.call-start = ((), (), s32[]{:S(2)}) async-start(), calls=%async_computation.4 | async-start | bytes 786432 | tf_op jit(solution)/shard_map/psum | solution.py:1073
  395.1 17.9 %all-to-all-start.1 = ((bf16[16,2,6144]{2,1,0:T(2,128)(2,1)}), bf16[16,2,6144]{2,1,0:T(2,128)(2,1)}, u32[]{:S(2)}, u32[]{:S(2)}) async-start(bf16[16,2,6144]{2,1,0:T(2,128)(2,1)} %reshape.308), calls=%async_computation.2 | async-start | bytes 786432 | tf_op jit(solution)/shard_map/all_to_all | solution.py:1074
  400.7 133.7 %all-reduce.9.cloned.1.call-start = ((), (), s32[]{:S(2)}) async-start(), calls=%async_computation.5 | async-start | bytes 786432 | tf_op jit(solution)/shard_map/psum | solution.py:1082
  405.3 57.9 %copy-start.1 = (bf16[128,2048]{1,0:T(8,128)(2,1)S(1)}, bf16[128,2048]{1,0:T(8,128)(2,1)}, u32[]{:S(2)}) copy-start(bf16[128,2048]{1,0:T(8,128)(2,1)} %param.26) | copy-start | bytes 1572868
  410.6 54.4 %copy-start.32 = (f32[16]{0:T(128)S(1)}, f32[16]{0:T(128)}, u32[]{:S(2)}) copy-start(f32[16]{0:T(128)} %copy-done.31) | copy-start | bytes 196
  410.6 54.6 %copy-start.24 = (bf16[128,128]{1,0:T(8,128)(2,1)S(1)}, bf16[128,128]{1,0:T(8,128)(2,1)}, u32[]{:S(2)}) copy-start(bf16[128,128]{1,0:T(8,128)(2,1)} %param.24) | copy-start | bytes 98308
  410.6 54.9 %copy-start.4 = (f32[4,16,16]{1,2,0:T(8,128)S(1)}, f32[4,16,16]{1,2,0:T(8,128)}, u32[]{:S(2)}) copy-start(f32[4,16,16]{1,2,0:T(8,128)} %copy-done.3) | copy-start | bytes 12292
  410.6 54.9 %copy-start.13 = (f32[16,4,32]{2,1,0:T(4,128)S(1)}, f32[16,4,32]{2,1,0:T(4,128)}, u32[]{:S(2)}) copy-start(f32[16,4,32]{2,1,0:T(4,128)} %copy-done.12) | copy-start | bytes 24580
  410.6 54.9 %copy-start.28 = (f32[4,16]{1,0:T(4,128)S(1)}, f32[4,16]{1,0:T(4,128)}, u32[]{:S(2)}) copy-start(f32[4,16]{1,0:T(4,128)} %copy-done.27) | copy-start | bytes 772
  410.6 54.9 %copy-start.34 = (f32[4,16]{1,0:T(4,128)S(1)}, f32[4,16]{1,0:T(4,128)}, u32[]{:S(2)}) copy-start(f32[4,16]{1,0:T(4,128)} %multiply_divide_fusion) | copy-start | bytes 772
  410.7 55.1 %copy-start.11 = (f32[16,4,32]{2,1,0:T(4,128)S(1)}, f32[16,4,32]{2,1,0:T(4,128)}, u32[]{:S(2)}) copy-start(f32[16,4,32]{2,1,0:T(4,128)} %copy-done.10) | copy-start | bytes 24580
  410.7 55.1 %copy-start.37 = (f32[4,16]{1,0:T(4,128)S(1)}, f32[4,16]{1,0:T(4,128)}, u32[]{:S(2)}) copy-start(f32[4,16]{1,0:T(4,128)} %copy-done.36) | copy-start | bytes 772
  410.7 55.4 %copy-start.9 = (f32[16,4,32]{2,1,0:T(4,128)S(1)}, f32[16,4,32]{2,1,0:T(4,128)}, u32[]{:S(2)}) copy-start(f32[16,4,32]{2,1,0:T(4,128)} %copy-done.8) | copy-start | bytes 24580
  410.7 60.6 %copy-start.22 = (bf16[16,128]{1,0:T(8,128)(2,1)S(1)}, bf16[16,128]{1,0:T(8,128)(2,1)}, u32[]{:S(2)}) copy-start(bf16[16,128]{1,0:T(8,128)(2,1)} %copy-done.21) | copy-start | bytes 12292
  418.6 56.7 %copy-start.15 = (f32[16,64]{1,0:T(8,128)S(1)}, f32[16,64]{1,0:T(8,128)}, u32[]{:S(2)}) copy-start(f32[16,64]{1,0:T(8,128)} %copy-done.14) | copy-start | bytes 12292
  418.6 56.7 %copy-start.17 = (f32[16,64]{1,0:T(8,128)S(1)}, f32[16,64]{1,0:T(8,128)}, u32[]{:S(2)}) copy-start(f32[16,64]{1,0:T(8,128)} %copy-done.16) | copy-start | bytes 12292
  418.6 57.9 %copy-start.20 = (f32[16,128]{1,0:T(8,128)S(1)}, f32[16,128]{1,0:T(8,128)}, u32[]{:S(2)}) copy-start(f32[16,128]{1,0:T(8,128)} %copy-done.19) | copy-start | bytes 24580
  418.6 115.8 %copy-start.5 = (bf16[128,768]{1,0:T(8,128)(2,1)S(1)}, bf16[128,768]{1,0:T(8,128)(2,1)}, u32[]{:S(2)}) copy-start(bf16[128,768]{1,0:T(8,128)(2,1)} %get-tuple-element.20) | copy-start | bytes 589828
  (30 other events, 394.4 us)
Sparse Core Ops, SparseCore 0:
  48.7 84.0 reduce-scatter.1
  306.9 47.2 all-gather.2
  364.7 24.5 all-reduce.6
  406.6 127.7 all-reduce.8

commit v3 on v2

--- a/solution.py
+++ b/solution.py
@@ -122,24 +122,35 @@
     return pl.multiple_of(rows, 16)
 
 
-def meet_neighbours():
-    z, x, core, y = place()
-    barrier = pltpu.get_barrier_semaphore()
-    near = [
-        (device(z, x, 1 - core, y), True),
-        (device(z, 1 - x, core, y), True),
-        (device(z, x, core, 1 - y), True),
-        (device(z + 1, x, core, y), z < 3),
-        (device(z - 1, x, core, y), z > 0),
-    ]
-    for target, cond in near:
-        when(
-            cond,
-            lambda target=target: pl.semaphore_signal(
-                barrier, inc=1, device_id=target, device_id_type=MESH
-            ),
-        )
-    pl.semaphore_wait(barrier, 5 - z // 3 - (3 - z) // 3)
+def meet_peers(barrier):
+    tell_peers(barrier)
+    pl.semaphore_wait(barrier, lax.axis_size("band"))
+
+
+def tell_peers(barrier):
+    band, y = lax.axis_index("band"), lax.axis_index("dp")
+    bands = lax.axis_size("band")
+    for step in range(1, bands):
+        pl.semaphore_signal(
+            barrier, inc=1, device_id=((band + step) % bands, y), device_id_type=MESH
+        )
+    pl.semaphore_signal(barrier, inc=1, device_id=(band, 1 - y), device_id_type=MESH)
+
+
+class Stream:
+    def __init__(self, events):
+        self.events = sorted(events, key=lambda event: event[:2])
+        self.at = 0
+
+    def run(self, count=None):
+        last = len(self.events) if count is None else min(len(self.events), self.at + count)
+        for _, _, work in self.events[self.at : last]:
+            work()
+        self.at = last
+
+    def until(self, time):
+        while self.at < len(self.events) and self.events[self.at][0] <= time:
+            self.run(1)
 
 
 class Gather:
@@ -150,6 +161,12 @@
         self.z, self.x, self.core, self.y = place()
         self.sends = []
         self.count = [0] * len(orders)
+
+    def rail(self, block):
+        return block[0] * 4 + block[1] * 2 + block[2]
+
+    def sibling(self):
+        return device(self.z, self.x, 1 - self.core, self.y)
 
     def send(self, chunk, block, dim, cond, direction=0):
         z, x, core, y = self.z, self.x, self.core, self.y
@@ -163,14 +180,13 @@
                 targets.append((device(z + 1, x, core, y), both(cond, z < 3)))
             if direction <= 0:
                 targets.append((device(z - 1, x, core, y), both(cond, z > 0)))
-        src = self.view(chunk, slot(block[0], block[1], core, block[2]))
-        rail = block[0] * 4 + block[1] * 2 + block[2]
+        src = self.view(chunk, block, core)
         for target, needed in targets:
             copy = pltpu.make_async_remote_copy(
                 src_ref=src,
                 dst_ref=src,
                 send_sem=self.send_sem.at[chunk, self.count[chunk]],
-                recv_sem=self.recv_sem.at[chunk, rail],
+                recv_sem=self.recv_sem.at[chunk, self.rail(block)],
                 device_id=target,
                 device_id_type=MESH,
             )
@@ -179,14 +195,13 @@
             self.sends.append((needed, copy))
 
     def pair(self, chunk, block, core):
-        src = self.view(chunk, slot(block[0], block[1], core, block[2]))
-        rail = block[0] * 4 + block[1] * 2 + block[2]
+        src = self.view(chunk, block, core)
         return pltpu.make_async_remote_copy(
             src_ref=src,
             dst_ref=src,
-            send_sem=self.pair_send.at[chunk, rail],
-            recv_sem=self.pair_recv.at[chunk, rail],
-            device_id=device(self.z, self.x, 1 - self.core, self.y),
+            send_sem=self.pair_send.at[chunk, self.rail(block)],
+            recv_sem=self.pair_recv.at[chunk, self.rail(block)],
+            device_id=self.sibling(),
             device_id_type=MESH,
         )
 
@@ -196,19 +211,19 @@
             self.send(chunk, own, dim, True)
         self.pair(chunk, own, self.core).start()
 
-    def events(self, chunk):
-        held, found = [(0, 0, 0, 0, 0.0)], []
+    def events(self, chunk, start=0.0, pace=1.0):
+        held, found = [(0, 0, 0, 0, start)], []
         for dim in self.orders[chunk]:
             clock, new = 0.0, []
             ordered = sorted(held, key=lambda item: item[4])
             if dim == "z":
                 for dist in (1, 2, 3):
                     for item in ordered:
-                        clock = max(clock, item[4]) + 1.0
+                        clock = max(clock, item[4]) + pace
                         new += [(dist, way, item[2], item[3], clock) for way in (1, -1)]
             else:
                 for item in ordered:
-                    clock = max(clock, item[4]) + 1.0
+                    clock = max(clock, item[4]) + pace
                     flip = (1, item[3]) if dim == "x" else (item[2], 1)
                     new.append((item[0], item[1], *flip, clock))
             found += [
@@ -229,14 +244,13 @@
             1 - self.x if flip_x else self.x,
             1 - self.y if flip_y else self.y,
         )
-        src = self.view(chunk, slot(block[0], block[1], self.core, block[2]))
-        rail = block[0] * 4 + block[1] * 2 + block[2]
+        src = self.view(chunk, block, self.core)
         arriving = pltpu.make_async_remote_copy(
             src_ref=src,
             dst_ref=src,
             send_sem=self.send_sem.at[chunk, 0],
-            recv_sem=self.recv_sem.at[chunk, rail],
-            device_id=device(self.z, self.x, 1 - self.core, self.y),
+            recv_sem=self.recv_sem.at[chunk, self.rail(block)],
+            device_id=self.sibling(),
             device_id_type=MESH,
         )
         when(cond, arriving.wait_recv)
@@ -247,19 +261,26 @@
             self.send(chunk, block, later, cond)
         when(cond, self.pair(chunk, block, self.core).start)
 
+    def blocks(self, chunk):
+        planes = (0, 1) if "y" in self.orders[chunk] else (self.y,)
+        return [(zz, xx, yy) for zz in range(4) for xx in (0, 1) for yy in planes]
+
+    def wait_pairs(self, chunk):
+        for block in self.blocks(chunk):
+            self.pair(chunk, block, 1 - self.core).wait_recv()
+
     def finish(self):
         for needed, copy in self.sends:
             when(needed, copy.wait_send)
         for chunk in range(len(self.orders)):
-            for rail in range(16):
-                block = (rail // 4, (rail // 2) % 2, rail % 2)
+            for block in self.blocks(chunk):
                 self.pair(chunk, block, self.core).wait_send()
-                self.pair(chunk, block, 1 - self.core).wait_recv()
 
 
 class Reduce:
-    def __init__(self, view, orders, pair_view, pair_buf, buf, pair_send, pair_recv, send, recv):
-        self.view, self.orders = view, tuple(order[::-1] for order in orders)
+    def __init__(self, parts, view, orders, final, pair_view, pair_buf, buf, pair_send, pair_recv, send, recv):
+        self.parts = parts
+        self.view, self.orders, self.final = view, orders, final
         self.pair_view, self.pair_buf, self.buf = pair_view, pair_buf, buf
         self.pair_send, self.pair_recv = pair_send, pair_recv
         self.send_sem, self.recv_sem = send, recv
@@ -268,87 +289,106 @@
         self.count = [0] * len(orders)
         self.index = [{} for _ in orders]
 
+    def rail(self, block):
+        if "y" not in self.orders[0]:
+            return block[0] * 2 + block[1]
+        return block[0] * 4 + block[1] * 2 + block[2]
+
     def coords(self, block):
         zz, flip_x, flip_y = block
         return (zz, 1 - self.x if flip_x else self.x, 1 - self.y if flip_y else self.y)
 
     def own(self, chunk, block):
-        zz, xx, yy = self.coords(block)
-        return self.view(chunk, slot(zz, xx, self.core, yy))
+        return self.view(chunk, self.coords(block), self.core)
 
     def add(self, target, source):
         target[...] = target[...] + source[...]
 
-    def pair_copy(self, part, rail):
-        block = (rail // 4, (rail // 2) % 2, rail % 2)
+    def sibling(self):
+        return device(self.z, self.x, 1 - self.core, self.y)
+
+    def pair_copy(self, part, block):
         return pltpu.make_async_remote_copy(
-            src_ref=self.pair_view(part, slot(block[0], block[1], 1 - self.core, block[2])),
-            dst_ref=self.pair_buf.at[part, rail],
-            send_sem=self.pair_send.at[part, rail],
-            recv_sem=self.pair_recv.at[part, rail],
-            device_id=device(self.z, self.x, 1 - self.core, self.y),
+            src_ref=self.pair_view(part, block, 1 - self.core),
+            dst_ref=self.pair_buf(part, self.rail(block)),
+            send_sem=self.pair_send.at[part, self.rail(block)],
+            recv_sem=self.pair_recv.at[part, self.rail(block)],
+            device_id=self.sibling(),
             device_id_type=MESH,
         )
+
+    def pair_start(self, part, blocks=None):
+        for block in blocks or self.blocks():
+            self.pair_copy(part, self.coords(block)).start()
+
+    def blocks(self):
+        dims = self.orders[0]
+        return [
+            (zz, fx, fy)
+            for fx in ((1, 0) if "x" in dims else (0,))
+            for fy in ((1, 0) if "y" in dims else (0,))
+            for zz in (3, 0, 2, 1)
+        ]
 
     def place_of(self, chunk, key):
         return self.index[chunk].setdefault(key, len(self.index[chunk]))
 
-    def copy(self, chunk, block, key, target):
+    def send(self, chunk, block, key, target, cond):
         where = self.place_of(chunk, key)
-        number = self.count[chunk]
-        self.count[chunk] += 1
-        return pltpu.make_async_remote_copy(
+        copy = pltpu.make_async_remote_copy(
             src_ref=self.own(chunk, block),
-            dst_ref=self.buf.at[chunk, where],
-            send_sem=self.send_sem.at[chunk, number],
+            dst_ref=self.buf(chunk, where),
+            send_sem=self.send_sem.at[chunk, self.count[chunk]],
             recv_sem=self.recv_sem.at[chunk, where],
             device_id=target,
             device_id_type=MESH,
         )
-
-    def send(self, chunk, block, key, target, cond):
-        copy = self.copy(chunk, block, key, target)
+        self.count[chunk] += 1
         when(cond, copy.start)
         self.sends.append((cond, copy))
 
-    def wait_add(self, chunk, block, key):
-        where = self.place_of(chunk, key)
-        landed = self.buf.at[chunk, where]
+    def landed(self, chunk, key):
+        return self.buf(chunk, self.place_of(chunk, key))
+
+    def wait(self, chunk, key):
+        landed = self.landed(chunk, key)
         pltpu.make_async_remote_copy(
             src_ref=landed,
             dst_ref=landed,
             send_sem=self.send_sem.at[chunk, 0],
-            recv_sem=self.recv_sem.at[chunk, where],
-            device_id=device(self.z, self.x, 1 - self.core, self.y),
+            recv_sem=self.recv_sem.at[chunk, self.place_of(chunk, key)],
+            device_id=self.sibling(),
             device_id_type=MESH,
         ).wait_recv()
-        self.add(self.own(chunk, block), landed)
 
     def flips(self, chunk, stage):
         left = self.orders[chunk][stage:]
-        out = [(fx, fy) for fx in ((1, 0) if "x" in left else (0,)) for fy in ((1, 0) if "y" in left else (0,))]
-        return out
-
-    def pair_order(self, part):
-        return [8 * h + r for h in (0, 1) for r in range(8)]
-
-    def ready(self, chunk, stage, block, cond=True):
+        return [
+            (fx, fy)
+            for fx in ((1, 0) if "x" in left else (0,))
+            for fy in ((1, 0) if "y" in left else (0,))
+        ]
+
+    def ready(self, chunk, stage, block):
         order = self.orders[chunk]
-        if stage == 3:
-            return
-        dim = order[stage]
         zz, fx, fy = block
-        if dim == "x" and fx:
+        where = zz if "z" in order[stage:] else "own"
+        if order[stage] == "x" and fx:
             target = device(self.z, 1 - self.x, self.core, self.y)
-            self.send(chunk, block, (stage, zz if "z" in order[stage:] else "own", 0, fy), target, cond)
-        elif dim == "y" and fy:
+            self.send(chunk, block, (stage, where, 0, fy), target, True)
+        elif order[stage] == "y" and fy:
             target = device(self.z, self.x, self.core, 1 - self.y)
-            self.send(chunk, block, (stage, zz if "z" in order[stage:] else "own", fx, 0), target, cond)
+            self.send(chunk, block, (stage, where, fx, 0), target, True)
+
+    def z_key(self, stage, step, way, flips):
+        return (stage, step, way if step else 0, *flips)
 
     def z_start(self, chunk, stage, step, flips):
         up, down = (3 - step, *flips), (step, *flips)
-        self.send(chunk, up, (stage, step, 1, *flips), device(self.z + 1, self.x, self.core, self.y), self.z == 0)
-        self.send(chunk, down, (stage, step, -1, *flips), device(self.z - 1, self.x, self.core, self.y), self.z == 3)
+        right = device(self.z + 1, self.x, self.core, self.y)
+        left = device(self.z - 1, self.x, self.core, self.y)
+        self.send(chunk, up, self.z_key(stage, step, 1, flips), right, self.z == 0)
+        self.send(chunk, down, self.z_key(stage, step, -1, flips), left, self.z == 3)
 
     def z_arrive(self, chunk, stage, step, flips, way):
         z = self.z if way == 1 else 3 - self.z
@@ -356,87 +396,143 @@
         zz = 2 + z - step
         zz = zz if way == 1 else 3 - zz
         block = (zz, *flips)
-        key = (stage, step, way, *flips)
-        when(cond, lambda: self.wait_add(chunk, block, key))
+        key = self.z_key(stage, step, way, flips)
+        last = stage + 1 == len(self.orders[chunk]) and step == 2
+
+        def take():
+            self.wait(chunk, key)
+            if not last:
+                self.add(self.own(chunk, block), self.landed(chunk, key))
+
+        when(cond, take)
         if step < 2:
-            self.send(
-                chunk, block, (stage, step + 1, way, *flips),
-                device(self.z + way, self.x, self.core, self.y), cond,
-            )
+            target = device(self.z + way, self.x, self.core, self.y)
+            self.send(chunk, block, self.z_key(stage, step + 1, way, flips), target, cond)
 
     def z_done(self, chunk, stage, flips):
-        self.ready(chunk, stage + 1, (self.z, *flips))
+        block = (self.z, *flips)
+        if stage + 1 < len(self.orders[chunk]):
+            self.ready(chunk, stage + 1, block)
+            return
+        final = self.final(chunk)
+        final[...] = self.own(chunk, block)[...].astype(F32)
+        for way, cond in ((1, self.z >= 1), (-1, self.z <= 2)):
+            landed = self.landed(chunk, self.z_key(stage, 2, way, flips))
+
+            @pl.when(cond)
+            def _(landed=landed):
+                final[...] += landed[...].astype(F32)
 
     def xy_arrive(self, chunk, stage, zz, fx, fy):
         key = (stage, zz, fx, fy)
         block = (self.z if zz == "own" else zz, fx, fy)
-        self.wait_add(chunk, block, key)
-        self.ready(chunk, stage + 1, block)
+        self.wait(chunk, key)
+        own, landed = self.own(chunk, block), self.landed(chunk, key)
+        if stage + 1 < len(self.orders[chunk]):
+            self.add(own, landed)
+            self.ready(chunk, stage + 1, block)
+        else:
+            final = self.final(chunk)
+            final[...] = own[...].astype(F32) + landed[...].astype(F32)
 
     def pair_arrive(self, part, block, chunks):
-        zz, xx, yy = self.coords(block)
-        rail = zz * 4 + xx * 2 + yy
-        copy = pltpu.make_async_remote_copy(
-            src_ref=self.pair_buf.at[part, rail],
-            dst_ref=self.pair_buf.at[part, rail],
-            send_sem=self.pair_send.at[part, rail],
-            recv_sem=self.pair_recv.at[part, rail],
-            device_id=device(self.z, self.x, 1 - self.core, self.y),
+        where = self.coords(block)
+        landed = self.pair_buf(part, self.rail(where))
+        pltpu.make_async_remote_copy(
+            src_ref=landed,
+            dst_ref=landed,
+            send_sem=self.pair_send.at[part, self.rail(where)],
+            recv_sem=self.pair_recv.at[part, self.rail(where)],
+            device_id=self.sibling(),
             device_id_type=MESH,
-        )
-        copy.wait_recv()
-        self.add(self.pair_view(part, slot(zz, xx, self.core, yy)), self.pair_buf.at[part, rail])
+        ).wait_recv()
+        self.add(self.pair_view(part, where, self.core), landed)
         for chunk in chunks:
             self.ready(chunk, 0, block)
 
-    def events(self, part, chunks):
+    def events(self, part, chunks, start=0.0, pace=1.0, pair_pace=0.5):
         found, ready = [], {}
-        number = 0
-        clock = 0.0
-        for fx, fy in ((1, 1), (1, 0), (0, 1), (0, 0)):
-            for zz in (3, 0, 2, 1):
-                clock += 0.5
-                found.append((clock, 0, functools.partial(self.pair_arrive, part, (zz, fx, fy), chunks)))
-                ready[(zz, fx, fy)] = clock
+        clock = start
+        for block in self.blocks():
+            clock += pair_pace
+            found.append((clock, 0, functools.partial(self.pair_arrive, part, block, chunks)))
+            ready[block] = clock
         for chunk in chunks:
             times = dict(ready)
-            order = self.orders[chunk]
-            for stage, dim in enumerate(order):
-                clock = 0.0
-                nxt = {}
-                flips = self.flips(chunk, stage)
+            for stage, dim in enumerate(self.orders[chunk]):
+                clock, later = 0.0, {}
                 if dim == "z":
                     for step in range(3):
-                        for fl in flips:
+                        for flips in self.flips(chunk, stage):
                             needed = (0, 3) if step == 0 else (0, 1, 2, 3)
-                            clock = max(clock, *(times[(zz, *fl)] for zz in needed)) + 0.001
-                            found.append((clock, chunk, functools.partial(self.z_start, chunk, stage, step, fl)))
-                            clock += 1.0
+                            clock = max(clock, *(times[(zz, *flips)] for zz in needed)) + 0.001
+                            work = functools.partial(self.z_start, chunk, stage, step, flips)
+                            found.append((clock, chunk, work))
+                            clock += pace
                             for way in (1, -1):
-                                found.append((clock, chunk, functools.partial(self.z_arrive, chunk, stage, step, fl, way)))
-                            nxt[("own", *fl)] = clock + 0.001
-                    for fl in flips:
-                        found.append((nxt[("own", *fl)], chunk, functools.partial(self.z_done, chunk, stage, fl)))
+                                work = functools.partial(self.z_arrive, chunk, stage, step, flips, way)
+                                found.append((clock, chunk, work))
+                            later[("own", *flips)] = clock + 0.001
+                    for flips in self.flips(chunk, stage):
+                        work = functools.partial(self.z_done, chunk, stage, flips)
+                        found.append((later[("own", *flips)], chunk, work))
                 else:
-                    pick = 0 if dim == "x" else 1
-                    sent = [key for key in times if key[1 + pick] == 1]
-                    kept = {}
-                    for key in sorted(sent, key=lambda key: times[key]):
-                        clock = max(clock, times[key]) + 1.0
+                    pick = 1 if dim == "x" else 2
+                    for key in sorted((k for k in times if k[pick]), key=lambda k: times[k]):
                         mine = (key[0], 0, key[2]) if dim == "x" else (key[0], key[1], 0)
-                        clock = max(clock, times[mine] + 0.001)
-                        kept[mine] = clock
-                        found.append((clock, chunk, functools.partial(self.xy_arrive, chunk, stage, *mine)))
-                    nxt = kept
-                times = nxt
-        return sorted(found, key=lambda event: event[:2])
+                        clock = max(max(clock, times[key]) + pace, times[mine] + 0.001)
+                        later[mine] = clock
+                        work = functools.partial(self.xy_arrive, chunk, stage, *mine)
+                        found.append((clock, chunk, work))
+                times = later
+        return found
 
     def finish(self):
         for cond, copy in self.sends:
             when(cond, copy.wait_send)
-        for part in range(self.pair_buf.shape[0]):
-            for rail in range(16):
-                self.pair_copy(part, rail).wait_send()
+        for part in range(self.parts):
+            for block in self.blocks():
+                self.pair_copy(part, self.coords(block)).wait_send()
+
+
+class Exchange:
+    def __init__(self, source, landing, send_sem, recv_sem):
+        self.source, self.landing = source, landing
+        self.send_sem, self.recv_sem = send_sem, recv_sem
+        self.band, self.y = lax.axis_index("band"), lax.axis_index("dp")
+        self.bands = lax.axis_size("band")
+
+    def copy(self, target):
+        return pltpu.make_async_remote_copy(
+            src_ref=self.source(target),
+            dst_ref=self.landing(self.band),
+            send_sem=self.send_sem.at[target],
+            recv_sem=self.recv_sem.at[self.band],
+            device_id=(target, self.y),
+            device_id_type=MESH,
+        )
+
+    def others(self):
+        return [(self.band + step) % self.bands for step in range(1, self.bands)]
+
+    def start(self):
+        for target in self.others():
+            self.copy(target).start()
+
+    def wait(self):
+        for other in self.others():
+            pltpu.make_async_remote_copy(
+                src_ref=self.landing(other),
+                dst_ref=self.landing(other),
+                send_sem=self.send_sem.at[other],
+                recv_sem=self.recv_sem.at[other],
+                device_id=(other, self.y),
+                device_id_type=MESH,
+            ).wait_recv()
+
+    def finish(self):
+        for target in self.others():
+            self.copy(target).wait_send()
 
 
 def dot_nt(left, right):
@@ -464,6 +560,9 @@
         self.width = weights.shape[1]
         self.halves = weights.shape[1] // (2 * HEAD_DIM)
 
+    def weight(self, part):
+        return self.weights[pl.ds(aligned(part * self.width), self.width), :]
+
     def masks(self):
         tokens = self.joint.shape[1]
         lane = lax.broadcasted_iota(jnp.int32, (tokens, 2 * HEAD_DIM), 1)
@@ -482,7 +581,7 @@
 
         @pl.loop(0, 3)
         def _(part):
-            self.joint[part] = dot_nn(self.normed_one[...], self.weights[part]).astype(B16)
+            self.joint[part] = dot_nn(self.normed_one[...], self.weight(part)).astype(B16)
 
     def attend(self):
         tokens = self.joint.shape[1]
@@ -501,7 +600,7 @@
             self.mixed[:, lanes] = jnp.where(where, mixed[:tokens], mixed[tokens:]).astype(B16)
 
     def widen(self):
-        middle = self.residual[...] + dot_nn(self.mixed[...], self.weights[3])
+        middle = self.residual[...] + dot_nn(self.mixed[...], self.weight(3))
         unit, inverse = unit_parts(middle)
         self.normed_two[...] = (unit * self.gain_two[...]).astype(B16)
         self.unit_two[...] = unit
@@ -510,7 +609,7 @@
 
         @pl.loop(0, 4)
         def _(part):
-            pre = dot_nn(self.normed_two[...], self.weights[4 + part])
+            pre = dot_nn(self.normed_two[...], self.weight(4 + part))
             self.pre_act[part] = pre
             self.act[part] = gelu_tanh(pre).astype(B16)
 
@@ -527,7 +626,7 @@
         grad_act = dot_nt(self.out_grad[...], self.down[rows, :])
         grad_pre = (grad_act * gelu_slope(self.pre_act[part])).astype(B16)
         self.grad_pre[part] = grad_pre
-        self.grad_normed[...] += dot_nt(grad_pre, self.weights[4 + part])
+        self.grad_normed[...] += dot_nt(grad_pre, self.weight(4 + part))
 
     def down_grad(self, part, store):
         turned = self.act[part].T
@@ -554,7 +653,7 @@
     def back_wide(self):
         grad_normed = self.grad_normed[...]
         unit = self.unit_two[...]
-        self.gain_grads[1:2, :] = jnp.sum(grad_normed * unit, axis=0, keepdims=True)
+        self.small[1:2, :] = jnp.sum(grad_normed * unit, axis=0, keepdims=True)
         scaled = grad_normed * self.gain_two[...]
         back = self.inverse_two[:, :1] * (
             scaled
@@ -565,7 +664,7 @@
         self.grad_middle[...] = grad_middle
         branch = grad_middle.astype(B16)
         self.grad_branch[...] = branch
-        self.grad_mixed[...] = dot_nt(branch, self.weights[3]).astype(B16)
+        self.grad_mixed[...] = dot_nt(branch, self.weight(3)).astype(B16)
         self.turned_mixed[...] = self.mixed[...].T
 
     def back_attend(self):
@@ -595,11 +694,11 @@
 
         @pl.loop(0, 3)
         def _(part):
-            self.grad_normed[...] += dot_nt(self.grad_joint[part], self.weights[part])
+            self.grad_normed[...] += dot_nt(self.grad_joint[part], self.weight(part))
 
         grad_normed = self.grad_normed[...]
         unit = self.unit_one[...]
-        self.gain_grads[0:1, :] = jnp.sum(grad_normed * unit, axis=0, keepdims=True)
+        self.small[0:1, :] = jnp.sum(grad_normed * unit, axis=0, keepdims=True)
         scaled = grad_normed * self.gain_one[...]
         back = self.inverse_one[:, :1] * (
             scaled
@@ -611,6 +710,7 @@
 
 def spread(gathered, weights, chunk):
     part, offset = chunk // 2, (chunk % 2) * CHUNK
+    width = weights.shape[1]
 
     @pl.loop(0, 16)
     def _(two):
@@ -618,25 +718,50 @@
             gathered[part, pl.ds(aligned((two * 2 + k) * PART + offset), CHUNK), :].astype(F32)
             for k in (0, 1)
         )
-        rows = pl.ds(aligned(two * CHUNK), CHUNK)
         half = CHUNK // 2
-        weights[2 * chunk, rows, :] = jnp.concatenate([one[:half], other[:half]], 0).astype(B16)
-        weights[2 * chunk + 1, rows, :] = jnp.concatenate([one[half:], other[half:]], 0).astype(B16)
-
-
-def middle_kernel(shard, residual, out_grad, gain_one, gain_two, block_out, grad_embed, shares, gain_grads, *scratch):
-    (gathered, weights, down_grads, pair_buf, buf, joint, probs, pre_act, act, grad_pre, mixed, normed_one, normed_two,
-     unit_one, unit_two, inverse_one, inverse_two, result, grad_normed, grad_middle, grad_branch, grad_mixed, grad_joint,
-     turned_mixed, turned_one, turned_two, local_sem, *sems) = scratch
-    names = dict(
-        residual=residual, out_grad=out_grad, gain_one=gain_one, gain_two=gain_two, block_out=block_out,
-        grad_embed=grad_embed, gain_grads=gain_grads, joint=joint, probs=probs, pre_act=pre_act, act=act,
-        grad_pre=grad_pre, mixed=mixed, normed_one=normed_one, normed_two=normed_two, unit_one=unit_one,
-        unit_two=unit_two, inverse_one=inverse_one, inverse_two=inverse_two, result=result, grad_normed=grad_normed,
-        grad_middle=grad_middle, grad_branch=grad_branch, grad_mixed=grad_mixed, grad_joint=grad_joint,
-        turned_mixed=turned_mixed,
-    )
-    me = slot(*place())
+        for k, rows in ((0, slice(0, half)), (1, slice(half, CHUNK))):
+            target = pl.ds(aligned((2 * chunk + k) * width + two * CHUNK), CHUNK)
+            weights[target, :] = jnp.concatenate([one[rows], other[rows]], 0).astype(B16)
+
+
+def swap_rows(rows):
+    count = rows.shape[0]
+    row = lax.broadcasted_iota(jnp.int32, (count, count), 0)
+    col = lax.broadcasted_iota(jnp.int32, (count, count), 1)
+    swap = (col == (row % 16) * 16 + row // 16).astype(F32).astype(B16)
+    return dot_nn(swap, rows).astype(B16)
+
+
+def rows16(ref, index):
+    return ref.at[pl.ds(aligned(index * 16), 16)]
+
+
+def layer_kernel(*refs):
+    (shard, pixels, kernel_gen, code_low, bias_gen, band_scale, out_grad, gain_one, gain_two,
+     block_out, pixel_out, shares, kernel_grads, code_grads, vectors,
+     gathered, weights, spare, pair_buf, buf, joint, probs, pre_act, act, grad_pre, mixed, normed_one, normed_two,
+     unit_one, unit_two, inverse_one, inverse_two, grad_normed, grad_middle, grad_branch, grad_mixed, grad_joint,
+     turned_mixed, turned_one, turned_two, residual, pixel_rows, turned_pixels, mixing, kernels, sending,
+     image_grads, kernel_total, partner_grads, landed_grads, small, small_partner, small_all, code_part, code_all,
+     local_sem, pix_sem, gen_sem, front_done, *sems) = refs
+    z, x, core, y = place()
+    band = lax.axis_index("band")
+    bands = lax.axis_size("band")
+    me = slot(z, x, core, y)
+    width = gain_one.shape[1]
+    tokens = out_grad.shape[0]
+    partner = (band, 1 - y)
+    (gather_sems, reduce_sems, embed_sems, grads_sems, kernel_sems, cols_sems, vec_sems, code_sems, half_sems, vec_half_sems) = (
+        sems[0:4], sems[4:8], sems[8:12], sems[12:16], sems[16:18], sems[18:20], sems[20:22], sems[22:24], sems[24:26], sems[26:28]
+    )
+
+    def gen_copy(piece, target, at):
+        return pltpu.make_async_copy(
+            kernel_gen.at[:, pl.ds(piece * width, width)], target.at[pl.ds(at, 128)], gen_sem.at[piece]
+        )
+
+    for piece in range(16):
+        gen_copy(piece, spare, piece * 128).start()
     own = [
         pltpu.make_async_copy(
             shard.at[pl.ds(part * PART, PART)],
@@ -647,24 +772,100 @@
     ]
     for copy in own:
         copy.start()
+    load_pixels = pltpu.make_async_copy(pixels, pixel_rows, pix_sem)
+    load_pixels.start()
+    meet_peers(pltpu.get_barrier_semaphore())
     for copy in own:
         copy.wait()
-    meet_neighbours()
-
-    def weight_view(chunk, where):
+
+    def weight_view(chunk, block, side):
+        where = slot(block[0], block[1], side, block[2])
         return gathered.at[chunk // 2, pl.ds(aligned(where * PART + (chunk % 2) * CHUNK), CHUNK)]
 
-    gather = Gather(weight_view, ORDERS, *sems[:4])
-    events = []
+    gather = Gather(weight_view, ORDERS, *gather_sems)
+    arrivals = []
     for chunk in range(len(ORDERS)):
+        arrivals += gather.events(chunk)
+    arrivals = Stream(arrivals)
+    for chunk in FIRST_CHUNKS:
         gather.start(chunk)
-        events += gather.events(chunk)
-    for _, _, run in sorted(events, key=lambda event: event[:2]):
-        run()
+
+    for piece in range(16):
+        gen_copy(piece, spare, piece * 128).wait()
+
+    @pl.loop(0, 16)
+    def _(piece):
+        part = dot_nn(code_low[...], spare[pl.ds(aligned(piece * 128), 128), :])
+        mixing[pl.ds(aligned(piece * 16), 16), :] = part.astype(B16)
+
+    sending[...] = swap_rows(mixing[...])
+    spread_kernels = Exchange(
+        lambda target: rows16(sending, target), lambda source: rows16(kernels, source), *kernel_sems
+    )
+    spread_kernels.start()
+    for chunk in range(len(ORDERS)):
+        if chunk not in FIRST_CHUNKS:
+            gather.start(chunk)
+    own_rows = pl.ds(aligned(band * 16), 16)
+    kernels[own_rows, :] = sending[own_rows, :]
+    biases = dot_nn(code_low[...], bias_gen[...])
+    chosen = lax.broadcasted_iota(jnp.int32, biases.shape, 0) == band
+    bias = jnp.sum(jnp.where(chosen, biases, 0.0), axis=0, keepdims=True)
+    load_pixels.wait()
+    for group in range(4):
+        turned_pixels[group] = pixel_rows[4 * group : 4 * group + 4].reshape(4 * tokens, -1).T
+    arrivals.run(EARLY)
+    spread_kernels.wait()
+
+    @pl.loop(0, 4)
+    def _(group):
+        rows = pixel_rows[pl.ds(group * 4, 4)].reshape(4 * tokens, -1)
+        for at in range(0, width, 256):
+            terms = dot_nn(rows, kernels[:, at : at + 256]) + bias[:, at : at + 256]
+            for image in range(4):
+                scale = band_scale[group * 4 + image][:1, :1]
+                target = pl.ds(aligned((group * 4 + image) * tokens), tokens)
+                spare[target, at : at + 256] = (
+                    terms[image * tokens : (image + 1) * tokens] * scale
+                ).astype(B16)
+
+    half = tokens // 2
+
+    def image_row(block, side):
+        return (block[0] * 4 + block[1] * 2 + side) * tokens
+
+    embed = Reduce(
+        1,
+        lambda chunk, block, side: spare.at[pl.ds(aligned(image_row(block, side) + chunk * half), half)],
+        ("xz", "xz"),
+        lambda chunk: residual.at[pl.ds(chunk * half, half)],
+        lambda part, block, side: spare.at[pl.ds(aligned(image_row(block, side)), tokens)],
+        lambda part, rail: pair_buf.at[0, pl.ds(aligned(rail * tokens), tokens)],
+        lambda chunk, where: pair_buf.at[1, pl.ds((chunk * 9 + where) * half, half)],
+        *embed_sems,
+    )
+    embed.pair_start(0)
+    sums = Stream(embed.events(0, (0, 1)))
+    while sums.at < len(sums.events):
+        sums.run(EMBED_RUN[0])
+        arrivals.run(EMBED_RUN[1])
+    tell_peers(front_done)
+    arrivals.run()
+    for chunk in range(4):
+        gather.wait_pairs(chunk)
+        spread(gathered, weights, chunk)
+    for chunk in (4, 5):
+        gather.wait_pairs(chunk)
     gather.finish()
-    for chunk in range(4):
-        spread(gathered, weights, chunk)
-
+
+    names = dict(
+        residual=residual, out_grad=out_grad, gain_one=gain_one, gain_two=gain_two, block_out=block_out,
+        joint=joint, probs=probs, pre_act=pre_act, act=act,
+        grad_pre=grad_pre, mixed=mixed, normed_one=normed_one, normed_two=normed_two, unit_one=unit_one,
+        unit_two=unit_two, inverse_one=inverse_one, inverse_two=inverse_two, result=residual, grad_normed=grad_normed,
+        grad_middle=grad_middle, grad_branch=grad_branch, grad_mixed=grad_mixed, grad_joint=grad_joint,
+        turned_mixed=turned_mixed, small=small, grad_embed=image_grads.at[band],
+    )
     block = Block(weights, gathered.at[2], names)
     block.project()
     block.attend()
@@ -672,84 +873,206 @@
     block.narrow()
 
     def part_ref(part):
-        return down_grads if part == 2 else gathered.at[part]
-
-    def grad_view(chunk, where):
+        return spare if part == 2 else gathered.at[part]
+
+    def grad_view(chunk, blk, side):
+        where = slot(blk[0], blk[1], side, blk[2])
         return part_ref(chunk // 2).at[pl.ds(aligned(where * PART + (chunk % 2) * CHUNK), CHUNK)]
 
-    def part_view(part, where):
-        return part_ref(part).at[pl.ds(aligned(where * PART), PART)]
-
-    reduce = Reduce(grad_view, ORDERS, part_view, pair_buf, buf, *sems[4:])
+    def part_view(part, blk, side):
+        return part_ref(part).at[pl.ds(aligned(slot(blk[0], blk[1], side, blk[2]) * PART), PART)]
+
+    reduce = Reduce(
+        3,
+        grad_view,
+        tuple(order[::-1] for order in ORDERS),
+        lambda chunk: shares.at[pl.ds(chunk * CHUNK, CHUNK)],
+        part_view,
+        lambda part, rail: pair_buf.at[part, pl.ds(aligned(rail * PART), PART)],
+        lambda chunk, where: buf.at[chunk, where],
+        *reduce_sems,
+    )
+    embed.finish()
     grad_normed[...] = jnp.zeros(grad_normed.shape, F32)
 
     @pl.loop(0, 4)
     def _(part):
         block.back_narrow(part)
-        block.down_grad(part, down_grads)
-
-    for rail in range(16):
-        reduce.pair_copy(2, rail).start()
+        block.down_grad(part, spare)
+
+    pl.semaphore_wait(front_done, bands)
+    reduce.pair_start(2)
+    rest = Stream(reduce.events(2, (4, 5)))
+    block.back_wide()
+    rest.run(BACK_RUN[0])
+    block.back_attend()
+    rest.run(BACK_RUN[1])
+    block.back_project()
+
+    def image_view(chunk, blk, side):
+        return image_grads.at[blk[0] * 4 + blk[1] * 2 + side, pl.ds(chunk * half, half)]
+
+    grads = Gather(image_view, ("zx", "zx"), *grads_sems)
+    grads.start(0)
+    grads.start(1)
+    images = Stream(grads.events(0) + grads.events(1))
     turned_two[...] = normed_two[...].T
     for part in (0, 2):
         block.pair_grad(
             turned_two, turned_two, lambda cols, part=part: grad_pre[part, :, cols],
             lambda cols, part=part: grad_pre[part + 1, :, cols], part_ref(1), part // 2 * CHUNK,
         )
-    for rail in range(16):
-        reduce.pair_copy(1, rail).start()
-    block.back_wide()
-    block.back_attend()
+        images.run(GRAD_RUN)
+    reduce.pair_start(1)
     turned_one[...] = normed_one[...].T
     block.pair_grad(
         turned_one, turned_one, lambda cols: grad_joint[0, :, cols], lambda cols: grad_joint[1, :, cols], part_ref(0), 0
     )
+    images.run(GRAD_RUN)
     block.pair_grad(
         turned_one, turned_mixed, lambda cols: grad_joint[2, :, cols], lambda cols: grad_branch[:, cols], part_ref(0), CHUNK
     )
-    for rail in range(16):
-        reduce.pair_copy(0, rail).start()
-    block.back_project()
-    events = []
-    for part, chunks in ((2, (4, 5)), (1, (2, 3)), (0, (0, 1))):
-        events += reduce.events(part, chunks)
-    for _, _, run in sorted(events, key=lambda event: event[:2]):
-        run()
-    for part in range(3):
-        shares[part * PART : (part + 1) * PART, :] = part_view(part, me)[...].astype(F32)
+    reduce.pair_start(0)
+    images.run()
+    for piece in range(16):
+        gen_copy(piece, weights, piece * 128).start()
+
+    kernel_total[...] = jnp.zeros(kernel_total.shape, F32)
+    small[2:3, :] = jnp.zeros((1, width), F32)
+    for chunk in (0, 1):
+        grads.wait_pairs(chunk)
+
+    @pl.loop(0, 4)
+    def _(group):
+        for image in range(4):
+            scaled = image_grads[group * 4 + image].astype(F32) * band_scale[group * 4 + image][:1, :1]
+            small[2:3, :] += jnp.sum(scaled, axis=0, keepdims=True)
+            act[image] = scaled.astype(B16)
+        scaled = act[...].reshape(4 * tokens, width)
+        pixel_rows[pl.ds(group * 4, 4)] = dot_nt(scaled, kernels[...]).astype(B16).reshape(4, tokens, -1)
+        kernel_total[...] += dot_nn(turned_pixels[group], scaled)
+
+    store_pixels = pltpu.make_async_copy(pixel_rows, pixel_out, pix_sem)
+    store_pixels.start()
+    spread_kernels.finish()
+    sending[...] = kernel_total[...].astype(B16)
+    quarter = sending.shape[0] // 4
+
+    def half_copy(piece):
+        rows = pl.ds(piece * quarter, quarter)
+        return pltpu.make_async_remote_copy(
+            src_ref=sending.at[rows], dst_ref=partner_grads.at[rows], send_sem=half_sems[0].at[piece],
+            recv_sem=half_sems[1].at[piece], device_id=partner, device_id_type=MESH,
+        )
+
+    for piece in range(4):
+        half_copy(piece).start()
+    vec_half = pltpu.make_async_remote_copy(
+        src_ref=small, dst_ref=small_partner, send_sem=vec_half_sems[0].at[0], recv_sem=vec_half_sems[1].at[0],
+        device_id=partner, device_id_type=MESH,
+    )
+    vec_half.start()
+    columns = Exchange(
+        lambda target: rows16(mixing, target), lambda source: rows16(landed_grads, source), *cols_sems
+    )
+    for piece in range(4):
+        half_copy(piece).wait_recv()
+        rows = pl.ds(piece * quarter, quarter)
+        mixing[rows, :] = sending[rows, :] + partner_grads[rows, :]
+        for near in range(4):
+            target = piece * 4 + near
+
+            @pl.when(target != band)
+            def _(target=target):
+                columns.copy(target).start()
+
+    landed_grads[own_rows, :] = mixing[own_rows, :]
+    vec_half.wait_recv()
+    small_all[band] = small[...] + small_partner[...]
+    vector_spread = Exchange(lambda target: small_all.at[band], lambda source: small_all.at[source], *vec_sems)
+    vector_spread.start()
+    events = reduce.events(1, (2, 3)) + reduce.events(0, (0, 1))
+    rest.events = rest.events + sorted(events, key=lambda event: event[:2])
+    rest.run(TAIL_RUN[0])
+    columns.wait()
+    for piece in range(4):
+        half_copy(piece).wait_send()
+    sending[...] = swap_rows(landed_grads[...])
+    kernel_grads[...] = landed_grads[...]
+    for piece in range(16):
+        gen_copy(piece, weights, piece * 128).wait()
+    code_part[...] = jnp.zeros(code_part.shape, F32)
+
+    @pl.loop(0, 16)
+    def _(piece):
+        code_part[...] += dot_nt(
+            sending[pl.ds(aligned(piece * 16), 16), :], weights[pl.ds(aligned(piece * 128), 128), :]
+        )
+
+    code_all[band] = code_part[...]
+    code_spread = Exchange(lambda target: code_all.at[band], lambda source: code_all.at[source], *code_sems)
+    code_spread.start()
+    rest.run(TAIL_RUN[1])
+    vector_spread.wait()
+    vectors[...] = small_all[...]
+    code_spread.wait()
+    total = code_all[0]
+    for source in range(1, bands):
+        total = total + code_all[source]
+    code_grads[...] = total
+    rest.run()
     reduce.finish()
-
-
-def middle(attn_qkv, attn_out, mlp_up, mlp_down, residual, out_grad, gain_one, gain_two):
-    width = attn_out.shape[1]
-    devices = lax.axis_size("band") * lax.axis_size("dp")
-    tokens = residual.shape[0]
+    grads.finish()
+    columns.finish()
+    vec_half.wait_send()
+    vector_spread.finish()
+    code_spread.finish()
+    store_pixels.wait()
+
+
+FIRST_CHUNKS = (0, 1, 2, 3, 4, 5)
+EARLY = 10
+EMBED_RUN = (2, 2)
+BACK_RUN = (20, 20)
+GRAD_RUN = 4
+TAIL_RUN = (20, 20)
+
+
+def layer(weights, pixels, kernel_gen, code_low, bias_gen, band_scale, out_grad, gain_one, gain_two):
+    width = weights[1].shape[1]
+    bands = lax.axis_size("band")
+    devices = bands * lax.axis_size("dp")
+    images, tokens, pix = pixels.shape
 
     def stack(weight):
         parts = weight.shape[1] // width
         return weight.reshape(weight.shape[0], parts, width).transpose(1, 0, 2).reshape(-1, width)
 
-    shard = jnp.concatenate([stack(w) for w in (attn_qkv, attn_out, mlp_up, mlp_down)], axis=0)
+    shard = jnp.concatenate([stack(w) for w in weights], axis=0)
     chunks = len(ORDERS)
     vmem = pl.BlockSpec(memory_space=pltpu.VMEM)
+    hbm = pl.BlockSpec(memory_space=pl.ANY)
+    shape = jax.ShapeDtypeStruct
     rows = lambda kind, *lead: pltpu.VMEM((*lead, tokens, width), kind)
     dma = pltpu.SemaphoreType.DMA
-    outs = pl.pallas_call(
-        middle_kernel,
+    return pl.pallas_call(
+        layer_kernel,
         out_shape=[
-            jax.ShapeDtypeStruct((tokens, width), B16),
-            jax.ShapeDtypeStruct((tokens, width), B16),
-            jax.ShapeDtypeStruct((3 * PART, width), F32),
-            jax.ShapeDtypeStruct((2, width), F32),
+            shape((tokens, width), B16),
+            shape(pixels.shape, B16),
+            shape((3 * PART, width), F32),
+            shape((pix, width), B16),
+            shape((bands, code_low.shape[1]), F32),
+            shape((bands, 8, width), F32),
         ],
-        in_specs=[pl.BlockSpec(memory_space=pl.ANY)] + [vmem] * 4,
-        out_specs=[vmem] * 4,
+        in_specs=[hbm, hbm, hbm] + [vmem] * 6,
+        out_specs=[vmem, hbm, vmem, vmem, vmem, vmem],
         scratch_shapes=[
             pltpu.VMEM((3, devices * PART, width), B16),
-            pltpu.VMEM((8, width, width), B16),
+            pltpu.VMEM((8 * width, width), B16),
             pltpu.VMEM((devices * PART, width), B16),
-            pltpu.VMEM((3, 16, PART, width), B16),
-            pltpu.VMEM((chunks, 21, CHUNK, width), B16),
+            pltpu.VMEM((3, devices // 2 * PART, width), B16),
+            pltpu.VMEM((chunks, 19, CHUNK, width), B16),
             rows(B16, 3),
             pltpu.VMEM((HEADS // 2, 2 * tokens, tokens), F32),
             rows(F32, 4),
@@ -764,36 +1087,61 @@
             pltpu.VMEM((tokens, 128), F32),
             rows(F32),
             rows(F32),
-            rows(F32),
             rows(B16),
             rows(B16),
             rows(B16, 3),
             pltpu.VMEM((width, tokens), B16),
             pltpu.VMEM((width, tokens), B16),
             pltpu.VMEM((width, tokens), B16),
+            rows(F32),
+            pltpu.VMEM(pixels.shape, B16),
+            pltpu.VMEM((4, pix, 4 * tokens), B16),
+            pltpu.VMEM((pix, width), B16),
+            pltpu.VMEM((pix, width), B16),
+            pltpu.VMEM((pix, width), B16),
+            pltpu.VMEM((images, tokens, width), B16),
+            pltpu.VMEM((pix, width), F32),
+            pltpu.VMEM((pix, width), B16),
+            pltpu.VMEM((pix, width), B16),
+            pltpu.VMEM((8, width), F32),
+            pltpu.VMEM((8, width), F32),
+            pltpu.VMEM((bands, 8, width), F32),
+            pltpu.VMEM((bands, code_low.shape[1]), F32),
+            pltpu.VMEM((bands, bands, code_low.shape[1]), F32),
             dma((3,)),
-            dma((chunks, 40)),
-            dma((chunks, 16)),
-            dma((chunks, 16)),
-            dma((chunks, 16)),
-            dma((3, 16)),
-            dma((3, 16)),
-            dma((chunks, 48)),
-            dma((chunks, 24)),
+            dma,
+            dma((16,)),
+            pltpu.SemaphoreType.REGULAR,
+            dma((chunks, 40)), dma((chunks, 16)), dma((chunks, 16)), dma((chunks, 16)),
+            dma((3, 16)), dma((3, 16)), dma((chunks, 48)), dma((chunks, 24)),
+            dma((1, 8)), dma((1, 8)), dma((2, 24)), dma((2, 16)),
+            dma((2, 16)), dma((2, 16)), dma((2, 16)), dma((2, 16)),
+            dma((bands,)), dma((bands,)),
+            dma((bands,)), dma((bands,)),
+            dma((bands,)), dma((bands,)),
+            dma((bands,)), dma((bands,)),
+            dma((4,)), dma((4,)),
+            dma((1,)), dma((1,)),
         ],
         compiler_params=pltpu.CompilerParams(
-            collective_id=0, has_side_effects=True, vmem_limit_bytes=62 * 2**20
+            collective_id=0, has_side_effects=True, vmem_limit_bytes=VMEM_BYTES
         ),
-        name="gather_block_reduce",
-    )(shard, residual, out_grad, gain_one, gain_two)
-    block_out, grad_embed, shares, gain_grads = outs
+        name="layer",
+    )(shard, pixels, kernel_gen, code_low, bias_gen, band_scale, out_grad, gain_one, gain_two)
+
+
+VMEM_BYTES = 63 * 2**20
+
+
+def split_shares(shares, weights):
+    width = shares.shape[1]
     grads, at = [], 0
-    for weight in (attn_qkv, attn_out, mlp_up, mlp_down):
+    for weight in weights:
         own_rows, parts = weight.shape[0], weight.shape[1] // width
         piece = shares[at : at + own_rows * parts].reshape(parts, own_rows, width)
         grads.append(piece.transpose(1, 0, 2).reshape(own_rows, parts * width))
         at += own_rows * parts
-    return block_out, grad_embed, grads, gain_grads
+    return grads
 
 
 def body(
@@ -1011,88 +1359,41 @@
     mlp_down,
     out_grad,
 ):
-    f32 = jnp.float32
-    b16 = jnp.bfloat16
-    band_local = pixels.shape[3]
-    pixel_local = pixels[0]
-    model_width = bias_gen.shape[1]
     hyper_params = tuple(
-        (
-            weight.astype(f32)
-            for weight in (hyper_qkv, hyper_out, hyper_gain1, hyper_up, hyper_down, hyper_gain2)
-        )
+        weight.astype(F32)
+        for weight in (hyper_qkv, hyper_out, hyper_gain1, hyper_up, hyper_down, hyper_gain2)
     )
     wave_tokens = wave_embed(wavelengths, HW)
     band_code, hyper_pull = jax.vjp(lambda *params: hyper_net(wave_tokens, *params), *hyper_params)
-    code_low = band_code.astype(b16)
-    column_part = jnp.dot(code_low, kernel_gen, preferred_element_type=f32).astype(b16)
-    kernel_rows = lax.all_to_all(column_part, "band", split_axis=0, concat_axis=1, tiled=True)
-    kernels = kernel_rows.reshape(band_local, -1, model_width)
-    first_band = lax.axis_index("band") * band_local
-    own_code = lax.dynamic_slice_in_dim(code_low, first_band, band_local, 0)
+    code_low = band_code.astype(B16)
+    band = lax.axis_index("band")
     count_row = band_counts[0]
-    biases = jnp.dot(own_code, bias_gen, preferred_element_type=f32)
-    slot_ids = first_band + jnp.arange(band_local, dtype=jnp.int32)
-    active = (slot_ids[None, :] < count_row[:, None]) & (band_mask[0] == 1)
-    band_weight = jnp.where(active, lax.rsqrt(count_row.astype(f32))[:, None], f32(0.0))
-    pixel_rows = pixel_local
-    weight_rows = band_weight
-    conv_out = jnp.einsum("inbp,bpd->inbd", pixel_rows, kernels, preferred_element_type=f32)
-    residual = lax.psum_scatter(
-        jnp.sum((conv_out + biases[None, None]) * weight_rows[:, None, :, None], axis=2),
-        "band",
-        scatter_dimension=0,
-        tiled=True,
-    )
-    block_out, grad_embed_low, shares, gain_grads = middle(
-        attn_qkv,
-        attn_out,
-        mlp_up,
-        mlp_down,
-        residual[0],
+    active = (band < count_row) & (band_mask[0, :, 0] == 1)
+    band_weight = jnp.where(active, lax.rsqrt(count_row.astype(F32)), F32(0.0))
+    weights = (attn_qkv, attn_out, mlp_up, mlp_down)
+    block_out, pixel_grad, shares, kernel_grads, grad_code, vectors = layer(
+        weights,
+        pixels[0, :, :, 0],
+        kernel_gen,
+        code_low,
+        bias_gen,
+        jnp.broadcast_to(band_weight[:, None, None], (band_weight.shape[0], 8, 128)),
         out_grad[0, 0],
-        norm_gain1.astype(f32)[None],
-        norm_gain2.astype(f32)[None],
-    )
-    block_out = block_out[None, None]
-    grad_embed_low = grad_embed_low[None, None]
-    grad_gain_one, grad_gain_two = gain_grads[0], gain_grads[1]
-    grad_rows = lax.all_gather(grad_embed_low, "band", axis=1, tiled=True)[0].astype(f32)
-    weight_rows = band_weight
-    pixel_rows = pixel_local
-    scaled = grad_rows[:, :, None, :] * weight_rows[:, None, :, None]
-    bias_total = jnp.sum(scaled, axis=(0, 1))
-    scaled_low = scaled.astype(b16)
-    kernel_total = jnp.einsum("inbp,inbd->bpd", pixel_rows, scaled_low, preferred_element_type=f32)
-    pixel_part = jnp.einsum(
-        "inbd,bpd->inbp", scaled_low, kernels, preferred_element_type=f32
-    ).astype(b16)
-    pixel_total = pixel_part
-    kernel_grad, bias_grad, pixel_total = (kernel_total, bias_total, pixel_total)
-    pixel_out = pixel_total[None]
-    kernel_grad_low = lax.psum(kernel_grad.astype(b16), "dp").reshape(band_local, -1)
-    grad_columns = lax.all_to_all(kernel_grad_low, "band", split_axis=1, concat_axis=0, tiled=True)
-    grad_kernel_part = jnp.einsum("nh,nc->hc", code_low, grad_columns, preferred_element_type=f32)
-    grad_code_part = jnp.einsum("nc,hc->nh", grad_columns, kernel_gen, preferred_element_type=f32)
-    bias_back = jnp.einsum("bd,hd->bh", bias_grad, bias_gen.astype(f32), precision=PRECISE)
-    grad_code_part = 0.5 * grad_code_part + lax.dynamic_update_slice_in_dim(
-        jnp.zeros_like(grad_code_part), bias_back, first_band, 0
-    )
-    grad_bias_part = jnp.einsum("bh,bd->hd", own_code.astype(f32), bias_grad, precision=PRECISE)
-    grad_code, grad_bias_gen, grad_norm_gain1, grad_norm_gain2 = lax.psum(
-        (grad_code_part, grad_bias_part, grad_gain_one, grad_gain_two), ("band", "dp")
-    )
-    grad_kernel_gen = grad_kernel_part
+        norm_gain1.astype(F32)[None],
+        norm_gain2.astype(F32)[None],
+    )
+    grad_columns = kernel_grads.reshape(band_code.shape[0], -1)
+    grad_kernel_gen = jnp.einsum("nh,nc->hc", code_low, grad_columns, preferred_element_type=F32)
+    bias_grads = vectors[:, 2]
+    grad_code = grad_code + jnp.dot(bias_grads, bias_gen.astype(F32).T, precision=PRECISE)
+    grad_bias_gen = jnp.dot(code_low.astype(F32).T, bias_grads, precision=PRECISE)
+    grad_norm_gain1, grad_norm_gain2 = (jnp.sum(vectors[:, row], axis=0) for row in (0, 1))
     hyper_grads = hyper_pull(grad_code)
+    shares = split_shares(shares, weights)
     return (
-        block_out,
-        pixel_out,
-        hyper_grads[0],
-        hyper_grads[1],
-        hyper_grads[2],
-        hyper_grads[3],
-        hyper_grads[4],
-        hyper_grads[5],
+        block_out[None, None],
+        pixel_grad[None, :, :, None],
+        *hyper_grads,
         grad_kernel_gen,
         grad_bias_gen,
         grad_norm_gain1,
@@ -1126,9 +1427,9 @@
         P(("band", "dp"), None),
         P("dp", "band", None, None),
     )
-    whole_block = (mesh.shape["band"], mesh.shape["dp"]) == (16, 2)
+    one_slot = (mesh.shape["band"], mesh.shape["dp"]) == (16, 2)
     return jax.shard_map(
-        fast_body if whole_block else body,
+        fast_body if one_slot else body,
         mesh=mesh,
         in_specs=placed,
         out_specs=(

time: 550 us -> 301 us (0.55)
  waiting for transfers between devices: 218 us -> 0 us
  Pallas kernels: 174 us -> 246 us
  blocking collectives: 38.9 us -> 0 us
  local copies, waits for them, and re-layouts: 28.8 us -> 14.7 us
  between operations: 15.1 us -> 1.05 us
  starting transfers between devices: 13.4 us -> 0 us
  matrix products: 38.5 us -> 26.4 us
  other arithmetic: 17 us -> 11.2 us
    reduce_scatter x1 -> x0, waiting for transfers between devices: 82.1 us -> none  [fast_body(): lax.psum_scatter(jnp.sum((conv_out + biases[None, None]) * weight_rows[:,...]
    psum x2 -> x0, waiting for transfers between devices: 75 us -> none  [the longest x1 57 us: fast_body(): lax.psum((grad_code_part, grad_bias_part, grad_gain_one, grad_gain_two),...]
    pallas_call x1, Pallas kernels: 174 us -> 246 us  [layer(): pl.pallas_call(layer_kernel, out_shape=[shape((tokens, width), B16), shap...]
    all_gather x1 -> x0, waiting for transfers between devices: 46.8 us -> none  [fast_body(): lax.all_gather(grad_embed_low, 'band', axis=1, tiled=True)[0].astype(f32)]
    psum x1 -> x0, blocking collectives: 38.9 us -> none  [fast_body(): lax.psum((grad_code_part, grad_bias_part, grad_gain_one, grad_gain_two),...]
    dot_general x8 -> x3, matrix products: 21.7 us -> 6.36 us  [the longest x1 3.7 us: fast_body(): jnp.einsum('nh,nc->hc', code_low, grad_columns, preferred_element_type=F32)]
    all_to_all x2 -> x0, waiting for transfers between devices: 14.2 us -> none  [the longest x1 11.9 us: fast_body(): lax.all_to_all(column_part, 'band', split_axis=0, concat_axis=1, tiled=True)]
    all_to_all x2 -> x0, starting transfers between devices: 13 us -> none  [the longest x1 7.36 us: fast_body(): lax.all_to_all(column_part, 'band', split_axis=0, concat_axis=1, tiled=True)]
  transfers between devices with their start and end apart: 6 -> 0, of which waited for: 6 -> 0; matrix products, arithmetic and copies ran while one was open for 8% -> 0% of each run, Pallas kernels for 0% -> 0%
where the time goes in v3:
time: 301 us; the launch traced here: 299 us
  Pallas kernels  246 us (82%)
  matrix products  26.4 us (9%)
  local copies, waits for them, and re-layouts  14.7 us (5%)
  other arithmetic  11.2 us (4%)
    pallas_call x1, Pallas kernels, layer(): pl.pallas_call(layer_kernel, out_shape=[shape((tokens, width), B16), shap...  246 us

profile of v3, /device:TPU:0, one launch (start us, length us, event | category | flops | bytes accessed | tf_op | source)
XLA Modules:
  0.0 299.4 jit_solution(8974559231332904873)
XLA Ops:
  3.4 1.3 reshape.198.refs_7_
  4.7 1.3 reshape.199.refs_8_
  6.1 1.1 fusion.67
  8.7 1.0 fusion.73
  11.0 1.5 fusion.74
  14.5 0.9 reshape.181
  16.4 1.7 pad_maximum_fusion.refs_0_
  18.1 246.0 %layer.1 = (bf16[128,768]{1,0:T(8,128)(2,1)}, bf16[16,128,256]{2,1,0:T(8,128)(2,1)}, f32[288,768]{1,0:T(8,128)}, bf16[256,768]{1,0:T(8,128)(2,1)}, f32[16,128]{1,0:T(8,128)}, /*index=5*/f32[16,8,768]{2,1,0:T(8,128)}) custom-call(bf16[288,768]{1,0:T(8,128)(2,1)} %pad_maximum_fusion.refs_0_, bf16[16,128,256]{2,1,0:T(8,128)(2,1)} %bitcast.72, ...), custom_call_target="tpu_custom_call" | custom-call | tf_op jit(solution)/shard_map/layer/pallas_call | solution.py:1058
  264.2 2.0 slice_reduce_fusion
  266.2 1.5 multiply_reduce_fusion.1
  269.3 1.5 slice.36
  270.8 1.6 fusion.2
  272.4 1.8 multiply_reduce_fusion.2
  276.7 1.0 multiply_reduce_fusion
  277.7 1.0 convolution_bitcast_fusion
  280.7 1.6 fusion.30
  282.4 1.1 fusion.22
  283.5 0.9 slice.35
  284.4 1.8 fusion.70
  287.9 1.1 fusion.6
  289.2 2.1 fusion.41
  291.3 2.8 fusion.5
  294.1 3.7 %fusion.75 = f32[128,12288]{1,0:T(8,128)} fusion(bf16[16,128]{1,0:T(8,128)(2,1)S(1)} %copy-done.7, bf16[16,12288]{1,0:T(8,128)(2,1)S(1)} %reshape.193), kind=kOutput, calls=%fused_computation.116 | convolution fusion | flops 50331648 | bytes 6688768 | tf_op jit(solution)/shard_map/nh,nc->hc/dot_general | solution.py:1386
  298.4 1.0 copy.116
  (91 shorter events, 17.0 us)
Async XLA Ops:
  0.6 10.0 %copy-start = (bf16[128,2048]{1,0:T(8,128)(2,1)S(1)}, bf16[128,2048]{1,0:T(8,128)(2,1)}, u32[]{:S(2)}) copy-start(bf16[128,2048]{1,0:T(8,128)(2,1)} %param.26) | copy-start | bytes 1572868
  0.7 265.5 %copy-start.3 = (bf16[128,768]{1,0:T(8,128)(2,1)S(1)}, bf16[128,768]{1,0:T(8,128)(2,1)}, u32[]{:S(2)}) copy-start(bf16[128,768]{1,0:T(8,128)(2,1)} %refs_4_.1) | copy-start | bytes 589828
  2.1 10.7 %copy-start.11 = (f32[128]{0:T(128)}, f32[128]{0:T(128)S(1)}, u32[]{:S(2)}) copy-start(f32[128]{0:T(128)S(1)} %convert_element_type.29) | copy-start | bytes 1540
  2.8 10.0 %copy-start.17 = (f32[128]{0:T(128)}, f32[128]{0:T(128)S(1)}, u32[]{:S(2)}) copy-start(f32[128]{0:T(128)S(1)} %convert_element_type.30) | copy-start | bytes 1540
  7.5 0.8 copy-start.5
  7.7 2.2 copy-start.10
  7.7 2.2 copy-start.15
  8.7 1.3 copy-start.6
  9.7 3.1 %copy-start.8 = (f32[16]{0:T(128)}, f32[16]{0:T(128)S(1)}, u32[]{:S(2)}) copy-start(f32[16]{0:T(128)S(1)} %broadcast_multiply_fusion.1) | copy-start | bytes 196
  9.9 2.7 copy-start.19
  9.9 2.9 copy-start.13
  12.6 0.5 copy-start.16
  12.8 0.5 copy-start.20
  13.3 0.5 copy-start.18
  264.1 23.7 %copy-start.7 = (bf16[16,128]{1,0:T(8,128)(2,1)S(1)}, bf16[16,128]{1,0:T(8,128)(2,1)}, u32[]{:S(2)}) copy-start(bf16[16,128]{1,0:T(8,128)(2,1)} %multiply_convert_fusion.refs_3_) | copy-start | bytes 12292
  264.1 24.8 %copy-start.2 = (bf16[256,768]{1,0:T(8,128)(2,1)S(1)}, bf16[256,768]{1,0:T(8,128)(2,1)}, u32[]{:S(2)}) copy-start(bf16[256,768]{1,0:T(8,128)(2,1)} %get-tuple-element.26) | copy-start | bytes 1179652
  264.1 25.0 %copy-start.9 = (f32[16]{0:T(128)S(1)}, f32[16]{0:T(128)}, u32[]{:S(2)}) copy-start(f32[16]{0:T(128)} %copy-done.8) | copy-start | bytes 196
  264.2 25.0 %copy-start.12 = (f32[128]{0:T(128)S(1)}, f32[128]{0:T(128)}, u32[]{:S(2)}) copy-start(f32[128]{0:T(128)} %copy-done.11) | copy-start | bytes 1540
  264.2 25.0 %copy-start.14 = (f32[16]{0:T(128)S(1)}, f32[16]{0:T(128)}, u32[]{:S(2)}) copy-start(f32[16]{0:T(128)} %copy-done.13) | copy-start | bytes 196
  284.4 13.3 %copy-start.4 = (bf16[128,768]{1,0:T(8,128)(2,1)S(1)}, bf16[128,768]{1,0:T(8,128)(2,1)}, u32[]{:S(2)}) copy-start(bf16[128,768]{1,0:T(8,128)(2,1)} %get-tuple-element.22) | copy-start | bytes 589828
  286.3 12.2 %copy-start.1 = (bf16[16,128,256]{2,1,0:T(8,128)(2,1)S(1)}, bf16[16,128,256]{2,1,0:T(8,128)(2,1)}, u32[]{:S(2)}) copy-start(bf16[16,128,256]{2,1,0:T(8,128)(2,1)} %get-tuple-element.23) | copy-start | bytes 3145732

commit v4 on v3

--- a/solution.py
+++ b/solution.py
@@ -90,13 +90,173 @@
 B16 = jnp.bfloat16
 F32 = jnp.float32
 CHUNK = 48
+DIMS = "xyz"
 PART = 96
-ORDERS = ("zxy", "xzy", "yzx", "zyx", "xzy", "yzx")
-
-
-def place():
+FRONT_PLAN = (
+    (
+        (),
+        (),
+        (),
+        (1, 2, 3),
+        (30, 11),
+        (54, 27),
+        (10,),
+        (13, 57, 29, 81, 82, 5),
+        (56, 83, 86),
+        (87, 92, 93, 33, 100, 60, 84, 90, 85, 22, 39, 91, 17, 32, 59, 9, 35, 14, 88, 66, 89, 62, 45, 94, 103, 95, 104, 21, 47, 24, 41, 101, 38, 109, 68, 65, 102, 110, 72, 51, 18, 49, 71, 26, 44, 74),
+        (112, 115, 53, 114, 116, 78),
+        (76, 80),
+        (),
+        (),
+        (),
+        (),
+    ),
+    (
+        (),
+        (),
+        (0, 1),
+        (2, 3),
+        (7,),
+        (30,),
+        (6, 28, 11),
+        (54, 27, 81, 10, 55, 82, 83, 29, 57, 86, 13, 5),
+        (31, 56, 87, 92),
+        (58, 93, 100, 84, 85, 96, 19, 36, 35, 98, 32, 62, 59, 88, 63, 33, 22, 89, 60, 39, 17, 14, 65, 38, 42, 94, 106, 66, 95, 108, 105, 69, 107, 47, 45, 101, 111, 24, 102, 113, 49, 112, 115, 114, 116),
+        (72, 74),
+        (76,),
+        (),
+        (),
+        (),
+        (),
+    ),
+    (
+        (),
+        (),
+        (0, 1),
+        (2, 3),
+        (7,),
+        (),
+        (30, 6, 11, 29),
+        (54, 81, 27, 82, 56, 10, 83, 86, 57, 4),
+        (13, 28, 55, 87, 92, 32, 59),
+        (93, 100, 19, 84, 85, 39, 34, 31, 61, 58, 33, 22, 66, 88, 15, 89, 60, 97, 99, 12, 37, 36, 64, 45, 94, 63, 112, 95, 105, 114, 107, 72, 42, 46, 111, 115, 101, 106, 113, 116, 102, 23, 108, 48, 69),
+        (73,),
+        (75,),
+        (),
+        (),
+        (),
+        (),
+    ),
+    (
+        (),
+        (),
+        (),
+        (0, 2, 3),
+        (30, 7, 54),
+        (27, 6),
+        (13, 57, 4),
+        (81, 28, 82, 83, 86, 55),
+        (87,),
+        (92, 60, 33, 93, 100, 19, 15, 84, 12, 85, 36, 31, 58, 8, 88, 34, 90, 89, 91, 63, 61, 42, 23, 94, 109, 20, 95, 110, 46, 40, 101, 103, 102, 64, 37, 104, 67, 69, 50, 48, 16, 73, 43, 25, 70, 52),
+        (111, 115, 77, 113, 75, 116),
+        (),
+        (79,),
+        (),
+        (),
+        (),
+    ),
+)
+TAIL_PLAN = (
+    (
+        (),
+        (0, 1, 2, 4, 5, 8, 9, 11, 12, 16, 17, 21, 22, 25, 26, 28, 3),
+        (6,),
+        (7, 15),
+        (10,),
+        (122, 123),
+        (135, 13, 136, 38, 39, 40, 125, 42, 18, 43, 45, 46, 138, 49, 50, 14, 129, 55, 56, 60, 128, 61, 63, 142, 23, 64, 67, 27, 141),
+        (24, 131, 29, 31),
+        (41, 48, 144, 83, 84, 85, 87, 133, 88, 91, 92, 94, 95, 99, 100),
+        (104, 44, 105, 54, 108, 109, 146, 36, 111, 37, 30, 34, 47, 51),
+        (86, 57, 66, 62, 71, 89, 93, 65, 74, 96, 76, 78, 68, 77, 101, 106, 80),
+        (110,),
+        (),
+        (90, 98, 112),
+        (),
+        (82, 97, 107, 114, 113, 117),
+        (),
+        (119, 120),
+    ),
+    (
+        (),
+        (0, 1, 2, 4, 5, 8, 9, 11, 12, 16, 17, 21, 22, 25, 26, 28, 3),
+        (6,),
+        (7,),
+        (10,),
+        (122, 123, 121),
+        (135, 136, 13, 134, 125, 38, 39, 40, 18, 42, 43, 45, 19, 138, 46, 49, 14, 50, 55, 129, 56, 60, 61, 126, 23, 63, 64, 142, 67, 27),
+        (29, 139),
+        (33, 41, 131, 83, 84, 85, 87, 88, 91, 24, 92, 144, 94, 32, 95, 99, 100, 44, 104, 105, 108, 109, 111, 52, 47, 30, 51),
+        (58, 86),
+        (35, 57, 89, 62, 36, 37, 69, 93, 70, 65, 96, 72, 68, 73, 101, 75, 106, 79),
+        (),
+        (90, 110),
+        (),
+        (),
+        (76, 112, 78, 97, 102, 107, 80, 113, 82),
+        (115, 118),
+        (116, 119, 120),
+    ),
+    (
+        (),
+        (0, 1, 2, 4, 5, 8, 9, 11, 12, 16, 17, 21, 22, 25, 26, 28, 3),
+        (6,),
+        (7,),
+        (10,),
+        (121, 122, 123),
+        (134, 135, 136, 13, 38, 39, 40, 124, 42, 18, 43, 45, 46, 49, 14, 137, 50, 126, 55, 56, 60, 129, 23, 61, 63, 64, 67, 27, 139, 32, 20, 29),
+        (142,),
+        (41, 130),
+        (83, 84, 24, 143, 85, 87, 36, 88, 91, 92, 44, 94, 95, 99, 100, 104, 105, 108, 109, 35, 111, 37, 30, 47, 51, 86, 33),
+        (53, 69, 57, 89, 62, 72, 93, 59, 65, 96, 75, 76, 78, 68, 80, 101, 79, 106, 70),
+        (),
+        (90,),
+        (73, 110),
+        (),
+        (112, 82, 97, 107, 113),
+        (103, 119, 115, 116),
+        (118, 120),
+    ),
+    (
+        (),
+        (0, 1, 2, 4, 5, 8, 9, 11, 12, 16, 17, 21, 22, 25, 26, 28, 3),
+        (6,),
+        (7,),
+        (10,),
+        (),
+        (121, 123, 134, 13, 136, 38, 39, 40, 124, 42, 18, 43, 45, 46, 49, 137, 50, 55, 126, 56, 14, 15, 60, 61, 63, 127, 139, 64, 23, 67, 140, 27),
+        (130, 29),
+        (24, 34, 143, 41, 35, 83, 84, 37, 85, 87, 132, 88, 91, 92, 94, 95, 99),
+        (100, 104, 44, 105, 145, 108, 109, 111, 30, 47, 31, 48, 51, 54),
+        (86, 57, 74, 62, 89, 77, 75, 78, 93, 65, 66, 96, 79, 68, 71, 101, 106),
+        (),
+        (),
+        (110,),
+        (),
+        (112, 90, 82, 97, 98, 107, 117, 113, 114),
+        (118, 120),
+        (),
+    ),
+)
+FIRST_PARTS = (0,)
+SUM_ORDERS = ('xyz', 'yzx', 'yxz')
+ORDERS = ("zxy", "xzy", "yzx")
+
+
+def place(known_z=None):
     band = lax.axis_index("band")
-    return (band // 4, (band // 2) % 2, band % 2, lax.axis_index("dp"))
+    z = band // 4 if known_z is None else known_z
+    return (z, (band // 2) % 2, band % 2, lax.axis_index("dp"))
 
 
 def device(z, x, core, y):
@@ -108,8 +268,9 @@
 
 
 def when(cond, run):
-    if cond is True:
-        run()
+    if isinstance(cond, bool):
+        if cond:
+            run()
     else:
         pl.when(cond)(run)
 
@@ -120,11 +281,6 @@
 
 def aligned(rows):
     return pl.multiple_of(rows, 16)
-
-
-def meet_peers(barrier):
-    tell_peers(barrier)
-    pl.semaphore_wait(barrier, lax.axis_size("band"))
 
 
 def tell_peers(barrier):
@@ -137,30 +293,71 @@
     pl.semaphore_signal(barrier, inc=1, device_id=(band, 1 - y), device_id_type=MESH)
 
 
-class Stream:
-    def __init__(self, events):
-        self.events = sorted(events, key=lambda event: event[:2])
+def tell_near(semaphore):
+    z, x, core, y = place()
+    near = [
+        (device(z, x, 1 - core, y), True),
+        (device(z, 1 - x, core, y), True),
+        (device(z, x, core, 1 - y), True),
+        (device(z + 1, x, core, y), z < 3),
+        (device(z - 1, x, core, y), z > 0),
+    ]
+    for target, cond in near:
+        when(
+            cond,
+            functools.partial(
+                pl.semaphore_signal, semaphore, inc=1, device_id=target, device_id_type=MESH
+            ),
+        )
+
+
+def hear_near(semaphore):
+    z = place()[0]
+    pl.semaphore_wait(semaphore, 5 - z // 3 - (3 - z) // 3)
+
+
+def bulk_copy(ref, send_sem, recv_sem):
+    band, y = lax.axis_index("band"), lax.axis_index("dp")
+    return pltpu.make_async_remote_copy(
+        src_ref=ref,
+        dst_ref=ref,
+        send_sem=send_sem,
+        recv_sem=recv_sem,
+        device_id=(band, 1 - y),
+        device_id_type=MESH,
+    )
+
+
+def in_order(events):
+    return [work for _, _, work in sorted(events, key=lambda event: event[:2])]
+
+
+class Plan:
+    def __init__(self, table, catalogues):
+        self.table, self.catalogues = table, catalogues
         self.at = 0
 
-    def run(self, count=None):
-        last = len(self.events) if count is None else min(len(self.events), self.at + count)
-        for _, _, work in self.events[self.at : last]:
-            work()
-        self.at = last
-
-    def until(self, time):
-        while self.at < len(self.events) and self.events[self.at][0] <= time:
-            self.run(1)
+    def run(self):
+        z = place()[0]
+        for known_z, works in enumerate(self.catalogues):
+            chosen = self.table[known_z][self.at]
+            if not chosen:
+                continue
+
+            @pl.when(z == known_z)
+            def _(works=works, chosen=chosen):
+                for index in chosen:
+                    works[index]()
+
+        self.at += 1
 
 
 class Gather:
-    def __init__(self, view, orders, send_sem, recv_sem, pair_send, pair_recv):
-        self.view, self.orders = view, orders
+    def __init__(self, known_z, view, orders, bulk, send_sem, recv_sem, pair_send, pair_recv):
+        self.view, self.orders, self.bulk = view, orders, bulk
         self.send_sem, self.recv_sem = send_sem, recv_sem
         self.pair_send, self.pair_recv = pair_send, pair_recv
-        self.z, self.x, self.core, self.y = place()
-        self.sends = []
-        self.count = [0] * len(orders)
+        self.z, self.x, self.core, self.y = place(known_z)
 
     def rail(self, block):
         return block[0] * 4 + block[1] * 2 + block[2]
@@ -182,25 +379,25 @@
                 targets.append((device(z - 1, x, core, y), both(cond, z > 0)))
         src = self.view(chunk, block, core)
         for target, needed in targets:
+            if needed is False:
+                continue
             copy = pltpu.make_async_remote_copy(
                 src_ref=src,
                 dst_ref=src,
-                send_sem=self.send_sem.at[chunk, self.count[chunk]],
+                send_sem=self.send_sem.at[chunk, DIMS.index(dim)],
                 recv_sem=self.recv_sem.at[chunk, self.rail(block)],
                 device_id=target,
                 device_id_type=MESH,
             )
-            self.count[chunk] += 1
             when(needed, copy.start)
-            self.sends.append((needed, copy))
 
     def pair(self, chunk, block, core):
         src = self.view(chunk, block, core)
         return pltpu.make_async_remote_copy(
             src_ref=src,
             dst_ref=src,
-            send_sem=self.pair_send.at[chunk, self.rail(block)],
-            recv_sem=self.pair_recv.at[chunk, self.rail(block)],
+            send_sem=self.pair_send.at[chunk, block[0] // 2],
+            recv_sem=self.pair_recv.at[chunk, block[0] // 2],
             device_id=self.sibling(),
             device_id_type=MESH,
         )
@@ -239,6 +436,8 @@
             cond = self.z >= dist
         elif way == -1:
             cond = self.z + dist <= 3
+        if cond is False:
+            return
         block = (
             self.z - dist * way,
             1 - self.x if flip_x else self.x,
@@ -261,33 +460,55 @@
             self.send(chunk, block, later, cond)
         when(cond, self.pair(chunk, block, self.core).start)
 
-    def blocks(self, chunk):
-        planes = (0, 1) if "y" in self.orders[chunk] else (self.y,)
-        return [(zz, xx, yy) for zz in range(4) for xx in (0, 1) for yy in planes]
+    def rails(self, chunk):
+        return 16 if "y" in self.orders[chunk] else 8
+
+    def sent(self, chunk, z, over):
+        order = self.orders[chunk]
+        fresh = (z < 3) + (z > 0) if over == "z" else 1
+        total = fresh if over in order else 0
+        for _, _, work in self.events(chunk):
+            _, dim, (dist, way, *_) = work.args
+            if (way == 1 and z < dist) or (way == -1 and z + dist > 3):
+                continue
+            total += fresh if over in order[order.index(dim) + 1 :] else 0
+            if dim == "z" and over == "z":
+                total += z < 3 if way == 1 else z > 0
+        return total
+
+    def wait_side(self, chunk, side):
+        every = self.bulk(chunk, self.rails(chunk) // 2)
+        bulk_copy(every, self.pair_send.at[chunk, side], self.pair_recv.at[chunk, side]).wait_recv()
 
     def wait_pairs(self, chunk):
-        for block in self.blocks(chunk):
-            self.pair(chunk, block, 1 - self.core).wait_recv()
+        for side in (0, 1):
+            self.wait_side(chunk, side)
 
     def finish(self):
-        for needed, copy in self.sends:
-            when(needed, copy.wait_send)
+        ends = (self.z == 0) | (self.z == 3)
+        inner = (self.z == 1) | (self.z == 2)
         for chunk in range(len(self.orders)):
-            for block in self.blocks(chunk):
-                self.pair(chunk, block, self.core).wait_send()
+            for dim in self.orders[chunk]:
+                send_sem = self.send_sem.at[chunk, DIMS.index(dim)]
+                for cond, z in ((ends, 0), (inner, 1)):
+                    copy = bulk_copy(self.bulk(chunk, self.sent(chunk, z, dim)), send_sem, self.recv_sem.at[chunk, 0])
+                    when(cond, copy.wait_send)
+            every = self.bulk(chunk, self.rails(chunk) // 2)
+            for side in (0, 1):
+                bulk_copy(every, self.pair_send.at[chunk, side], self.pair_recv.at[chunk, side]).wait_send()
 
 
 class Reduce:
-    def __init__(self, parts, view, orders, final, pair_view, pair_buf, buf, pair_send, pair_recv, send, recv):
-        self.parts = parts
+    def __init__(
+        self, known_z, parts, view, orders, final, pair_view, pair_buf, buf, bulk, pair_bulk, pair_send, pair_recv, send, recv
+    ):
+        self.parts, self.bulk, self.pair_bulk = parts, bulk, pair_bulk
         self.view, self.orders, self.final = view, orders, final
         self.pair_view, self.pair_buf, self.buf = pair_view, pair_buf, buf
         self.pair_send, self.pair_recv = pair_send, pair_recv
         self.send_sem, self.recv_sem = send, recv
-        self.z, self.x, self.core, self.y = place()
-        self.sends = []
-        self.count = [0] * len(orders)
-        self.index = [{} for _ in orders]
+        self.z, self.x, self.core, self.y = place(known_z)
+        self.index = [self.places(chunk) for chunk in range(len(orders))]
 
     def rail(self, block):
         if "y" not in self.orders[0]:
@@ -311,7 +532,7 @@
         return pltpu.make_async_remote_copy(
             src_ref=self.pair_view(part, block, 1 - self.core),
             dst_ref=self.pair_buf(part, self.rail(block)),
-            send_sem=self.pair_send.at[part, self.rail(block)],
+            send_sem=self.pair_send.at[part, block[0] // 2],
             recv_sem=self.pair_recv.at[part, self.rail(block)],
             device_id=self.sibling(),
             device_id_type=MESH,
@@ -322,30 +543,40 @@
             self.pair_copy(part, self.coords(block)).start()
 
     def blocks(self):
-        dims = self.orders[0]
-        return [
-            (zz, fx, fy)
-            for fx in ((1, 0) if "x" in dims else (0,))
-            for fy in ((1, 0) if "y" in dims else (0,))
-            for zz in (3, 0, 2, 1)
-        ]
+        return [(zz, fx, fy) for zz in (3, 0, 2, 1) for fx, fy in self.flips(0, 0)]
+
+    def places(self, chunk):
+        order, keys = self.orders[chunk], []
+        for stage, dim in enumerate(order):
+            if dim == "z":
+                keys += [
+                    self.z_key(stage, step, way, flips)
+                    for step in range(3)
+                    for way in ((1, -1) if step else (1,))
+                    for flips in self.flips(chunk, stage)
+                ]
+                continue
+            wheres = range(4) if "z" in order[stage:] else ("own",)
+            later = self.flips(chunk, stage + 1)
+            keys += [(stage, where, *flips) for where in wheres for flips in later]
+        return {key: at for at, key in enumerate(keys)}
 
     def place_of(self, chunk, key):
-        return self.index[chunk].setdefault(key, len(self.index[chunk]))
+        return self.index[chunk][key]
 
     def send(self, chunk, block, key, target, cond):
+        if cond is False:
+            return
         where = self.place_of(chunk, key)
         copy = pltpu.make_async_remote_copy(
             src_ref=self.own(chunk, block),
             dst_ref=self.buf(chunk, where),
-            send_sem=self.send_sem.at[chunk, self.count[chunk]],
+            send_sem=self.send_sem.at[chunk, key[0]],
             recv_sem=self.recv_sem.at[chunk, where],
             device_id=target,
             device_id_type=MESH,
         )
-        self.count[chunk] += 1
         when(cond, copy.start)
-        self.sends.append((cond, copy))
 
     def landed(self, chunk, key):
         return self.buf(chunk, self.place_of(chunk, key))
@@ -419,9 +650,10 @@
         for way, cond in ((1, self.z >= 1), (-1, self.z <= 2)):
             landed = self.landed(chunk, self.z_key(stage, 2, way, flips))
 
-            @pl.when(cond)
-            def _(landed=landed):
+            def add(landed=landed):
                 final[...] += landed[...].astype(F32)
+
+            when(cond, add)
 
     def xy_arrive(self, chunk, stage, zz, fx, fy):
         key = (stage, zz, fx, fy)
@@ -441,7 +673,7 @@
         pltpu.make_async_remote_copy(
             src_ref=landed,
             dst_ref=landed,
-            send_sem=self.pair_send.at[part, self.rail(where)],
+            send_sem=self.pair_send.at[part, 0],
             recv_sem=self.pair_recv.at[part, self.rail(where)],
             device_id=self.sibling(),
             device_id_type=MESH,
@@ -488,51 +720,45 @@
         return found
 
     def finish(self):
-        for cond, copy in self.sends:
-            when(cond, copy.wait_send)
+        rails = len(self.blocks())
+        for chunk, order in enumerate(self.orders):
+            for stage, dim in enumerate(order):
+                after = len(self.flips(chunk, stage + 1)) if stage + 1 < len(order) else 1
+                count = 3 * after if dim == "z" else after * (4 if "z" in order[stage + 1 :] else 1)
+                every = self.bulk(chunk, count)
+                bulk_copy(every, self.send_sem.at[chunk, stage], self.recv_sem.at[chunk, 0]).wait_send()
         for part in range(self.parts):
-            for block in self.blocks():
-                self.pair_copy(part, self.coords(block)).wait_send()
+            every = self.pair_bulk(part, rails // 2)
+            for side in (0, 1):
+                bulk_copy(every, self.pair_send.at[part, side], self.pair_recv.at[part, 0]).wait_send()
 
 
 class Exchange:
-    def __init__(self, source, landing, send_sem, recv_sem):
-        self.source, self.landing = source, landing
+    def __init__(self, source, landing, bulk, send_sem, recv_sem):
+        self.source, self.landing, self.bulk = source, landing, bulk
         self.send_sem, self.recv_sem = send_sem, recv_sem
         self.band, self.y = lax.axis_index("band"), lax.axis_index("dp")
         self.bands = lax.axis_size("band")
 
-    def copy(self, target):
-        return pltpu.make_async_remote_copy(
+    def send(self, target):
+        pltpu.make_async_remote_copy(
             src_ref=self.source(target),
             dst_ref=self.landing(self.band),
-            send_sem=self.send_sem.at[target],
-            recv_sem=self.recv_sem.at[self.band],
+            send_sem=self.send_sem,
+            recv_sem=self.recv_sem,
             device_id=(target, self.y),
             device_id_type=MESH,
-        )
-
-    def others(self):
-        return [(self.band + step) % self.bands for step in range(1, self.bands)]
+        ).start()
 
     def start(self):
-        for target in self.others():
-            self.copy(target).start()
+        for step in range(1, self.bands):
+            self.send((self.band + step) % self.bands)
 
     def wait(self):
-        for other in self.others():
-            pltpu.make_async_remote_copy(
-                src_ref=self.landing(other),
-                dst_ref=self.landing(other),
-                send_sem=self.send_sem.at[other],
-                recv_sem=self.recv_sem.at[other],
-                device_id=(other, self.y),
-                device_id_type=MESH,
-            ).wait_recv()
+        bulk_copy(self.bulk(self.bands - 1), self.send_sem, self.recv_sem).wait_recv()
 
     def finish(self):
-        for target in self.others():
-            self.copy(target).wait_send()
+        bulk_copy(self.bulk(self.bands - 1), self.send_sem, self.recv_sem).wait_send()
 
 
 def dot_nt(left, right):
@@ -705,23 +931,131 @@
             - jnp.mean(scaled, axis=-1, keepdims=True)
             - unit * jnp.mean(scaled * unit, axis=-1, keepdims=True)
         )
-        self.grad_embed[...] = (self.grad_middle[...] + back).astype(B16)
-
-
-def spread(gathered, weights, chunk):
-    part, offset = chunk // 2, (chunk % 2) * CHUNK
+        self.grad_middle[...] += back
+
+    def embed_grad(self):
+        return self.grad_middle[...].astype(B16)
+
+
+def split3(rows):
+    first = rows.astype(B16)
+    rest = rows - first.astype(F32)
+    second = rest.astype(B16)
+    return first, second, (rest - second.astype(F32)).astype(B16)
+
+
+def fold3(stacked):
+    rows = stacked.shape[0] // 3
+    return stacked[:rows] + (stacked[rows : 2 * rows] + stacked[2 * rows :])
+
+
+def wide_nn(rows, weight):
+    return fold3(dot_nn(jnp.concatenate(split3(rows), axis=0), weight))
+
+
+def wide_nt(rows, weight):
+    return fold3(dot_nt(jnp.concatenate(split3(rows), axis=0), weight))
+
+
+def wide_tn(left, right):
+    one, two = split3(left), split3(right)
+    pairs = ((0, 0), (0, 1), (1, 0), (0, 2), (1, 1), (2, 0))
+    return dot_tn(
+        jnp.concatenate([one[a] for a, _ in pairs], axis=0),
+        jnp.concatenate([two[b] for _, b in pairs], axis=0),
+    )
+
+
+def exact_dot(left, right, dims):
+    return lax.dot_general(
+        left, right, (dims, ((), ())), precision=PRECISE, preferred_element_type=F32
+    )
+
+
+def hyper_unit(rows):
+    centred = rows - jnp.mean(rows, axis=-1, keepdims=True)
+    inverse = lax.rsqrt(jnp.mean(centred * centred, axis=-1, keepdims=True) + EPS_HYPER)
+    return centred * inverse, inverse
+
+
+def unit_back(scaled, unit, inverse):
+    return inverse * (
+        scaled
+        - jnp.mean(scaled, axis=-1, keepdims=True)
+        - unit * jnp.mean(scaled * unit, axis=-1, keepdims=True)
+    )
+
+
+def by_head(rows):
+    lane = lax.broadcasted_iota(jnp.int32, rows.shape, 1) // (rows.shape[1] // HHEADS)
+    return jnp.concatenate([jnp.where(lane == head, rows, 0.0) for head in range(HHEADS)], axis=0)
+
+
+def own_lanes(stacked):
+    tokens = stacked.shape[0] // HHEADS
+    out = jnp.zeros((tokens, stacked.shape[1]), F32)
+    for head in range(HHEADS):
+        rows = stacked[head * tokens : (head + 1) * tokens]
+        lane = lax.broadcasted_iota(jnp.int32, rows.shape, 1) // (rows.shape[1] // HHEADS)
+        out = out + jnp.where(lane == head, rows, 0.0)
+    return out
+
+
+def hyper_forward(waves, qkv, out, gain_one, up, down, gain_two):
+    width = waves.shape[1]
+    joint = wide_nn(waves, qkv)
+    query, key, value = (joint[:, at * width : (at + 1) * width] for at in range(3))
+    scores = exact_dot(by_head(query), key, ((1,), (1,))) / math.sqrt(width // HHEADS)
+    raised = jnp.exp(scores - jnp.max(scores, axis=-1, keepdims=True))
+    soft = raised / jnp.sum(raised, axis=-1, keepdims=True)
+    mixed = own_lanes(exact_dot(soft, value, ((1,), (0,))))
+    unit_one, inverse_one = hyper_unit(waves + wide_nn(mixed, out))
+    first = unit_one * gain_one
+    inner = wide_nn(first, up)
+    unit_two, inverse_two = hyper_unit(first + wide_nn(gelu_tanh(inner), down))
+    kept = (joint, soft, mixed, unit_one, inverse_one, inner, unit_two, inverse_two)
+    return unit_two * gain_two, kept
+
+
+def hyper_backward(grad_code, kept, waves, qkv, out, gain_one, up, down, gain_two):
+    joint, soft, mixed, unit_one, inverse_one, inner, unit_two, inverse_two = kept
+    width = waves.shape[1]
+    query, key, value = (joint[:, at * width : (at + 1) * width] for at in range(3))
+    first = unit_one * gain_one
+    grad_gain_two = jnp.sum(grad_code * unit_two, axis=0, keepdims=True)
+    grad_second = unit_back(grad_code * gain_two, unit_two, inverse_two)
+    grad_down = wide_tn(gelu_tanh(inner), grad_second)
+    grad_inner = wide_nt(grad_second, down) * gelu_slope(inner)
+    grad_up = wide_tn(first, grad_inner)
+    grad_first = grad_second + wide_nt(grad_inner, up)
+    grad_gain_one = jnp.sum(grad_first * unit_one, axis=0, keepdims=True)
+    grad_mid = unit_back(grad_first * gain_one, unit_one, inverse_one)
+    grad_out = wide_tn(mixed, grad_mid)
+    grad_mixed = by_head(wide_nt(grad_mid, out))
+    grad_value = exact_dot(soft, grad_mixed, ((0,), (0,)))
+    grad_soft = exact_dot(grad_mixed, value, ((1,), (1,)))
+    total = jnp.sum(grad_soft * soft, axis=-1, keepdims=True)
+    grad_scores = soft * (grad_soft - total) / math.sqrt(width // HHEADS)
+    grad_query = own_lanes(exact_dot(grad_scores, key, ((1,), (0,))))
+    grad_key = exact_dot(grad_scores, by_head(query), ((0,), (0,)))
+    grad_qkv = wide_tn(waves, jnp.concatenate([grad_query, grad_key, grad_value], axis=1))
+    return grad_qkv, grad_out, grad_gain_one, grad_up, grad_down, grad_gain_two
+
+
+def spread(gathered, weights, part):
     width = weights.shape[1]
+    half = CHUNK // 2
 
     @pl.loop(0, 16)
     def _(two):
-        one, other = (
-            gathered[part, pl.ds(aligned((two * 2 + k) * PART + offset), CHUNK), :].astype(F32)
-            for k in (0, 1)
-        )
-        half = CHUNK // 2
-        for k, rows in ((0, slice(0, half)), (1, slice(half, CHUNK))):
-            target = pl.ds(aligned((2 * chunk + k) * width + two * CHUNK), CHUNK)
-            weights[target, :] = jnp.concatenate([one[rows], other[rows]], 0).astype(B16)
+        for pair in (0, 1):
+            one, other = (
+                gathered[part, pl.ds(aligned((two * 2 + k) * PART + pair * CHUNK), CHUNK), :].astype(F32)
+                for k in (0, 1)
+            )
+            for k, rows in ((0, slice(0, half)), (1, slice(half, CHUNK))):
+                target = pl.ds(aligned((4 * part + 2 * pair + k) * width + two * CHUNK), CHUNK)
+                weights[target, :] = jnp.concatenate([one[rows], other[rows]], 0).astype(B16)
 
 
 def swap_rows(rows):
@@ -736,226 +1070,287 @@
     return ref.at[pl.ds(aligned(index * 16), 16)]
 
 
+KEPT = ("joint", "soft", "mixed", "unit_one", "inverse_one", "inner", "unit_two", "inverse_two")
+
+
 def layer_kernel(*refs):
-    (shard, pixels, kernel_gen, code_low, bias_gen, band_scale, out_grad, gain_one, gain_two,
-     block_out, pixel_out, shares, kernel_grads, code_grads, vectors,
-     gathered, weights, spare, pair_buf, buf, joint, probs, pre_act, act, grad_pre, mixed, normed_one, normed_two,
+    (pixels, kernel_gen, attn_qkv, attn_out, mlp_up, mlp_down, waves, hyper_qkv, hyper_out, hyper_gains, hyper_up, hyper_down,
+     bias_gen, band_scale, out_grad, gains,
+     block_out, pixel_out, shares, kernel_grads, code_out, code_grads, vectors, *rest_refs) = refs
+    kept_refs, rest_refs = rest_refs[: len(KEPT)], rest_refs[len(KEPT) :]
+    (gathered, weights, spare, pair_buf, buf, joint, probs, pre_act, act, grad_pre, mixed, normed_one, normed_two,
      unit_one, unit_two, inverse_one, inverse_two, grad_normed, grad_middle, grad_branch, grad_mixed, grad_joint,
-     turned_mixed, turned_one, turned_two, residual, pixel_rows, turned_pixels, mixing, kernels, sending,
-     image_grads, kernel_total, partner_grads, landed_grads, small, small_partner, small_all, code_part, code_all,
-     local_sem, pix_sem, gen_sem, front_done, *sems) = refs
+     turned_mixed, turned_one, residual, pixel_rows, turned_pixels, mixing, kernels, sending,
+     partner_grads, landed_grads, small, small_partner, small_all, code_part, code_all,
+     pix_sem, gen_sem, front_done, narrow_done, *sems) = rest_refs
     z, x, core, y = place()
     band = lax.axis_index("band")
     bands = lax.axis_size("band")
     me = slot(z, x, core, y)
-    width = gain_one.shape[1]
+    width = gains.shape[1]
     tokens = out_grad.shape[0]
     partner = (band, 1 - y)
-    (gather_sems, reduce_sems, embed_sems, grads_sems, kernel_sems, cols_sems, vec_sems, code_sems, half_sems, vec_half_sems) = (
-        sems[0:4], sems[4:8], sems[8:12], sems[12:16], sems[16:18], sems[18:20], sems[20:22], sems[22:24], sems[24:26], sems[26:28]
-    )
-
-    def gen_copy(piece, target, at):
+    own_rows = pl.ds(aligned(band * 16), 16)
+    gather_sems, reduce_sems, embed_sems, grads_sems = (sems[at : at + 4] for at in (0, 4, 8, 12))
+    kernel_sems, cols_sems, vec_sems, code_sems, half_sems, vec_half_sems = (
+        sems[at : at + 2] for at in (16, 18, 20, 22, 24, 26)
+    )
+
+    def gen_copy(piece, target):
         return pltpu.make_async_copy(
-            kernel_gen.at[:, pl.ds(piece * width, width)], target.at[pl.ds(at, 128)], gen_sem.at[piece]
+            kernel_gen.at[:, pl.ds(piece * width, width)], target.at[pl.ds(piece * 128, 128)], gen_sem
         )
 
+    def gen_wait(target):
+        every = target.at[pl.ds(0, 16 * 128)]
+        pltpu.make_async_copy(every, every, gen_sem).wait()
+
+    barrier = pltpu.get_barrier_semaphore()
+    tell_peers(barrier)
     for piece in range(16):
-        gen_copy(piece, spare, piece * 128).start()
-    own = [
-        pltpu.make_async_copy(
-            shard.at[pl.ds(part * PART, PART)],
-            gathered.at[part, pl.ds(aligned(me * PART), PART)],
-            local_sem.at[part],
-        )
-        for part in range(3)
-    ]
-    for copy in own:
-        copy.start()
+        gen_copy(piece, spare).start()
     load_pixels = pltpu.make_async_copy(pixels, pixel_rows, pix_sem)
     load_pixels.start()
-    meet_peers(pltpu.get_barrier_semaphore())
-    for copy in own:
-        copy.wait()
-
-    def weight_view(chunk, block, side):
+
+    def rows_of(weight, piece):
+        return weight[:, piece * width : (piece + 1) * width].astype(F32)
+
+    pieces = [rows_of(attn_qkv, at) for at in range(3)] + [rows_of(attn_out, 0)]
+    pieces += [rows_of(mlp_up, at) for at in range(4)]
+    for at in range(4):
+        rows = jnp.concatenate(pieces[2 * at : 2 * at + 2], axis=0).astype(B16)
+        gathered[at // 2, pl.ds(aligned(me * PART + at % 2 * CHUNK), CHUNK), :] = rows
+    gathered[2, pl.ds(aligned(me * PART), PART), :] = mlp_down[...]
+    code, kept = hyper_forward(
+        waves[...], hyper_qkv[...], hyper_out[...], hyper_gains[0:1, :], hyper_up[...], hyper_down[...], hyper_gains[1:2, :]
+    )
+    code_low = code.astype(B16)
+    code_out[...] = code_low
+    for ref, value in zip(kept_refs, kept):
+        ref[...] = value
+
+    def weight_view(part, block, side):
         where = slot(block[0], block[1], side, block[2])
-        return gathered.at[chunk // 2, pl.ds(aligned(where * PART + (chunk % 2) * CHUNK), CHUNK)]
-
-    gather = Gather(weight_view, ORDERS, *gather_sems)
-    arrivals = []
-    for chunk in range(len(ORDERS)):
-        arrivals += gather.events(chunk)
-    arrivals = Stream(arrivals)
-    for chunk in FIRST_CHUNKS:
-        gather.start(chunk)
-
-    for piece in range(16):
-        gen_copy(piece, spare, piece * 128).wait()
+        return gathered.at[part, pl.ds(aligned(where * PART), PART)]
+
+    half = tokens // 2
+
+    def image_row(block, side):
+        return (block[0] * 4 + block[1] * 2 + side) * tokens
+
+    def gather_at(known_z=None):
+        return Gather(
+            known_z, weight_view, ORDERS, lambda part, count: gathered.at[part, pl.ds(0, count * PART)], *gather_sems
+        )
+
+    def embed_at(known_z=None):
+        return Reduce(
+            known_z,
+            1,
+            lambda chunk, block, side: spare.at[pl.ds(aligned(image_row(block, side) + chunk * half), half)],
+            ("xz", "xz"),
+            lambda chunk: residual.at[pl.ds(chunk * half, half)],
+            lambda part, block, side: spare.at[pl.ds(aligned(image_row(block, side)), tokens)],
+            lambda part, rail: pair_buf.at[0, pl.ds(aligned(rail * tokens), tokens)],
+            lambda chunk, where: pair_buf.at[1, pl.ds((chunk * 9 + where) * half, half)],
+            lambda chunk, count: pair_buf.at[1, pl.ds(0, count * half)],
+            lambda part, count: pair_buf.at[0, pl.ds(0, count * tokens)],
+            *embed_sems,
+        )
+
+    def front_works(known_z):
+        known, sums = gather_at(known_z), embed_at(known_z)
+        works = [work for part in range(3) for work in in_order(known.events(part))]
+        return works + in_order(sums.events(0, (0, 1)))
+
+    gather, embed = gather_at(), embed_at()
+    plan = Plan(FRONT_PLAN, [front_works(known_z) for known_z in range(4)])
+    pl.semaphore_wait(barrier, bands)
+    plan.run()
+    for part in FIRST_PARTS:
+        gather.start(part)
+    plan.run()
+
+    gen_wait(spare)
 
     @pl.loop(0, 16)
     def _(piece):
-        part = dot_nn(code_low[...], spare[pl.ds(aligned(piece * 128), 128), :])
+        part = dot_nn(code_out[...], spare[pl.ds(aligned(piece * 128), 128), :])
         mixing[pl.ds(aligned(piece * 16), 16), :] = part.astype(B16)
 
     sending[...] = swap_rows(mixing[...])
     spread_kernels = Exchange(
-        lambda target: rows16(sending, target), lambda source: rows16(kernels, source), *kernel_sems
+        lambda target: rows16(sending, target),
+        lambda source: rows16(kernels, source),
+        lambda count: kernels.at[pl.ds(0, count * 16)],
+        *[sem.at[0] for sem in kernel_sems],
     )
     spread_kernels.start()
-    for chunk in range(len(ORDERS)):
-        if chunk not in FIRST_CHUNKS:
-            gather.start(chunk)
-    own_rows = pl.ds(aligned(band * 16), 16)
+    plan.run()
+    for part in range(3):
+        if part not in FIRST_PARTS:
+            gather.start(part)
+    plan.run()
     kernels[own_rows, :] = sending[own_rows, :]
-    biases = dot_nn(code_low[...], bias_gen[...])
+    biases = dot_nn(code_out[...], bias_gen[...])
     chosen = lax.broadcasted_iota(jnp.int32, biases.shape, 0) == band
     bias = jnp.sum(jnp.where(chosen, biases, 0.0), axis=0, keepdims=True)
     load_pixels.wait()
     for group in range(4):
         turned_pixels[group] = pixel_rows[4 * group : 4 * group + 4].reshape(4 * tokens, -1).T
-    arrivals.run(EARLY)
+    plan.run()
     spread_kernels.wait()
 
-    @pl.loop(0, 4)
-    def _(group):
-        rows = pixel_rows[pl.ds(group * 4, 4)].reshape(4 * tokens, -1)
+    def term(group):
+        rows = pixel_rows[4 * group : 4 * group + 4].reshape(4 * tokens, -1)
         for at in range(0, width, 256):
             terms = dot_nn(rows, kernels[:, at : at + 256]) + bias[:, at : at + 256]
             for image in range(4):
                 scale = band_scale[group * 4 + image][:1, :1]
-                target = pl.ds(aligned((group * 4 + image) * tokens), tokens)
-                spare[target, at : at + 256] = (
-                    terms[image * tokens : (image + 1) * tokens] * scale
-                ).astype(B16)
-
-    half = tokens // 2
-
-    def image_row(block, side):
-        return (block[0] * 4 + block[1] * 2 + side) * tokens
-
-    embed = Reduce(
-        1,
-        lambda chunk, block, side: spare.at[pl.ds(aligned(image_row(block, side) + chunk * half), half)],
-        ("xz", "xz"),
-        lambda chunk: residual.at[pl.ds(chunk * half, half)],
-        lambda part, block, side: spare.at[pl.ds(aligned(image_row(block, side)), tokens)],
-        lambda part, rail: pair_buf.at[0, pl.ds(aligned(rail * tokens), tokens)],
-        lambda chunk, where: pair_buf.at[1, pl.ds((chunk * 9 + where) * half, half)],
-        *embed_sems,
-    )
-    embed.pair_start(0)
-    sums = Stream(embed.events(0, (0, 1)))
-    while sums.at < len(sums.events):
-        sums.run(EMBED_RUN[0])
-        arrivals.run(EMBED_RUN[1])
-    tell_peers(front_done)
-    arrivals.run()
-    for chunk in range(4):
-        gather.wait_pairs(chunk)
-        spread(gathered, weights, chunk)
-    for chunk in (4, 5):
-        gather.wait_pairs(chunk)
-    gather.finish()
+                target = pl.ds((group * 4 + image) * tokens, tokens)
+                spare[target, at : at + 256] = (terms[image * tokens : (image + 1) * tokens] * scale).astype(B16)
+
+    for group in (3, 0, 2, 1):
+        plan.run()
+        term(group)
+        embed.pair_start(0, [(group, 1, 0), (group, 0, 0)])
+    plan.run()
+    gather.wait_pairs(0)
+    spread(gathered, weights, 0)
 
     names = dict(
-        residual=residual, out_grad=out_grad, gain_one=gain_one, gain_two=gain_two, block_out=block_out,
+        residual=residual, out_grad=out_grad, gain_one=gains.at[0:1], gain_two=gains.at[1:2], block_out=block_out,
         joint=joint, probs=probs, pre_act=pre_act, act=act,
         grad_pre=grad_pre, mixed=mixed, normed_one=normed_one, normed_two=normed_two, unit_one=unit_one,
         unit_two=unit_two, inverse_one=inverse_one, inverse_two=inverse_two, result=residual, grad_normed=grad_normed,
         grad_middle=grad_middle, grad_branch=grad_branch, grad_mixed=grad_mixed, grad_joint=grad_joint,
-        turned_mixed=turned_mixed, small=small, grad_embed=image_grads.at[band],
+        turned_mixed=turned_mixed, small=small,
     )
     block = Block(weights, gathered.at[2], names)
+    plan.run()
     block.project()
+    plan.run()
     block.attend()
+    plan.run()
+    gather.wait_pairs(1)
+    spread(gathered, weights, 1)
+    plan.run()
     block.widen()
+    plan.run()
+    gather.wait_pairs(2)
+    gather.finish()
+    embed.finish()
+    tell_near(front_done)
     block.narrow()
+    plan.run()
 
     def part_ref(part):
         return spare if part == 2 else gathered.at[part]
 
-    def grad_view(chunk, blk, side):
-        where = slot(blk[0], blk[1], side, blk[2])
-        return part_ref(chunk // 2).at[pl.ds(aligned(where * PART + (chunk % 2) * CHUNK), CHUNK)]
-
     def part_view(part, blk, side):
         return part_ref(part).at[pl.ds(aligned(slot(blk[0], blk[1], side, blk[2]) * PART), PART)]
 
-    reduce = Reduce(
-        3,
-        grad_view,
-        tuple(order[::-1] for order in ORDERS),
-        lambda chunk: shares.at[pl.ds(chunk * CHUNK, CHUNK)],
-        part_view,
-        lambda part, rail: pair_buf.at[part, pl.ds(aligned(rail * PART), PART)],
-        lambda chunk, where: buf.at[chunk, where],
-        *reduce_sems,
-    )
-    embed.finish()
+    def reduce_at(known_z=None):
+        return Reduce(
+            known_z,
+            3,
+            part_view,
+            SUM_ORDERS,
+            lambda part: shares.at[pl.ds(part * PART, PART)],
+            part_view,
+            lambda part, rail: pair_buf.at[part, pl.ds(aligned(rail * PART), PART)],
+            lambda part, where: buf.at[part, where],
+            lambda part, count: part_ref(part).at[pl.ds(0, count * PART)],
+            lambda part, count: part_ref(part).at[pl.ds(0, count * PART)],
+            *reduce_sems,
+        )
+
+    image_grads = gathered.at[2]
+
+    def image_view(chunk, blk, side):
+        return image_grads.at[pl.ds(aligned(image_row(blk, side) + chunk * half), half)]
+
+    def grads_at(known_z=None):
+        return Gather(
+            known_z, image_view, ("zx", "zx"), lambda chunk, count: image_grads.at[pl.ds(0, count * half)], *grads_sems
+        )
+
+    def tail_works(known_z):
+        known, images = reduce_at(known_z), grads_at(known_z)
+        works = [work for part in (2, 1, 0) for work in in_order(known.events(part, (part,)))]
+        return works + [work for chunk in (0, 1) for work in in_order(images.events(chunk))]
+
+    reduce, grads = reduce_at(), grads_at()
+    plan = Plan(TAIL_PLAN, [tail_works(known_z) for known_z in range(4)])
     grad_normed[...] = jnp.zeros(grad_normed.shape, F32)
+    hear_near(front_done)
+    plan.run()
 
     @pl.loop(0, 4)
-    def _(part):
-        block.back_narrow(part)
-        block.down_grad(part, spare)
-
-    pl.semaphore_wait(front_done, bands)
-    reduce.pair_start(2)
-    rest = Stream(reduce.events(2, (4, 5)))
+    def _(step):
+        odd = step % 2
+        zz = (1 - odd) * (3 - step // 2) + odd * (step // 2)
+        block.back_narrow(zz)
+        block.down_grad(zz, spare)
+        reduce.pair_start(2, [(zz, fx, fy) for fx, fy in ((1, 1), (1, 0), (0, 1), (0, 0))])
+
+    tell_near(narrow_done)
+    plan.run()
     block.back_wide()
-    rest.run(BACK_RUN[0])
+    plan.run()
     block.back_attend()
-    rest.run(BACK_RUN[1])
+    plan.run()
     block.back_project()
-
-    def image_view(chunk, blk, side):
-        return image_grads.at[blk[0] * 4 + blk[1] * 2 + side, pl.ds(chunk * half, half)]
-
-    grads = Gather(image_view, ("zx", "zx"), *grads_sems)
+    hear_near(narrow_done)
+    image_grads[pl.ds(aligned(band * tokens), tokens), :] = block.embed_grad()
     grads.start(0)
     grads.start(1)
-    images = Stream(grads.events(0) + grads.events(1))
-    turned_two[...] = normed_two[...].T
+    turned_one[...] = normed_two[...].T
     for part in (0, 2):
+        plan.run()
         block.pair_grad(
-            turned_two, turned_two, lambda cols, part=part: grad_pre[part, :, cols],
+            turned_one, turned_one, lambda cols, part=part: grad_pre[part, :, cols],
             lambda cols, part=part: grad_pre[part + 1, :, cols], part_ref(1), part // 2 * CHUNK,
         )
-        images.run(GRAD_RUN)
     reduce.pair_start(1)
+    plan.run()
     turned_one[...] = normed_one[...].T
     block.pair_grad(
         turned_one, turned_one, lambda cols: grad_joint[0, :, cols], lambda cols: grad_joint[1, :, cols], part_ref(0), 0
     )
-    images.run(GRAD_RUN)
+    plan.run()
     block.pair_grad(
         turned_one, turned_mixed, lambda cols: grad_joint[2, :, cols], lambda cols: grad_branch[:, cols], part_ref(0), CHUNK
     )
     reduce.pair_start(0)
-    images.run()
     for piece in range(16):
-        gen_copy(piece, weights, piece * 128).start()
-
+        gen_copy(piece, weights).start()
+
+    kernel_total = pre_act.at[0:2]
     kernel_total[...] = jnp.zeros(kernel_total.shape, F32)
     small[2:3, :] = jnp.zeros((1, width), F32)
-    for chunk in (0, 1):
-        grads.wait_pairs(chunk)
-
-    @pl.loop(0, 4)
-    def _(group):
-        for image in range(4):
-            scaled = image_grads[group * 4 + image].astype(F32) * band_scale[group * 4 + image][:1, :1]
-            small[2:3, :] += jnp.sum(scaled, axis=0, keepdims=True)
-            act[image] = scaled.astype(B16)
-        scaled = act[...].reshape(4 * tokens, width)
-        pixel_rows[pl.ds(group * 4, 4)] = dot_nt(scaled, kernels[...]).astype(B16).reshape(4, tokens, -1)
-        kernel_total[...] += dot_nn(turned_pixels[group], scaled)
+    near_side = z // 2
+    for side in (near_side, 1 - near_side):
+        plan.run()
+        for chunk in (0, 1):
+            grads.wait_side(chunk, side)
+
+        @pl.loop(0, 2)
+        def _(step, side=side):
+            group = 2 * side + step
+            for image in range(4):
+                rows = pl.ds(aligned((group * 4 + image) * tokens), tokens)
+                scaled = image_grads[rows, :].astype(F32) * band_scale[group * 4 + image][:1, :1]
+                small[2:3, :] += jnp.sum(scaled, axis=0, keepdims=True)
+                act[image] = scaled.astype(B16)
+            scaled = act[...].reshape(4 * tokens, width)
+            pixel_rows[pl.ds(group * 4, 4)] = dot_nt(scaled, kernels[...]).astype(B16).reshape(4, tokens, -1)
+            kernel_total[...] += dot_nn(turned_pixels[group], scaled).reshape(kernel_total.shape)
 
     store_pixels = pltpu.make_async_copy(pixel_rows, pixel_out, pix_sem)
     store_pixels.start()
     spread_kernels.finish()
-    sending[...] = kernel_total[...].astype(B16)
+    sending[...] = kernel_total[...].astype(B16).reshape(sending.shape)
     quarter = sending.shape[0] // 4
 
     def half_copy(piece):
@@ -973,9 +1368,13 @@
     )
     vec_half.start()
     columns = Exchange(
-        lambda target: rows16(mixing, target), lambda source: rows16(landed_grads, source), *cols_sems
+        lambda target: rows16(mixing, target),
+        lambda source: rows16(landed_grads, source),
+        lambda count: landed_grads.at[pl.ds(0, count * 16)],
+        *[sem.at[0] for sem in cols_sems],
     )
     for piece in range(4):
+        plan.run()
         half_copy(piece).wait_recv()
         rows = pl.ds(piece * quarter, quarter)
         mixing[rows, :] = sending[rows, :] + partner_grads[rows, :]
@@ -984,23 +1383,24 @@
 
             @pl.when(target != band)
             def _(target=target):
-                columns.copy(target).start()
+                columns.send(target)
 
     landed_grads[own_rows, :] = mixing[own_rows, :]
+    plan.run()
     vec_half.wait_recv()
     small_all[band] = small[...] + small_partner[...]
-    vector_spread = Exchange(lambda target: small_all.at[band], lambda source: small_all.at[source], *vec_sems)
+    vector_spread = Exchange(
+        lambda target: small_all.at[band], lambda source: small_all.at[source], lambda count: small_all.at[pl.ds(0, count)],
+        *[sem.at[0] for sem in vec_sems],
+    )
     vector_spread.start()
-    events = reduce.events(1, (2, 3)) + reduce.events(0, (0, 1))
-    rest.events = rest.events + sorted(events, key=lambda event: event[:2])
-    rest.run(TAIL_RUN[0])
+    plan.run()
     columns.wait()
     for piece in range(4):
         half_copy(piece).wait_send()
     sending[...] = swap_rows(landed_grads[...])
-    kernel_grads[...] = landed_grads[...]
-    for piece in range(16):
-        gen_copy(piece, weights, piece * 128).wait()
+    store_columns = pltpu.make_async_copy(landed_grads, kernel_grads, pix_sem)
+    gen_wait(weights)
     code_part[...] = jnp.zeros(code_part.shape, F32)
 
     @pl.loop(0, 16)
@@ -1010,9 +1410,14 @@
         )
 
     code_all[band] = code_part[...]
-    code_spread = Exchange(lambda target: code_all.at[band], lambda source: code_all.at[source], *code_sems)
+    code_spread = Exchange(
+        lambda target: code_all.at[band], lambda source: code_all.at[source], lambda count: code_all.at[pl.ds(0, count)],
+        *[sem.at[0] for sem in code_sems],
+    )
     code_spread.start()
-    rest.run(TAIL_RUN[1])
+    store_pixels.wait()
+    store_columns.start()
+    plan.run()
     vector_spread.wait()
     vectors[...] = small_all[...]
     code_spread.wait()
@@ -1020,41 +1425,32 @@
     for source in range(1, bands):
         total = total + code_all[source]
     code_grads[...] = total
-    rest.run()
+    plan.run()
     reduce.finish()
     grads.finish()
     columns.finish()
     vec_half.wait_send()
     vector_spread.finish()
     code_spread.finish()
-    store_pixels.wait()
-
-
-FIRST_CHUNKS = (0, 1, 2, 3, 4, 5)
-EARLY = 10
-EMBED_RUN = (2, 2)
-BACK_RUN = (20, 20)
-GRAD_RUN = 4
-TAIL_RUN = (20, 20)
-
-
-def layer(weights, pixels, kernel_gen, code_low, bias_gen, band_scale, out_grad, gain_one, gain_two):
-    width = weights[1].shape[1]
+    store_columns.wait()
+
+
+VMEM_BYTES = 63 * 2**20
+
+
+def layer(pixels, kernel_gen, weights, waves, hyper, bias_gen, band_scale, out_grad, gains):
+    width = gains.shape[1]
     bands = lax.axis_size("band")
     devices = bands * lax.axis_size("dp")
     images, tokens, pix = pixels.shape
-
-    def stack(weight):
-        parts = weight.shape[1] // width
-        return weight.reshape(weight.shape[0], parts, width).transpose(1, 0, 2).reshape(-1, width)
-
-    shard = jnp.concatenate([stack(w) for w in weights], axis=0)
-    chunks = len(ORDERS)
+    hidden = hyper[3].shape[1]
     vmem = pl.BlockSpec(memory_space=pltpu.VMEM)
     hbm = pl.BlockSpec(memory_space=pl.ANY)
     shape = jax.ShapeDtypeStruct
     rows = lambda kind, *lead: pltpu.VMEM((*lead, tokens, width), kind)
     dma = pltpu.SemaphoreType.DMA
+    code = (bands, HW)
+    kept = [(bands, 3 * HW), (HHEADS * bands, bands), code, code, (bands, 1), (bands, hidden), code, (bands, 1)]
     return pl.pallas_call(
         layer_kernel,
         out_shape=[
@@ -1062,17 +1458,19 @@
             shape(pixels.shape, B16),
             shape((3 * PART, width), F32),
             shape((pix, width), B16),
-            shape((bands, code_low.shape[1]), F32),
+            shape(code, B16),
+            shape(code, F32),
             shape((bands, 8, width), F32),
+            *[shape(dims, F32) for dims in kept],
         ],
-        in_specs=[hbm, hbm, hbm] + [vmem] * 6,
-        out_specs=[vmem, hbm, vmem, vmem, vmem, vmem],
+        in_specs=[hbm, hbm] + [vmem] * 14,
+        out_specs=[vmem, hbm, vmem, hbm] + [vmem] * 11,
         scratch_shapes=[
             pltpu.VMEM((3, devices * PART, width), B16),
             pltpu.VMEM((8 * width, width), B16),
             pltpu.VMEM((devices * PART, width), B16),
             pltpu.VMEM((3, devices // 2 * PART, width), B16),
-            pltpu.VMEM((chunks, 19, CHUNK, width), B16),
+            pltpu.VMEM((3, 19, PART, width), B16),
             rows(B16, 3),
             pltpu.VMEM((HEADS // 2, 2 * tokens, tokens), F32),
             rows(F32, 4),
@@ -1092,56 +1490,120 @@
             rows(B16, 3),
             pltpu.VMEM((width, tokens), B16),
             pltpu.VMEM((width, tokens), B16),
-            pltpu.VMEM((width, tokens), B16),
             rows(F32),
             pltpu.VMEM(pixels.shape, B16),
             pltpu.VMEM((4, pix, 4 * tokens), B16),
             pltpu.VMEM((pix, width), B16),
             pltpu.VMEM((pix, width), B16),
             pltpu.VMEM((pix, width), B16),
-            pltpu.VMEM((images, tokens, width), B16),
-            pltpu.VMEM((pix, width), F32),
             pltpu.VMEM((pix, width), B16),
             pltpu.VMEM((pix, width), B16),
             pltpu.VMEM((8, width), F32),
             pltpu.VMEM((8, width), F32),
             pltpu.VMEM((bands, 8, width), F32),
-            pltpu.VMEM((bands, code_low.shape[1]), F32),
-            pltpu.VMEM((bands, bands, code_low.shape[1]), F32),
-            dma((3,)),
+            pltpu.VMEM(code, F32),
+            pltpu.VMEM((bands, *code), F32),
             dma,
-            dma((16,)),
+            dma,
             pltpu.SemaphoreType.REGULAR,
-            dma((chunks, 40)), dma((chunks, 16)), dma((chunks, 16)), dma((chunks, 16)),
-            dma((3, 16)), dma((3, 16)), dma((chunks, 48)), dma((chunks, 24)),
-            dma((1, 8)), dma((1, 8)), dma((2, 24)), dma((2, 16)),
-            dma((2, 16)), dma((2, 16)), dma((2, 16)), dma((2, 16)),
-            dma((bands,)), dma((bands,)),
-            dma((bands,)), dma((bands,)),
-            dma((bands,)), dma((bands,)),
-            dma((bands,)), dma((bands,)),
-            dma((4,)), dma((4,)),
-            dma((1,)), dma((1,)),
+            pltpu.SemaphoreType.REGULAR,
+            *[dma((3, 3)), dma((3, 16)), dma((3, 2)), dma((3, 2))],
+            *[dma((3, 2)), dma((3, 16)), dma((3, 3)), dma((3, 19))],
+            *[dma((1, 2)), dma((1, 8)), dma((2, 2)), dma((2, 9))],
+            *[dma((2, 3)), dma((2, 16)), dma((2, 2)), dma((2, 2))],
+            *[dma((1,))] * 8,
+            *[dma((4,))] * 2,
+            *[dma((1,))] * 2,
         ],
         compiler_params=pltpu.CompilerParams(
             collective_id=0, has_side_effects=True, vmem_limit_bytes=VMEM_BYTES
         ),
         name="layer",
-    )(shard, pixels, kernel_gen, code_low, bias_gen, band_scale, out_grad, gain_one, gain_two)
-
-
-VMEM_BYTES = 63 * 2**20
-
-
-def split_shares(shares, weights):
-    width = shares.shape[1]
-    grads, at = [], 0
-    for weight in weights:
-        own_rows, parts = weight.shape[0], weight.shape[1] // width
-        piece = shares[at : at + own_rows * parts].reshape(parts, own_rows, width)
-        grads.append(piece.transpose(1, 0, 2).reshape(own_rows, parts * width))
-        at += own_rows * parts
-    return grads
+    )(pixels, kernel_gen, *weights, waves, *hyper, bias_gen, band_scale, out_grad, gains)
+
+
+def finish_kernel(*refs):
+    count = 12 + len(KEPT)
+    block_in, pixel_in, *outside = refs[: count + 2]
+    (block_out, pixel_out, grad_qkv, grad_out, grad_gain_one, grad_up, grad_down, grad_gain_two, grad_gen, grad_bias,
+     gain_sums, share_qkv, share_out, share_up, share_down, *scratch) = refs[count + 2 :]
+    inside, (store, in_sem, copy_sem, gen_sem) = scratch[:count], scratch[count:]
+    loads = [pltpu.make_async_copy(*pair, in_sem.at[at]) for at, pair in enumerate(zip(outside, inside))]
+    for load in loads:
+        load.start()
+    (code_low, columns, shares, waves, hyper_qkv, hyper_out, hyper_gains, hyper_up, hyper_down, bias_gen, code_grads, vectors,
+     *kept_refs) = inside
+    width = bias_gen.shape[1]
+    copies = [
+        pltpu.make_async_copy(block_in, block_out, copy_sem.at[0]),
+        pltpu.make_async_copy(pixel_in, pixel_out, copy_sem.at[1]),
+    ]
+    for copy in copies:
+        copy.start()
+    for load in loads[:2]:
+        load.wait()
+    code = code_low[...]
+    swapped = swap_rows(columns[...])
+    gen_copies = []
+    for piece in range(16):
+        slot_at = piece % store.shape[0]
+        if piece >= store.shape[0]:
+            gen_copies[piece - store.shape[0]].wait()
+        store[slot_at] = dot_tn(code, swapped[piece * 16 : (piece + 1) * 16])
+        gen_copies.append(
+            pltpu.make_async_copy(
+                store.at[slot_at], grad_gen.at[:, pl.ds(piece * width, width)], gen_sem.at[slot_at]
+            )
+        )
+        gen_copies[-1].start()
+    for load in loads[2:]:
+        load.wait()
+    share_qkv[...] = jnp.concatenate([shares[at * 24 : at * 24 + 24, :] for at in range(3)], axis=1)
+    share_out[...] = shares[72:96, :]
+    share_up[...] = jnp.concatenate([shares[at * 24 : at * 24 + 24, :] for at in range(4, 8)], axis=1)
+    share_down[...] = shares[192:288, :]
+    gain_sums[...] = jnp.sum(vectors[...], axis=0)
+    bias_grads = vectors[:, 2, :]
+    grad_bias[...] = dot_tn(jnp.concatenate([code] * 3, axis=0), jnp.concatenate(split3(bias_grads), axis=0))
+    grad_code = code_grads[...] + wide_nt(bias_grads, bias_gen[...])
+    grads = hyper_backward(
+        grad_code, [ref[...] for ref in kept_refs], waves[...], hyper_qkv[...], hyper_out[...], hyper_gains[0:1, :],
+        hyper_up[...], hyper_down[...], hyper_gains[1:2, :],
+    )
+    for ref, value in zip((grad_qkv, grad_out, grad_gain_one, grad_up, grad_down, grad_gain_two), grads):
+        ref[...] = value
+    for copy in copies + gen_copies[-store.shape[0] :]:
+        copy.wait()
+
+
+def finish(waves, hyper, bias_gen, code_low, code_grads, vectors, columns, shares, block_out, pixel_grad, kept, kernel_gen, weights):
+    width = bias_gen.shape[1]
+    vmem = pl.BlockSpec(memory_space=pltpu.VMEM)
+    hbm = pl.BlockSpec(memory_space=pl.ANY)
+    shape = lambda array: jax.ShapeDtypeStruct(array.shape, F32)
+    line = jax.ShapeDtypeStruct((1, HW), F32)
+    operands = (code_low, columns, shares, waves, *hyper, bias_gen, code_grads, vectors, *kept)
+    return pl.pallas_call(
+        finish_kernel,
+        out_shape=[
+            jax.ShapeDtypeStruct(block_out.shape, B16),
+            jax.ShapeDtypeStruct(pixel_grad.shape, B16),
+            shape(hyper[0]), shape(hyper[1]), line, shape(hyper[3]), shape(hyper[4]), line,
+            shape(kernel_gen), shape(bias_gen), jax.ShapeDtypeStruct((8, width), F32),
+            *[shape(weight) for weight in weights],
+        ],
+        in_specs=[hbm] * (2 + len(operands)),
+        out_specs=[hbm, hbm] + [vmem] * 6 + [hbm] + [vmem] * 6,
+        scratch_shapes=[
+            *[pltpu.VMEM(operand.shape, operand.dtype) for operand in operands],
+            pltpu.VMEM((4, HW, width), F32),
+            pltpu.SemaphoreType.DMA((len(operands),)),
+            pltpu.SemaphoreType.DMA((2,)),
+            pltpu.SemaphoreType.DMA((4,)),
+        ],
+        compiler_params=pltpu.CompilerParams(vmem_limit_bytes=40 * 2**20),
+        name="finish",
+    )(block_out, pixel_grad, *operands)
 
 
 def body(
@@ -1359,49 +1821,54 @@
     mlp_down,
     out_grad,
 ):
-    hyper_params = tuple(
-        weight.astype(F32)
-        for weight in (hyper_qkv, hyper_out, hyper_gain1, hyper_up, hyper_down, hyper_gain2)
-    )
-    wave_tokens = wave_embed(wavelengths, HW)
-    band_code, hyper_pull = jax.vjp(lambda *params: hyper_net(wave_tokens, *params), *hyper_params)
-    code_low = band_code.astype(B16)
+    waves = wave_embed(wavelengths, HW)
     band = lax.axis_index("band")
     count_row = band_counts[0]
     active = (band < count_row) & (band_mask[0, :, 0] == 1)
     band_weight = jnp.where(active, lax.rsqrt(count_row.astype(F32)), F32(0.0))
     weights = (attn_qkv, attn_out, mlp_up, mlp_down)
-    block_out, pixel_grad, shares, kernel_grads, grad_code, vectors = layer(
-        weights,
+    hyper_gains = jnp.stack([hyper_gain1, hyper_gain2]).astype(F32)
+    hyper = (hyper_qkv, hyper_out, hyper_gains, hyper_up, hyper_down)
+    block_out, pixel_grad, shares, columns, code_low, code_grads, vectors, *kept = layer(
         pixels[0, :, :, 0],
         kernel_gen,
-        code_low,
+        weights,
+        waves,
+        hyper,
         bias_gen,
         jnp.broadcast_to(band_weight[:, None, None], (band_weight.shape[0], 8, 128)),
         out_grad[0, 0],
-        norm_gain1.astype(F32)[None],
-        norm_gain2.astype(F32)[None],
-    )
-    grad_columns = kernel_grads.reshape(band_code.shape[0], -1)
-    grad_kernel_gen = jnp.einsum("nh,nc->hc", code_low, grad_columns, preferred_element_type=F32)
-    bias_grads = vectors[:, 2]
-    grad_code = grad_code + jnp.dot(bias_grads, bias_gen.astype(F32).T, precision=PRECISE)
-    grad_bias_gen = jnp.dot(code_low.astype(F32).T, bias_grads, precision=PRECISE)
-    grad_norm_gain1, grad_norm_gain2 = (jnp.sum(vectors[:, row], axis=0) for row in (0, 1))
-    hyper_grads = hyper_pull(grad_code)
-    shares = split_shares(shares, weights)
+        jnp.stack([norm_gain1, norm_gain2]).astype(F32),
+    )
+    outs = finish(
+        waves,
+        hyper,
+        bias_gen,
+        code_low,
+        code_grads,
+        vectors,
+        columns,
+        shares,
+        block_out,
+        pixel_grad,
+        kept,
+        kernel_gen,
+        weights,
+    )
+    block_out, pixel_grad, *hyper_grads, grad_gen, grad_bias, gain_sums = outs[:11]
+    hyper_grads[2], hyper_grads[5] = hyper_grads[2][0], hyper_grads[5][0]
     return (
         block_out[None, None],
         pixel_grad[None, :, :, None],
         *hyper_grads,
-        grad_kernel_gen,
-        grad_bias_gen,
-        grad_norm_gain1,
-        shares[0],
-        shares[1],
-        grad_norm_gain2,
-        shares[2],
-        shares[3],
+        grad_gen,
+        grad_bias,
+        gain_sums[0],
+        outs[11],
+        outs[12],
+        gain_sums[1],
+        outs[13],
+        outs[14],
     )
 
 

time: 301 us -> 213 us (0.71)
  Pallas kernels: 246 us -> 191 us
  matrix products: 26.4 us -> 0 us
  other arithmetic: 11.2 us -> 4.08 us
    pallas_call x1, Pallas kernels: 246 us -> 182 us  [layer(): pl.pallas_call(layer_kernel, out_shape=[shape((tokens, width), B16), shap...]
    dot_general x20 -> x0, matrix products: 26.4 us -> none  [the longest x3 5.92 us: hyper_net(): jnp.dot(inner_act, down_weight, precision=PRECISE)]
    unnamed x45 -> x44, local copies, waits for them, and re-layouts: 3.47 us -> 13.6 us
    pallas_call x0 -> x1, Pallas kernels: none -> 9.5 us  [finish(): pl.pallas_call(finish_kernel, out_shape=[jax.ShapeDtypeStruct(block_out.s...]
    reduce_sum x6 -> x0, other arithmetic: 4.15 us -> none  [the longest x1 2.02 us: fast_body(): jnp.sum(vectors[:, row], axis=0)]
    slice x4 -> x1, local copies, waits for them, and re-layouts: 4.32 us -> 0.61 us  [fast_body(): gain_sums[1]]
    reshape x13 -> x0, local copies, waits for them, and re-layouts: 3.63 us -> none  [the longest x2 1.87 us: stack(): weight.reshape(weight.shape[0], parts, width).transpose(1, 0, 2)]
where the time goes in v4:
time: 213 us; the launch traced here: 212 us
  Pallas kernels  191 us (90%)
  local copies, waits for them, and re-layouts  16.3 us (8%)
  other arithmetic  4.08 us (2%)
    pallas_call x1, Pallas kernels, layer(): pl.pallas_call(layer_kernel, out_shape=[shape((tokens, width), B16), shap...  182 us
    unnamed x44, local copies, waits for them, and re-layouts  13.6 us
    pallas_call x1, Pallas kernels, finish(): pl.pallas_call(finish_kernel, out_shape=[jax.ShapeDtypeStruct(block_out.s...  9.5 us

profile of v4, /device:TPU:0, one launch (start us, length us, event | category | flops | bytes accessed | tf_op | source)
XLA Modules:
  0.0 212.3 jit_solution(8003869457396717266)
XLA Ops:
  0.7 0.8 fusion
  2.1 1.2 maximum_convert_fusion.1.refs_9_.refs_8_
  3.4 0.7 stack.21
  4.1 0.7 stack.22
  5.5 0.7 pad_maximum_fusion.refs_6_.refs_5_
  6.2 0.7 broadcast_in_dim.19.refs_13_
  6.9 181.6 %layer.1 = (bf16[128,768]{1,0:T(8,128)(2,1)}, bf16[16,128,256]{2,1,0:T(8,128)(2,1)}, f32[288,768]{1,0:T(8,128)}, bf16[256,768]{1,0:T(8,128)(2,1)}, bf16[16,128]{...) custom-call(bf16[16,128,256]{2,1,0:T(8,128)(2,1)} %bitcast.18, ...), custom_call_target="tpu_custom_call" | custom-call | tf_op jit(solution)/shard_map/layer/pallas_call | solution.py:1454
  188.6 1.0 copy-done.1
  189.6 1.2 copy-done.2
  190.9 1.2 copy-done.3
  192.0 1.0 copy-done.5
  193.0 1.0 copy-done.6
  194.0 0.9 copy-done.8
  195.0 0.9 copy-done.10
  195.9 0.8 copy-done.12
  196.6 0.7 copy-done.13
  197.4 0.7 copy-done.15
  198.1 0.7 copy-done.16
  198.7 0.7 copy-done.17
  199.4 0.7 copy-done.18
  200.1 0.7 copy-done.19
  200.8 0.7 copy-done.20
  201.5 0.7 copy-done.21
  202.2 9.5 %finish.1 = (bf16[128,768]{1,0:T(8,128)(2,1)}, bf16[16,128,256]{2,1,0:T(8,128)(2,1)}, f32[128,384]{1,0:T(8,128)}, f32[128,128]{1,0:T(8,128)}, f32[1,128]{1,0:T(1...) custom-call(bf16[128,768]{1,0:T(8,128)(2,1)S(1)} %copy-done.8, ...), custom_call_target="tpu_custom_call" | custom-call | tf_op jit(solution)/shard_map/finish/pallas_call | solution.py:1586
  (33 shorter events, 2.1 us)
Async XLA Ops:
  0.6 187.9 %copy-start.4 = (bf16[128,768]{1,0:T(8,128)(2,1)S(1)}, bf16[128,768]{1,0:T(8,128)(2,1)}, u32[]{:S(2)}) copy-start(bf16[128,768]{1,0:T(8,128)(2,1)} %refs_11_.3) | copy-start | bytes 589828
  0.7 187.9 %copy-start = (bf16[128,2048]{1,0:T(8,128)(2,1)S(1)}, bf16[128,2048]{1,0:T(8,128)(2,1)}, u32[]{:S(2)}) copy-start(bf16[128,2048]{1,0:T(8,128)(2,1)} %refs_9_.1) | copy-start | bytes 1572868
  0.7 187.9 %copy-start.9 = (bf16[128,128]{1,0:T(8,128)(2,1)S(1)}, bf16[128,128]{1,0:T(8,128)(2,1)}, u32[]{:S(2)}) copy-start(bf16[128,128]{1,0:T(8,128)(2,1)} %refs_7_.3) | copy-start | bytes 98308
  0.7 187.9 %copy-start.7 = (bf16[128,384]{1,0:T(8,128)(2,1)S(1)}, bf16[128,384]{1,0:T(8,128)(2,1)}, u32[]{:S(2)}) copy-start(bf16[128,384]{1,0:T(8,128)(2,1)} %refs_6_.1) | copy-start | bytes 294916
  3.4 185.2 %copy-start.14 = (f32[2,128]{1,0:T(2,128)S(1)}, f32[2,128]{1,0:T(2,128)}, u32[]{:S(2)}) copy-start(f32[2,128]{1,0:T(2,128)} %maximum_convert_fusion.1.refs_9_.refs_8_) | copy-start | bytes 3076
  6.2 182.4 %copy-start.11 = (f32[16,128]{1,0:T(8,128)S(1)}, f32[16,128]{1,0:T(8,128)}, u32[]{:S(2)}) copy-start(f32[16,128]{1,0:T(8,128)} %pad_maximum_fusion.refs_6_.refs_5_) | copy-start | bytes 24580
  188.6 1.0 copy-start.1
  189.6 1.2 copy-start.2
  190.9 1.2 copy-start.3
  192.0 1.0 copy-start.5
  193.0 1.0 copy-start.6
  194.0 0.9 copy-start.8
  194.9 0.9 copy-start.10
  195.9 0.8 copy-start.12
  196.6 0.7 copy-start.13
  197.4 0.7 copy-start.15
  198.0 0.7 copy-start.16
  198.7 0.7 copy-start.17
  199.4 0.7 copy-start.18
  200.1 0.7 copy-start.19
  200.8 0.7 copy-start.20
  201.5 0.7 copy-start.21

commit v5 on v4

--- a/solution.py
+++ b/solution.py
@@ -97,15 +97,16 @@
         (),
         (),
         (),
-        (1, 2, 3),
-        (30, 11),
+        (),
+        (1, 2, 3, 30),
         (54, 27),
-        (10,),
-        (13, 57, 29, 81, 82, 5),
-        (56, 83, 86),
-        (87, 92, 93, 33, 100, 60, 84, 90, 85, 22, 39, 91, 17, 32, 59, 9, 35, 14, 88, 66, 89, 62, 45, 94, 103, 95, 104, 21, 47, 24, 41, 101, 38, 109, 68, 65, 102, 110, 72, 51, 18, 49, 71, 26, 44, 74),
-        (112, 115, 53, 114, 116, 78),
-        (76, 80),
+        (),
+        (11, 29, 57),
+        (),
+        (56,),
+        (13, 10, 5, 33, 60, 81, 85, 59, 39, 82, 86, 32, 22, 83, 84, 35, 17, 87, 95, 62, 45, 88, 96, 9, 47, 66, 93, 101, 65, 21, 94, 102, 38, 14, 41, 49, 72, 68, 24, 74, 71, 51, 18, 44, 76, 104, 107, 26, 106, 108, 78),
+        (53,),
+        (80,),
         (),
         (),
         (),
@@ -114,15 +115,16 @@
     (
         (),
         (),
-        (0, 1),
-        (2, 3),
-        (7,),
-        (30,),
-        (6, 28, 11),
-        (54, 27, 81, 10, 55, 82, 83, 29, 57, 86, 13, 5),
-        (31, 56, 87, 92),
-        (58, 93, 100, 84, 85, 96, 19, 36, 35, 98, 32, 62, 59, 88, 63, 33, 22, 89, 60, 39, 17, 14, 65, 38, 42, 94, 106, 66, 95, 108, 105, 69, 107, 47, 45, 101, 111, 24, 102, 113, 49, 112, 115, 114, 116),
-        (72, 74),
+        (),
+        (0, 1, 2, 3),
+        (30, 54, 27),
+        (28, 7, 57),
+        (),
+        (29,),
+        (55, 11, 6),
+        (56,),
+        (58, 13, 10, 5, 31, 33, 60, 59, 81, 89, 36, 82, 32, 91, 39, 83, 35, 84, 19, 62, 63, 22, 87, 97, 65, 17, 88, 99, 38, 42, 98, 66, 93, 103, 100, 45, 94, 105, 104, 107, 47, 106, 108, 69, 49, 14, 72, 24, 74),
+        (),
         (76,),
         (),
         (),
@@ -132,15 +134,16 @@
     (
         (),
         (),
-        (0, 1),
-        (2, 3),
-        (7,),
-        (),
-        (30, 6, 11, 29),
-        (54, 81, 27, 82, 56, 10, 83, 86, 57, 4),
-        (13, 28, 55, 87, 92, 32, 59),
-        (93, 100, 19, 84, 85, 39, 34, 31, 61, 58, 33, 22, 66, 88, 15, 89, 60, 97, 99, 12, 37, 36, 64, 45, 94, 63, 112, 95, 105, 114, 107, 72, 42, 46, 111, 115, 101, 106, 113, 116, 102, 23, 108, 48, 69),
-        (73,),
+        (),
+        (0, 1, 2, 3),
+        (30,),
+        (54, 27),
+        (),
+        (29, 7, 57),
+        (28,),
+        (56, 11, 6),
+        (55, 59, 13, 10, 4, 32, 33, 60, 58, 81, 39, 82, 31, 36, 83, 90, 34, 84, 92, 19, 87, 61, 22, 88, 64, 104, 15, 66, 106, 37, 93, 98, 45, 97, 94, 100, 99, 42, 63, 103, 107, 46, 105, 108, 72, 48, 12, 69, 23, 73),
+        (),
         (75,),
         (),
         (),
@@ -151,16 +154,17 @@
         (),
         (),
         (),
-        (0, 2, 3),
-        (30, 7, 54),
-        (27, 6),
-        (13, 57, 4),
-        (81, 28, 82, 83, 86, 55),
-        (87,),
-        (92, 60, 33, 93, 100, 19, 15, 84, 12, 85, 36, 31, 58, 8, 88, 34, 90, 89, 91, 63, 61, 42, 23, 94, 109, 20, 95, 110, 46, 40, 101, 103, 102, 64, 37, 104, 67, 69, 50, 48, 16, 73, 43, 25, 70, 52),
-        (111, 115, 77, 113, 75, 116),
-        (),
+        (),
+        (0, 2, 3, 30, 54, 27),
+        (28, 7, 57),
+        (),
+        (),
+        (13, 6, 55),
+        (),
+        (4, 33, 60, 81, 58, 36, 82, 31, 19, 83, 85, 84, 86, 34, 15, 63, 61, 42, 87, 101, 8, 46, 88, 102, 93, 95, 64, 94, 96, 20, 37, 12, 40, 69, 48, 67, 73, 23, 70, 16, 50, 43, 75, 103, 107, 25, 105, 108, 77),
+        (52,),
         (79,),
+        (),
         (),
         (),
         (),
@@ -169,87 +173,83 @@
 TAIL_PLAN = (
     (
         (),
-        (0, 1, 2, 4, 5, 8, 9, 11, 12, 16, 17, 21, 22, 25, 26, 28, 3),
-        (6,),
-        (7, 15),
-        (10,),
-        (122, 123),
-        (135, 13, 136, 38, 39, 40, 125, 42, 18, 43, 45, 46, 138, 49, 50, 14, 129, 55, 56, 60, 128, 61, 63, 142, 23, 64, 67, 27, 141),
-        (24, 131, 29, 31),
-        (41, 48, 144, 83, 84, 85, 87, 133, 88, 91, 92, 94, 95, 99, 100),
-        (104, 44, 105, 54, 108, 109, 146, 36, 111, 37, 30, 34, 47, 51),
-        (86, 57, 66, 62, 71, 89, 93, 65, 74, 96, 76, 78, 68, 77, 101, 106, 80),
-        (110,),
-        (),
-        (90, 98, 112),
-        (),
-        (82, 97, 107, 114, 113, 117),
-        (),
-        (119, 120),
+        (),
+        (),
+        (),
+        (),
+        (),
+        (),
+        (),
+        (),
+        (),
+        (),
+        (81, 94, 0, 3, 1, 7, 2, 4, 8, 13, 29, 84, 11, 17, 30, 97, 12, 20, 31, 87, 100, 14, 23, 33, 82, 32, 37, 95, 22, 88, 36, 40, 101, 26, 42, 41),
+        (90, 103, 46, 43, 92, 49, 58, 105),
+        (59, 60, 61, 52, 62, 64, 65, 63, 68, 51, 53, 69, 73, 70, 55, 24, 57, 71, 72, 76),
+        (),
+        (28, 78),
+        (79,),
     ),
     (
         (),
-        (0, 1, 2, 4, 5, 8, 9, 11, 12, 16, 17, 21, 22, 25, 26, 28, 3),
-        (6,),
-        (7,),
-        (10,),
-        (122, 123, 121),
-        (135, 136, 13, 134, 125, 38, 39, 40, 18, 42, 43, 45, 19, 138, 46, 49, 14, 50, 55, 129, 56, 60, 61, 126, 23, 63, 64, 142, 67, 27),
-        (29, 139),
-        (33, 41, 131, 83, 84, 85, 87, 88, 91, 24, 92, 144, 94, 32, 95, 99, 100, 44, 104, 105, 108, 109, 111, 52, 47, 30, 51),
-        (58, 86),
-        (35, 57, 89, 62, 36, 37, 69, 93, 70, 65, 96, 72, 68, 73, 101, 75, 106, 79),
-        (),
-        (90, 110),
-        (),
-        (),
-        (76, 112, 78, 97, 102, 107, 80, 113, 82),
-        (115, 118),
-        (116, 119, 120),
+        (),
+        (),
+        (),
+        (),
+        (),
+        (),
+        (),
+        (),
+        (),
+        (),
+        (80, 81, 93, 94, 0, 1, 2, 4, 8, 29, 84, 11, 30, 5, 97, 12, 31, 9, 14, 33, 16, 15, 82, 37, 19, 95, 18, 85, 40, 21, 88, 41, 98, 25),
+        (101, 22, 90, 43, 34, 26, 58, 103, 38),
+        (59, 60, 45, 61, 44, 48, 62, 50, 47, 65, 63, 68, 69, 70, 24, 54, 51, 53, 71, 66, 55, 72, 74),
+        (),
+        (57, 75, 77, 28),
+        (78, 79),
     ),
     (
         (),
-        (0, 1, 2, 4, 5, 8, 9, 11, 12, 16, 17, 21, 22, 25, 26, 28, 3),
-        (6,),
-        (7,),
-        (10,),
-        (121, 122, 123),
-        (134, 135, 136, 13, 38, 39, 40, 124, 42, 18, 43, 45, 46, 49, 14, 137, 50, 126, 55, 56, 60, 129, 23, 61, 63, 64, 67, 27, 139, 32, 20, 29),
-        (142,),
-        (41, 130),
-        (83, 84, 24, 143, 85, 87, 36, 88, 91, 92, 44, 94, 95, 99, 100, 104, 105, 108, 109, 35, 111, 37, 30, 47, 51, 86, 33),
-        (53, 69, 57, 89, 62, 72, 93, 59, 65, 96, 75, 76, 78, 68, 80, 101, 79, 106, 70),
-        (),
-        (90,),
-        (73, 110),
-        (),
-        (112, 82, 97, 107, 113),
-        (103, 119, 115, 116),
-        (118, 120),
+        (),
+        (),
+        (),
+        (),
+        (),
+        (),
+        (),
+        (),
+        (),
+        (),
+        (80, 81, 93, 94, 0, 1, 2, 4, 8, 29, 83, 11, 30, 96, 6, 12, 31, 10, 15, 14, 33, 22, 82, 18, 37, 95, 26, 21, 85, 40, 16, 88, 25, 41, 98, 19, 101, 43),
+        (89, 35, 102, 58, 39),
+        (59, 44, 60, 61, 47, 45, 62, 51, 48, 65, 63, 68, 69, 50, 53, 70, 24, 55, 54, 71, 67, 57, 78),
+        (),
+        (72, 74, 28, 77, 79, 75),
+        (),
     ),
     (
         (),
-        (0, 1, 2, 4, 5, 8, 9, 11, 12, 16, 17, 21, 22, 25, 26, 28, 3),
-        (6,),
-        (7,),
-        (10,),
-        (),
-        (121, 123, 134, 13, 136, 38, 39, 40, 124, 42, 18, 43, 45, 46, 49, 137, 50, 55, 126, 56, 14, 15, 60, 61, 63, 127, 139, 64, 23, 67, 140, 27),
-        (130, 29),
-        (24, 34, 143, 41, 35, 83, 84, 37, 85, 87, 132, 88, 91, 92, 94, 95, 99),
-        (100, 104, 44, 105, 145, 108, 109, 111, 30, 47, 31, 48, 51, 54),
-        (86, 57, 74, 62, 89, 77, 75, 78, 93, 65, 66, 96, 79, 68, 71, 101, 106),
-        (),
-        (),
-        (110,),
-        (),
-        (112, 90, 82, 97, 98, 107, 117, 113, 114),
-        (118, 120),
+        (),
+        (),
+        (),
+        (),
+        (),
+        (),
+        (),
+        (),
+        (),
+        (),
+        (80, 93, 0, 1, 2, 3, 4, 7, 8, 20, 29, 83, 11, 30, 23, 96, 12, 31, 86, 13, 99, 14, 33, 17, 82, 37, 32, 95, 21, 85, 40, 36, 25, 98, 41),
+        (89, 42, 102, 43, 46, 91, 58, 49, 104),
+        (59, 60, 61, 62, 52, 65, 63, 64, 68, 50, 53, 69, 76, 70, 24, 54, 57, 71, 72, 73),
+        (),
+        (28, 77, 79),
         (),
     ),
 )
 FIRST_PARTS = (0,)
-SUM_ORDERS = ('xyz', 'yzx', 'yxz')
+SUM_ORDERS = ('yxz', 'yzx', 'xzy')
 ORDERS = ("zxy", "xzy", "yzx")
 
 
@@ -286,11 +286,11 @@
 def tell_peers(barrier):
     band, y = lax.axis_index("band"), lax.axis_index("dp")
     bands = lax.axis_size("band")
-    for step in range(1, bands):
-        pl.semaphore_signal(
-            barrier, inc=1, device_id=((band + step) % bands, y), device_id_type=MESH
-        )
-    pl.semaphore_signal(barrier, inc=1, device_id=(band, 1 - y), device_id_type=MESH)
+    for step in range(bands):
+        for plane in (y, 1 - y) if step else (1 - y,):
+            pl.semaphore_signal(
+                barrier, inc=1, device_id=((band + step) % bands, plane), device_id_type=MESH
+            )
 
 
 def tell_near(semaphore):
@@ -499,48 +499,25 @@
 
 
 class Reduce:
-    def __init__(
-        self, known_z, parts, view, orders, final, pair_view, pair_buf, buf, bulk, pair_bulk, pair_send, pair_recv, send, recv
-    ):
-        self.parts, self.bulk, self.pair_bulk = parts, bulk, pair_bulk
+    def __init__(self, known_z, view, orders, final, buf, bulk, send, recv):
         self.view, self.orders, self.final = view, orders, final
-        self.pair_view, self.pair_buf, self.buf = pair_view, pair_buf, buf
-        self.pair_send, self.pair_recv = pair_send, pair_recv
+        self.buf, self.bulk = buf, bulk
         self.send_sem, self.recv_sem = send, recv
         self.z, self.x, self.core, self.y = place(known_z)
         self.index = [self.places(chunk) for chunk in range(len(orders))]
 
-    def rail(self, block):
-        if "y" not in self.orders[0]:
-            return block[0] * 2 + block[1]
-        return block[0] * 4 + block[1] * 2 + block[2]
-
     def coords(self, block):
         zz, flip_x, flip_y = block
         return (zz, 1 - self.x if flip_x else self.x, 1 - self.y if flip_y else self.y)
 
     def own(self, chunk, block):
-        return self.view(chunk, self.coords(block), self.core)
+        return self.view(chunk, self.coords(block))
 
     def add(self, target, source):
         target[...] = target[...] + source[...]
 
     def sibling(self):
         return device(self.z, self.x, 1 - self.core, self.y)
-
-    def pair_copy(self, part, block):
-        return pltpu.make_async_remote_copy(
-            src_ref=self.pair_view(part, block, 1 - self.core),
-            dst_ref=self.pair_buf(part, self.rail(block)),
-            send_sem=self.pair_send.at[part, block[0] // 2],
-            recv_sem=self.pair_recv.at[part, self.rail(block)],
-            device_id=self.sibling(),
-            device_id_type=MESH,
-        )
-
-    def pair_start(self, part, blocks=None):
-        for block in blocks or self.blocks():
-            self.pair_copy(part, self.coords(block)).start()
 
     def blocks(self):
         return [(zz, fx, fy) for zz in (3, 0, 2, 1) for fx, fy in self.flips(0, 0)]
@@ -667,30 +644,13 @@
             final = self.final(chunk)
             final[...] = own[...].astype(F32) + landed[...].astype(F32)
 
-    def pair_arrive(self, part, block, chunks):
-        where = self.coords(block)
-        landed = self.pair_buf(part, self.rail(where))
-        pltpu.make_async_remote_copy(
-            src_ref=landed,
-            dst_ref=landed,
-            send_sem=self.pair_send.at[part, 0],
-            recv_sem=self.pair_recv.at[part, self.rail(where)],
-            device_id=self.sibling(),
-            device_id_type=MESH,
-        ).wait_recv()
-        self.add(self.pair_view(part, where, self.core), landed)
+    def start(self, chunk, block):
+        self.ready(chunk, 0, block)
+
+    def events(self, chunks, start=0.0, pace=1.0):
+        found = []
         for chunk in chunks:
-            self.ready(chunk, 0, block)
-
-    def events(self, part, chunks, start=0.0, pace=1.0, pair_pace=0.5):
-        found, ready = [], {}
-        clock = start
-        for block in self.blocks():
-            clock += pair_pace
-            found.append((clock, 0, functools.partial(self.pair_arrive, part, block, chunks)))
-            ready[block] = clock
-        for chunk in chunks:
-            times = dict(ready)
+            times = {block: start for block in self.blocks()}
             for stage, dim in enumerate(self.orders[chunk]):
                 clock, later = 0.0, {}
                 if dim == "z":
@@ -720,17 +680,12 @@
         return found
 
     def finish(self):
-        rails = len(self.blocks())
         for chunk, order in enumerate(self.orders):
             for stage, dim in enumerate(order):
                 after = len(self.flips(chunk, stage + 1)) if stage + 1 < len(order) else 1
                 count = 3 * after if dim == "z" else after * (4 if "z" in order[stage + 1 :] else 1)
                 every = self.bulk(chunk, count)
                 bulk_copy(every, self.send_sem.at[chunk, stage], self.recv_sem.at[chunk, 0]).wait_send()
-        for part in range(self.parts):
-            every = self.pair_bulk(part, rails // 2)
-            for side in (0, 1):
-                bulk_copy(every, self.pair_send.at[part, side], self.pair_recv.at[part, 0]).wait_send()
 
 
 class Exchange:
@@ -784,6 +739,7 @@
         self.weights, self.down = weights, down
         self.__dict__.update(refs)
         self.width = weights.shape[1]
+        self.tokens = self.joint.shape[1]
         self.halves = weights.shape[1] // (2 * HEAD_DIM)
 
     def weight(self, part):
@@ -798,16 +754,18 @@
     def pair_rows(self, rows, low, high):
         return jnp.concatenate([rows * low, rows * high], axis=0)
 
+    def own(self, ref):
+        return ref[: self.tokens]
+
     def project(self):
         unit, inverse = unit_parts(self.residual[...])
-        normed = (unit * self.gain_one[...]).astype(B16)
-        self.normed_one[...] = normed
+        self.normed_one[: self.tokens] = (unit * self.gain_one[...]).astype(B16)
         self.unit_one[...] = unit
         self.inverse_one[...] = jnp.broadcast_to(inverse, self.inverse_one.shape)
 
         @pl.loop(0, 3)
         def _(part):
-            self.joint[part] = dot_nn(self.normed_one[...], self.weight(part)).astype(B16)
+            self.joint[part] = dot_nn(self.own(self.normed_one), self.weight(part)).astype(B16)
 
     def attend(self):
         tokens = self.joint.shape[1]
@@ -823,58 +781,68 @@
             probs = raised / jnp.sum(raised, axis=-1, keepdims=True)
             self.probs[pair] = probs
             mixed = dot_nn(probs.astype(B16), value)
-            self.mixed[:, lanes] = jnp.where(where, mixed[:tokens], mixed[tokens:]).astype(B16)
+            self.mixed[:tokens, lanes] = jnp.where(where, mixed[:tokens], mixed[tokens:]).astype(B16)
 
     def widen(self):
-        middle = self.residual[...] + dot_nn(self.mixed[...], self.weight(3))
+        middle = self.residual[...] + dot_nn(self.own(self.mixed), self.weight(3))
         unit, inverse = unit_parts(middle)
-        self.normed_two[...] = (unit * self.gain_two[...]).astype(B16)
+        self.normed_two[: self.tokens] = (unit * self.gain_two[...]).astype(B16)
         self.unit_two[...] = unit
         self.inverse_two[...] = jnp.broadcast_to(inverse, self.inverse_two.shape)
         self.result[...] = middle
 
         @pl.loop(0, 4)
         def _(part):
-            pre = dot_nn(self.normed_two[...], self.weight(4 + part))
+            pre = dot_nn(self.own(self.normed_two), self.weight(4 + part))
             self.pre_act[part] = pre
-            self.act[part] = gelu_tanh(pre).astype(B16)
+            self.act[part, : self.tokens] = gelu_tanh(pre).astype(B16)
 
     def narrow(self):
         @pl.loop(0, 4)
         def _(part):
             rows = pl.ds(aligned(part * self.width), self.width)
-            self.result[...] += dot_nn(self.act[part], self.down[rows, :])
+            self.result[...] += dot_nn(self.act[part, : self.tokens], self.down[rows, :])
 
         self.block_out[...] = self.result[...].astype(B16)
 
-    def back_narrow(self, part):
-        rows = pl.ds(aligned(part * self.width), self.width)
-        grad_act = dot_nt(self.out_grad[...], self.down[rows, :])
-        grad_pre = (grad_act * gelu_slope(self.pre_act[part])).astype(B16)
-        self.grad_pre[part] = grad_pre
-        self.grad_normed[...] += dot_nt(grad_pre, self.weight(4 + part))
-
-    def down_grad(self, part, store):
-        turned = self.act[part].T
-        for at in range(0, self.width, 256):
-            store[pl.ds(aligned(part * self.width), self.width), at : at + 256] = dot_nn(
-                turned, self.out_grad[:, at : at + 256]
-            ).astype(B16)
-
-    def pair_grad(self, first, second, first_grad, second_grad, store, offset):
+    def back_narrow(self):
+        self.grad_normed[...] = jnp.zeros(self.grad_normed.shape, F32)
+
         @pl.loop(0, 4)
-        def _(group):
-            rows = pl.ds(aligned(group * 192), 192)
+        def _(part):
+            rows = pl.ds(aligned(part * self.width), self.width)
+            grad_act = dot_nt(self.own(self.out_grad), self.down[rows, :])
+            grad_pre = (grad_act * gelu_slope(self.pre_act[part])).astype(B16)
+            self.grad_pre[part, : self.tokens] = grad_pre
+            self.grad_normed[...] += dot_nt(grad_pre, self.weight(4 + part))
+
+    def down_grad(self, part, core, store):
+        self.turned[...] = self.act[part].T
+        for x in (0, 1):
+            rows = self.turned[pl.ds(aligned((x * 2 + core) * 2 * PART), 2 * PART), :]
             for at in range(0, self.width, 256):
                 cols = slice(at, at + 256)
-                one = dot_nn(first[rows, :], first_grad(cols))
-                two = dot_nn(second[rows, :], second_grad(cols))
-                for owner in range(8):
-                    piece = jnp.concatenate(
-                        [one[owner * 24 : owner * 24 + 24], two[owner * 24 : owner * 24 + 24]], axis=0
-                    )
-                    target = aligned((group * 8 + owner) * PART + offset)
-                    store[pl.ds(target, CHUNK), cols] = piece.astype(B16)
+                store[(part * 4 + x * 2) * PART : (part * 4 + x * 2 + 2) * PART, cols] = dot_nn(
+                    rows, self.out_grad[:, cols]
+                ).astype(B16)
+
+    def turn_rail(self, which, ref, core):
+        self.turned[...] = ref[...].T
+        for chip in range(8):
+            self.rail_rows[which, chip * CHUNK : (chip + 1) * CHUNK, :] = self.turned[
+                pl.ds(aligned((chip * 2 + core) * CHUNK), CHUNK), :
+            ]
+
+    def pair_grad(self, first, second, first_grad, second_grad, store, offset):
+        half = CHUNK // 2
+        for at in range(0, self.width, 256):
+            cols = slice(at, at + 256)
+            one = dot_nn(self.rail_rows[first], first_grad(cols))
+            two = dot_nn(self.rail_rows[second], second_grad(cols))
+            for owner in range(16):
+                rows = slice(owner * half, owner * half + half)
+                piece = jnp.concatenate([one[rows], two[rows]], axis=0)
+                store[owner * PART + offset : owner * PART + offset + CHUNK, cols] = piece.astype(B16)
 
     def back_wide(self):
         grad_normed = self.grad_normed[...]
@@ -886,12 +854,11 @@
             - jnp.mean(scaled, axis=-1, keepdims=True)
             - unit * jnp.mean(scaled * unit, axis=-1, keepdims=True)
         )
-        grad_middle = self.out_grad[...].astype(F32) + back
+        grad_middle = self.own(self.out_grad).astype(F32) + back
         self.grad_middle[...] = grad_middle
         branch = grad_middle.astype(B16)
-        self.grad_branch[...] = branch
+        self.grad_branch[: self.tokens] = branch
         self.grad_mixed[...] = dot_nt(branch, self.weight(3)).astype(B16)
-        self.turned_mixed[...] = self.mixed[...].T
 
     def back_attend(self):
         tokens = self.joint.shape[1]
@@ -904,23 +871,23 @@
             query, key, value = (self.joint[part, :, lanes] for part in range(3))
             grads = self.pair_rows(self.grad_mixed[:, lanes], low, high)
             probs = self.probs[pair]
-            self.grad_joint[2, :, lanes] = dot_tn(probs.astype(B16), grads).astype(B16)
+            self.grad_joint[2, :tokens, lanes] = dot_tn(probs.astype(B16), grads).astype(B16)
             grad_probs = dot_nt(grads, value)
             total = jnp.sum(grad_probs * probs, axis=-1, keepdims=True)
             grad_scores = (probs * (grad_probs - total)).astype(B16)
             queries = dot_nn(grad_scores, key) * scale
-            self.grad_joint[0, :, lanes] = jnp.where(
+            self.grad_joint[0, :tokens, lanes] = jnp.where(
                 where, queries[:tokens], queries[tokens:]
             ).astype(B16)
             keys = dot_tn(grad_scores, self.pair_rows(query, low, high)) * scale
-            self.grad_joint[1, :, lanes] = keys.astype(B16)
+            self.grad_joint[1, :tokens, lanes] = keys.astype(B16)
 
     def back_project(self):
         self.grad_normed[...] = jnp.zeros(self.grad_normed.shape, F32)
 
         @pl.loop(0, 3)
         def _(part):
-            self.grad_normed[...] += dot_nt(self.grad_joint[part], self.weight(part))
+            self.grad_normed[...] += dot_nt(self.grad_joint[part, : self.tokens], self.weight(part))
 
         grad_normed = self.grad_normed[...]
         unit = self.unit_one[...]
@@ -1070,31 +1037,53 @@
     return ref.at[pl.ds(aligned(index * 16), 16)]
 
 
-KEPT = ("joint", "soft", "mixed", "unit_one", "inverse_one", "inner", "unit_two", "inverse_two")
+KEPT = ("joint", "soft", "mixed", "unit_one", "inverse_one", "inner", "unit_two", "inverse_two", "gains")
+SHARED = ("out_grad", "normed_one", "mixed", "normed_two", "act0", "act1", "act2", "act3")
+SHARED += ("pre0", "pre1", "pre2", "pre3", "grad_branch", "joint0", "joint1", "joint2")
 
 
 def layer_kernel(*refs):
-    (pixels, kernel_gen, attn_qkv, attn_out, mlp_up, mlp_down, waves, hyper_qkv, hyper_out, hyper_gains, hyper_up, hyper_down,
-     bias_gen, band_scale, out_grad, gains,
+    (counts, mask, pixels, kernel_gen, attn_qkv, attn_out, mlp_up, mlp_down, waves, hyper_qkv, hyper_out, hyper_one, hyper_two,
+     hyper_up, hyper_down, bias_gen, out_grad_in, norm_one, norm_two,
      block_out, pixel_out, shares, kernel_grads, code_out, code_grads, vectors, *rest_refs) = refs
     kept_refs, rest_refs = rest_refs[: len(KEPT)], rest_refs[len(KEPT) :]
-    (gathered, weights, spare, pair_buf, buf, joint, probs, pre_act, act, grad_pre, mixed, normed_one, normed_two,
+    (gathered, weights, spare, buf, joint, probs, pre_act, act, grad_pre, out_grad, mixed, normed_one, normed_two,
      unit_one, unit_two, inverse_one, inverse_two, grad_normed, grad_middle, grad_branch, grad_mixed, grad_joint,
-     turned_mixed, turned_one, residual, pixel_rows, turned_pixels, mixing, kernels, sending,
-     partner_grads, landed_grads, small, small_partner, small_all, code_part, code_all,
+     turned, rail_rows, residual, pixel_rows, turned_pixels, pair_pixels, mixing, kernels, pair_kernels, sending,
+     landed_grads, summed, small, small_partner, small_all, code_part, code_all, gains, band_scale, pair_scale,
      pix_sem, gen_sem, front_done, narrow_done, *sems) = rest_refs
     z, x, core, y = place()
     band = lax.axis_index("band")
     bands = lax.axis_size("band")
     me = slot(z, x, core, y)
     width = gains.shape[1]
-    tokens = out_grad.shape[0]
+    tokens = out_grad_in.shape[0]
+    sibling = (band + 1 - 2 * core, y)
     partner = (band, 1 - y)
     own_rows = pl.ds(aligned(band * 16), 16)
-    gather_sems, reduce_sems, embed_sems, grads_sems = (sems[at : at + 4] for at in (0, 4, 8, 12))
-    kernel_sems, cols_sems, vec_sems, code_sems, half_sems, vec_half_sems = (
-        sems[at : at + 2] for at in (16, 18, 20, 22, 24, 26)
-    )
+    gather_sems, grads_sems = sems[0:4], sems[4:8]
+    reduce_sems, embed_sems, share_sems, front_sems, kernel_sems, cols_sems, summed_sems, vec_half_sems, vec_sems, code_sems = (
+        sems[at : at + 2] for at in range(8, 28, 2)
+    )
+
+    def to_pair(index, source, target, pair=share_sems):
+        return pltpu.make_async_remote_copy(
+            src_ref=source,
+            dst_ref=target,
+            send_sem=pair[0].at[index],
+            recv_sem=pair[1].at[index],
+            device_id=sibling,
+            device_id_type=MESH,
+        )
+
+    def shared(name):
+        index = SHARED.index(name)
+        ref = dict(
+            out_grad=out_grad, normed_one=normed_one, mixed=mixed, normed_two=normed_two, grad_branch=grad_branch
+        ).get(name)
+        if ref is None:
+            ref = dict(act=act, pre=grad_pre, joint=grad_joint)[name[:-1]].at[int(name[-1])]
+        return to_pair(index, ref.at[pl.ds(0, tokens)], ref.at[pl.ds(tokens, tokens)])
 
     def gen_copy(piece, target):
         return pltpu.make_async_copy(
@@ -1112,6 +1101,14 @@
     load_pixels = pltpu.make_async_copy(pixels, pixel_rows, pix_sem)
     load_pixels.start()
 
+    gains[0:1, :] = norm_one[...].astype(F32).reshape(1, width)
+    gains[1:2, :] = norm_two[...].astype(F32).reshape(1, width)
+    out_grad[0:tokens, :] = out_grad_in[...]
+    for image in range(band_scale.shape[0]):
+        used = jnp.where((band < counts[image]) & (mask[image] == 1), 1.0, 0.0)
+        bands_here = jnp.full(band_scale.shape[1:], counts[image], jnp.int32).astype(F32)
+        band_scale[image] = lax.rsqrt(bands_here) * used
+
     def rows_of(weight, piece):
         return weight[:, piece * width : (piece + 1) * width].astype(F32)
 
@@ -1121,9 +1118,11 @@
         rows = jnp.concatenate(pieces[2 * at : 2 * at + 2], axis=0).astype(B16)
         gathered[at // 2, pl.ds(aligned(me * PART + at % 2 * CHUNK), CHUNK), :] = rows
     gathered[2, pl.ds(aligned(me * PART), PART), :] = mlp_down[...]
+    hyper_gains = [gain[...].astype(F32).reshape(1, HW) for gain in (hyper_one, hyper_two)]
     code, kept = hyper_forward(
-        waves[...], hyper_qkv[...], hyper_out[...], hyper_gains[0:1, :], hyper_up[...], hyper_down[...], hyper_gains[1:2, :]
-    )
+        waves[...], hyper_qkv[...], hyper_out[...], hyper_gains[0], hyper_up[...], hyper_down[...], hyper_gains[1]
+    )
+    kept = (*kept, jnp.concatenate(hyper_gains, axis=0))
     code_low = code.astype(B16)
     code_out[...] = code_low
     for ref, value in zip(kept_refs, kept):
@@ -1138,6 +1137,9 @@
     def image_row(block, side):
         return (block[0] * 4 + block[1] * 2 + side) * tokens
 
+    def rail_row(block):
+        return (block[0] * 2 + block[1]) * tokens
+
     def gather_at(known_z=None):
         return Gather(
             known_z, weight_view, ORDERS, lambda part, count: gathered.at[part, pl.ds(0, count * PART)], *gather_sems
@@ -1146,26 +1148,27 @@
     def embed_at(known_z=None):
         return Reduce(
             known_z,
-            1,
-            lambda chunk, block, side: spare.at[pl.ds(aligned(image_row(block, side) + chunk * half), half)],
+            lambda chunk, block: spare.at[pl.ds(aligned(rail_row(block) + chunk * half), half)],
             ("xz", "xz"),
             lambda chunk: residual.at[pl.ds(chunk * half, half)],
-            lambda part, block, side: spare.at[pl.ds(aligned(image_row(block, side)), tokens)],
-            lambda part, rail: pair_buf.at[0, pl.ds(aligned(rail * tokens), tokens)],
-            lambda chunk, where: pair_buf.at[1, pl.ds((chunk * 9 + where) * half, half)],
-            lambda chunk, count: pair_buf.at[1, pl.ds(0, count * half)],
-            lambda part, count: pair_buf.at[0, pl.ds(0, count * tokens)],
+            lambda chunk, where: buf.at[pl.ds((chunk * 9 + where) * half, half)],
+            lambda chunk, count: buf.at[pl.ds(0, count * half)],
             *embed_sems,
         )
 
     def front_works(known_z):
         known, sums = gather_at(known_z), embed_at(known_z)
         works = [work for part in range(3) for work in in_order(known.events(part))]
-        return works + in_order(sums.events(0, (0, 1)))
+        return works + in_order(sums.events((0, 1)))
 
     gather, embed = gather_at(), embed_at()
     plan = Plan(FRONT_PLAN, [front_works(known_z) for known_z in range(4)])
-    pl.semaphore_wait(barrier, bands)
+    pl.semaphore_wait(barrier, 2 * bands - 1)
+    load_pixels.wait()
+    for chip in range(8):
+        to_pair(0, pixel_rows.at[chip * 2 + 1 - core], pair_pixels.at[chip], front_sems).start()
+    to_pair(1, band_scale, pair_scale, front_sems).start()
+    shared("out_grad").start()
     plan.run()
     for part in FIRST_PARTS:
         gather.start(part)
@@ -1193,27 +1196,39 @@
     plan.run()
     kernels[own_rows, :] = sending[own_rows, :]
     biases = dot_nn(code_out[...], bias_gen[...])
-    chosen = lax.broadcasted_iota(jnp.int32, biases.shape, 0) == band
-    bias = jnp.sum(jnp.where(chosen, biases, 0.0), axis=0, keepdims=True)
-    load_pixels.wait()
+    row = lax.broadcasted_iota(jnp.int32, biases.shape, 0)
+    bias, pair_bias = (
+        jnp.sum(jnp.where(row == of, biases, 0.0), axis=0, keepdims=True) for of in (band, sibling[0])
+    )
     for group in range(4):
         turned_pixels[group] = pixel_rows[4 * group : 4 * group + 4].reshape(4 * tokens, -1).T
     plan.run()
     spread_kernels.wait()
+    to_pair(2, kernels, pair_kernels, front_sems).start()
+    plan.run()
+    to_pair(0, pair_pixels, pair_pixels, front_sems).wait_recv()
+    to_pair(1, band_scale, pair_scale, front_sems).wait_recv()
+    to_pair(2, kernels, pair_kernels, front_sems).wait_recv()
 
     def term(group):
-        rows = pixel_rows[4 * group : 4 * group + 4].reshape(4 * tokens, -1)
+        mine = [group * 4 + x_of * 2 + core for x_of in (0, 1)]
+        rows = jnp.concatenate([pixel_rows[image] for image in mine], axis=0)
+        pair_rows = pair_pixels[2 * group : 2 * group + 2].reshape(2 * tokens, -1)
         for at in range(0, width, 256):
-            terms = dot_nn(rows, kernels[:, at : at + 256]) + bias[:, at : at + 256]
-            for image in range(4):
-                scale = band_scale[group * 4 + image][:1, :1]
-                target = pl.ds((group * 4 + image) * tokens, tokens)
-                spare[target, at : at + 256] = (terms[image * tokens : (image + 1) * tokens] * scale).astype(B16)
+            cols = slice(at, at + 256)
+            one = dot_nn(rows, kernels[:, cols]) + bias[:, cols]
+            two = dot_nn(pair_rows, pair_kernels[:, cols]) + pair_bias[:, cols]
+            for x_of, image in enumerate(mine):
+                own = slice(x_of * tokens, (x_of + 1) * tokens)
+                total = one[own] * band_scale[image][:1, :1] + two[own] * pair_scale[image][:1, :1]
+                start = (2 * group + x_of) * tokens
+                spare[start : start + tokens, cols] = total.astype(B16)
 
     for group in (3, 0, 2, 1):
         plan.run()
         term(group)
-        embed.pair_start(0, [(group, 1, 0), (group, 0, 0)])
+        for chunk in (0, 1):
+            embed.start(chunk, (group, 1, 0))
     plan.run()
     gather.wait_pairs(0)
     spread(gathered, weights, 0)
@@ -1224,46 +1239,51 @@
         grad_pre=grad_pre, mixed=mixed, normed_one=normed_one, normed_two=normed_two, unit_one=unit_one,
         unit_two=unit_two, inverse_one=inverse_one, inverse_two=inverse_two, result=residual, grad_normed=grad_normed,
         grad_middle=grad_middle, grad_branch=grad_branch, grad_mixed=grad_mixed, grad_joint=grad_joint,
-        turned_mixed=turned_mixed, small=small,
+        turned=turned, rail_rows=rail_rows, small=small,
     )
     block = Block(weights, gathered.at[2], names)
     plan.run()
     block.project()
+    shared("normed_one").start()
     plan.run()
     block.attend()
+    shared("mixed").start()
     plan.run()
     gather.wait_pairs(1)
     spread(gathered, weights, 1)
     plan.run()
     block.widen()
+    for name in ("normed_two", "act0", "act1", "act2", "act3"):
+        shared(name).start()
     plan.run()
     gather.wait_pairs(2)
     gather.finish()
     embed.finish()
+    for copy in ((0, pair_pixels, pair_pixels), (1, band_scale, pair_scale), (2, kernels, pair_kernels)):
+        to_pair(*copy, front_sems).wait_send()
     tell_near(front_done)
-    block.narrow()
-    plan.run()
 
     def part_ref(part):
         return spare if part == 2 else gathered.at[part]
 
-    def part_view(part, blk, side):
-        return part_ref(part).at[pl.ds(aligned(slot(blk[0], blk[1], side, blk[2]) * PART), PART)]
+    def part_view(part, blk):
+        return part_ref(part).at[pl.ds(aligned((blk[0] * 4 + blk[1] * 2 + blk[2]) * PART), PART)]
 
     def reduce_at(known_z=None):
         return Reduce(
             known_z,
-            3,
             part_view,
             SUM_ORDERS,
             lambda part: shares.at[pl.ds(part * PART, PART)],
-            part_view,
-            lambda part, rail: pair_buf.at[part, pl.ds(aligned(rail * PART), PART)],
-            lambda part, where: buf.at[part, where],
-            lambda part, count: part_ref(part).at[pl.ds(0, count * PART)],
+            lambda part, where: buf.at[pl.ds((part * 19 + where) * PART, PART)],
             lambda part, count: part_ref(part).at[pl.ds(0, count * PART)],
             *reduce_sems,
         )
+
+    def send_terms(part, planes):
+        for zz in planes:
+            for flips in reduce.flips(part, 0):
+                reduce.start(part, (zz, *flips))
 
     image_grads = gathered.at[2]
 
@@ -1277,52 +1297,60 @@
 
     def tail_works(known_z):
         known, images = reduce_at(known_z), grads_at(known_z)
-        works = [work for part in (2, 1, 0) for work in in_order(known.events(part, (part,)))]
+        works = [work for part in (2, 1, 0) for work in in_order(known.events((part,)))]
         return works + [work for chunk in (0, 1) for work in in_order(images.events(chunk))]
 
     reduce, grads = reduce_at(), grads_at()
     plan = Plan(TAIL_PLAN, [tail_works(known_z) for known_z in range(4)])
-    grad_normed[...] = jnp.zeros(grad_normed.shape, F32)
     hear_near(front_done)
-    plan.run()
-
-    @pl.loop(0, 4)
-    def _(step):
-        odd = step % 2
-        zz = (1 - odd) * (3 - step // 2) + odd * (step // 2)
-        block.back_narrow(zz)
-        block.down_grad(zz, spare)
-        reduce.pair_start(2, [(zz, fx, fy) for fx, fy in ((1, 1), (1, 0), (0, 1), (0, 0))])
-
+    shared("out_grad").wait_recv()
+    for part in (3, 0, 2, 1):
+        plan.run()
+        shared(f"act{part}").wait_recv()
+        block.down_grad(part, core, spare)
+        send_terms(2, (part,))
+    plan.run()
+    block.back_narrow()
+    for part in range(4):
+        shared(f"pre{part}").start()
+    plan.run()
+    block.narrow()
     tell_near(narrow_done)
     plan.run()
     block.back_wide()
+    shared("grad_branch").start()
     plan.run()
     block.back_attend()
+    for part in range(3):
+        shared(f"joint{part}").start()
     plan.run()
     block.back_project()
     hear_near(narrow_done)
     image_grads[pl.ds(aligned(band * tokens), tokens), :] = block.embed_grad()
     grads.start(0)
     grads.start(1)
-    turned_one[...] = normed_two[...].T
+    plan.run()
+    for name in ("normed_two", "pre0", "pre1", "pre2", "pre3"):
+        shared(name).wait_recv()
+    block.turn_rail(0, normed_two, core)
     for part in (0, 2):
-        plan.run()
         block.pair_grad(
-            turned_one, turned_one, lambda cols, part=part: grad_pre[part, :, cols],
+            0, 0, lambda cols, part=part: grad_pre[part, :, cols],
             lambda cols, part=part: grad_pre[part + 1, :, cols], part_ref(1), part // 2 * CHUNK,
         )
-    reduce.pair_start(1)
-    plan.run()
-    turned_one[...] = normed_one[...].T
+    send_terms(1, (3, 0, 2, 1))
+    plan.run()
+    for name in ("normed_one", "mixed", "grad_branch", "joint0", "joint1", "joint2"):
+        shared(name).wait_recv()
+    block.turn_rail(0, normed_one, core)
+    block.turn_rail(1, mixed, core)
+    block.pair_grad(0, 0, lambda cols: grad_joint[0, :, cols], lambda cols: grad_joint[1, :, cols], part_ref(0), 0)
     block.pair_grad(
-        turned_one, turned_one, lambda cols: grad_joint[0, :, cols], lambda cols: grad_joint[1, :, cols], part_ref(0), 0
-    )
-    plan.run()
-    block.pair_grad(
-        turned_one, turned_mixed, lambda cols: grad_joint[2, :, cols], lambda cols: grad_branch[:, cols], part_ref(0), CHUNK
-    )
-    reduce.pair_start(0)
+        0, 1, lambda cols: grad_joint[2, :, cols], lambda cols: grad_branch[:, cols], part_ref(0), CHUNK
+    )
+    send_terms(0, (3, 0, 2, 1))
+    for name in SHARED:
+        shared(name).wait_send()
     for piece in range(16):
         gen_copy(piece, weights).start()
 
@@ -1342,8 +1370,8 @@
                 rows = pl.ds(aligned((group * 4 + image) * tokens), tokens)
                 scaled = image_grads[rows, :].astype(F32) * band_scale[group * 4 + image][:1, :1]
                 small[2:3, :] += jnp.sum(scaled, axis=0, keepdims=True)
-                act[image] = scaled.astype(B16)
-            scaled = act[...].reshape(4 * tokens, width)
+                act[image, :tokens] = scaled.astype(B16)
+            scaled = act[:, :tokens].reshape(4 * tokens, width)
             pixel_rows[pl.ds(group * 4, 4)] = dot_nt(scaled, kernels[...]).astype(B16).reshape(4, tokens, -1)
             kernel_total[...] += dot_nn(turned_pixels[group], scaled).reshape(kernel_total.shape)
 
@@ -1351,41 +1379,35 @@
     store_pixels.start()
     spread_kernels.finish()
     sending[...] = kernel_total[...].astype(B16).reshape(sending.shape)
-    quarter = sending.shape[0] // 4
-
-    def half_copy(piece):
-        rows = pl.ds(piece * quarter, quarter)
+    owner = core == y
+
+    def column_copy(target, plane):
         return pltpu.make_async_remote_copy(
-            src_ref=sending.at[rows], dst_ref=partner_grads.at[rows], send_sem=half_sems[0].at[piece],
-            recv_sem=half_sems[1].at[piece], device_id=partner, device_id_type=MESH,
+            src_ref=rows16(sending, target),
+            dst_ref=rows16(landed_grads, y * bands + band),
+            send_sem=cols_sems[0].at[0],
+            recv_sem=cols_sems[1].at[0],
+            device_id=(target, plane),
+            device_id_type=MESH,
         )
 
-    for piece in range(4):
-        half_copy(piece).start()
+    for step in range(1, bands):
+        target = (band + step) % bands
+        column_copy(target, target % 2).start()
+
+    @pl.when(core != y)
+    def _():
+        column_copy(band, 1 - y).start()
+
+    @pl.when(owner)
+    def _():
+        landed_grads[pl.ds(aligned((y * bands + band) * 16), 16), :] = sending[own_rows, :]
+
     vec_half = pltpu.make_async_remote_copy(
         src_ref=small, dst_ref=small_partner, send_sem=vec_half_sems[0].at[0], recv_sem=vec_half_sems[1].at[0],
         device_id=partner, device_id_type=MESH,
     )
     vec_half.start()
-    columns = Exchange(
-        lambda target: rows16(mixing, target),
-        lambda source: rows16(landed_grads, source),
-        lambda count: landed_grads.at[pl.ds(0, count * 16)],
-        *[sem.at[0] for sem in cols_sems],
-    )
-    for piece in range(4):
-        plan.run()
-        half_copy(piece).wait_recv()
-        rows = pl.ds(piece * quarter, quarter)
-        mixing[rows, :] = sending[rows, :] + partner_grads[rows, :]
-        for near in range(4):
-            target = piece * 4 + near
-
-            @pl.when(target != band)
-            def _(target=target):
-                columns.send(target)
-
-    landed_grads[own_rows, :] = mixing[own_rows, :]
     plan.run()
     vec_half.wait_recv()
     small_all[band] = small[...] + small_partner[...]
@@ -1395,32 +1417,57 @@
     )
     vector_spread.start()
     plan.run()
-    columns.wait()
-    for piece in range(4):
-        half_copy(piece).wait_send()
-    sending[...] = swap_rows(landed_grads[...])
-    store_columns = pltpu.make_async_copy(landed_grads, kernel_grads, pix_sem)
+    pix = summed.shape[0]
+
+    def tell_code(target, plane):
+        return pltpu.make_async_remote_copy(
+            src_ref=code_all.at[band],
+            dst_ref=code_all.at[band],
+            send_sem=code_sems[0].at[0],
+            recv_sem=code_sems[1].at[0],
+            device_id=(target, plane),
+            device_id_type=MESH,
+        )
+
+    pass_summed = pltpu.make_async_remote_copy(
+        src_ref=summed, dst_ref=summed, send_sem=summed_sems[0].at[0], recv_sem=summed_sems[1].at[0],
+        device_id=partner, device_id_type=MESH,
+    )
     gen_wait(weights)
-    code_part[...] = jnp.zeros(code_part.shape, F32)
-
-    @pl.loop(0, 16)
-    def _(piece):
-        code_part[...] += dot_nt(
-            sending[pl.ds(aligned(piece * 16), 16), :], weights[pl.ds(aligned(piece * 128), 128), :]
-        )
-
-    code_all[band] = code_part[...]
-    code_spread = Exchange(
-        lambda target: code_all.at[band], lambda source: code_all.at[source], lambda count: code_all.at[pl.ds(0, count)],
-        *[sem.at[0] for sem in code_sems],
-    )
-    code_spread.start()
+
+    @pl.when(owner)
+    def _():
+        bulk_copy(landed_grads.at[pl.ds(0, (2 * bands - 1) * 16)], cols_sems[0].at[0], cols_sems[1].at[0]).wait_recv()
+        summed[...] = landed_grads[0:pix, :] + landed_grads[pix : 2 * pix, :]
+        pass_summed.start()
+        mixing[...] = swap_rows(summed[...])
+        code_part[...] = jnp.zeros(code_part.shape, F32)
+
+        @pl.loop(0, 16)
+        def _(piece):
+            code_part[...] += dot_nt(
+                mixing[pl.ds(aligned(piece * 16), 16), :], weights[pl.ds(aligned(piece * 128), 128), :]
+            )
+
+        code_all[band] = code_part[...]
+        for step in range(bands):
+            for plane in (y, 1 - y) if step else (1 - y,):
+                tell_code((band + step) % bands, plane).start()
+
+    @pl.when(core != y)
+    def _():
+        pass_summed.wait_recv()
+
+    store_columns = pltpu.make_async_copy(summed, kernel_grads, pix_sem)
     store_pixels.wait()
     store_columns.start()
     plan.run()
     vector_spread.wait()
     vectors[...] = small_all[...]
-    code_spread.wait()
+    bulk = code_all.at[pl.ds(0, bands - 1)]
+    pl.when(owner)(bulk_copy(bulk, code_sems[0].at[0], code_sems[1].at[0]).wait_recv)
+    bulk = code_all.at[pl.ds(0, bands)]
+    pl.when(core != y)(bulk_copy(bulk, code_sems[0].at[0], code_sems[1].at[0]).wait_recv)
     total = code_all[0]
     for source in range(1, bands):
         total = total + code_all[source]
@@ -1428,29 +1475,43 @@
     plan.run()
     reduce.finish()
     grads.finish()
-    columns.finish()
     vec_half.wait_send()
     vector_spread.finish()
-    code_spread.finish()
+
+    @pl.when(owner)
+    def _():
+        sent = landed_grads.at[pl.ds(0, (bands - 1) * 16)]
+        bulk_copy(sent, cols_sems[0].at[0], cols_sems[1].at[0]).wait_send()
+        sent = code_all.at[pl.ds(0, 2 * bands - 1)]
+        bulk_copy(sent, code_sems[0].at[0], code_sems[1].at[0]).wait_send()
+        pass_summed.wait_send()
+
+    @pl.when(core != y)
+    def _():
+        sent = landed_grads.at[pl.ds(0, bands * 16)]
+        bulk_copy(sent, cols_sems[0].at[0], cols_sems[1].at[0]).wait_send()
+
     store_columns.wait()
 
 
 VMEM_BYTES = 63 * 2**20
 
 
-def layer(pixels, kernel_gen, weights, waves, hyper, bias_gen, band_scale, out_grad, gains):
-    width = gains.shape[1]
+def layer(counts, mask, pixels, kernel_gen, weights, waves, hyper, bias_gen, out_grad, gains):
+    width = bias_gen.shape[1]
     bands = lax.axis_size("band")
     devices = bands * lax.axis_size("dp")
     images, tokens, pix = pixels.shape
-    hidden = hyper[3].shape[1]
+    hidden = hyper[4].shape[1]
     vmem = pl.BlockSpec(memory_space=pltpu.VMEM)
     hbm = pl.BlockSpec(memory_space=pl.ANY)
+    smem = pl.BlockSpec(memory_space=pltpu.SMEM)
     shape = jax.ShapeDtypeStruct
     rows = lambda kind, *lead: pltpu.VMEM((*lead, tokens, width), kind)
+    pair = lambda *lead: pltpu.VMEM((*lead, 2 * tokens, width), B16)
     dma = pltpu.SemaphoreType.DMA
     code = (bands, HW)
-    kept = [(bands, 3 * HW), (HHEADS * bands, bands), code, code, (bands, 1), (bands, hidden), code, (bands, 1)]
+    kept = [(bands, 3 * HW), (HHEADS * bands, bands), code, code, (bands, 1), (bands, hidden), code, (bands, 1), (2, HW)]
     return pl.pallas_call(
         layer_kernel,
         out_shape=[
@@ -1463,83 +1524,82 @@
             shape((bands, 8, width), F32),
             *[shape(dims, F32) for dims in kept],
         ],
-        in_specs=[hbm, hbm] + [vmem] * 14,
-        out_specs=[vmem, hbm, vmem, hbm] + [vmem] * 11,
+        in_specs=[smem] * 2 + [hbm] * 2 + [vmem] * 15,
+        out_specs=[vmem, hbm, vmem, hbm] + [vmem] * 12,
         scratch_shapes=[
             pltpu.VMEM((3, devices * PART, width), B16),
             pltpu.VMEM((8 * width, width), B16),
-            pltpu.VMEM((devices * PART, width), B16),
-            pltpu.VMEM((3, devices // 2 * PART, width), B16),
-            pltpu.VMEM((3, 19, PART, width), B16),
+            pltpu.VMEM((16 * HW, width), B16),
+            pltpu.VMEM((3 * 19 * PART, width), B16),
             rows(B16, 3),
             pltpu.VMEM((HEADS // 2, 2 * tokens, tokens), F32),
             rows(F32, 4),
-            rows(B16, 4),
-            rows(B16, 4),
-            rows(B16),
-            rows(B16),
-            rows(B16),
+            pair(4),
+            pair(4),
+            pair(),
+            pair(),
+            pair(),
+            pair(),
             rows(F32),
             rows(F32),
             pltpu.VMEM((tokens, 128), F32),
             pltpu.VMEM((tokens, 128), F32),
             rows(F32),
             rows(F32),
+            pair(),
             rows(B16),
-            rows(B16),
-            rows(B16, 3),
-            pltpu.VMEM((width, tokens), B16),
-            pltpu.VMEM((width, tokens), B16),
+            pair(3),
+            pltpu.VMEM((width, 2 * tokens), B16),
+            pltpu.VMEM((2, width // 2, 2 * tokens), B16),
             rows(F32),
             pltpu.VMEM(pixels.shape, B16),
             pltpu.VMEM((4, pix, 4 * tokens), B16),
+            pltpu.VMEM((images // 2, tokens, pix), B16),
             pltpu.VMEM((pix, width), B16),
             pltpu.VMEM((pix, width), B16),
             pltpu.VMEM((pix, width), B16),
             pltpu.VMEM((pix, width), B16),
+            pltpu.VMEM((2 * pix, width), B16),
             pltpu.VMEM((pix, width), B16),
             pltpu.VMEM((8, width), F32),
             pltpu.VMEM((8, width), F32),
             pltpu.VMEM((bands, 8, width), F32),
             pltpu.VMEM(code, F32),
-            pltpu.VMEM((bands, *code), F32),
+            pltpu.VMEM((2 * bands, *code), F32),
+            pltpu.VMEM((2, width), F32),
+            pltpu.VMEM((images, 8, 128), F32),
+            pltpu.VMEM((images, 8, 128), F32),
             dma,
             dma,
             pltpu.SemaphoreType.REGULAR,
             pltpu.SemaphoreType.REGULAR,
             *[dma((3, 3)), dma((3, 16)), dma((3, 2)), dma((3, 2))],
-            *[dma((3, 2)), dma((3, 16)), dma((3, 3)), dma((3, 19))],
-            *[dma((1, 2)), dma((1, 8)), dma((2, 2)), dma((2, 9))],
             *[dma((2, 3)), dma((2, 16)), dma((2, 2)), dma((2, 2))],
-            *[dma((1,))] * 8,
-            *[dma((4,))] * 2,
-            *[dma((1,))] * 2,
+            *[dma((3, 3)), dma((3, 19))],
+            *[dma((2, 2)), dma((2, 9))],
+            *[dma((len(SHARED),))] * 2,
+            *[dma((3,))] * 2,
+            *[dma((1,))] * 12,
         ],
         compiler_params=pltpu.CompilerParams(
             collective_id=0, has_side_effects=True, vmem_limit_bytes=VMEM_BYTES
         ),
         name="layer",
-    )(pixels, kernel_gen, *weights, waves, *hyper, bias_gen, band_scale, out_grad, gains)
+    )(counts, mask, pixels, kernel_gen, *weights, waves, *hyper, bias_gen, out_grad, *gains)
 
 
 def finish_kernel(*refs):
-    count = 12 + len(KEPT)
-    block_in, pixel_in, *outside = refs[: count + 2]
+    count = 13 + len(KEPT)
+    outside = refs[:count]
     (block_out, pixel_out, grad_qkv, grad_out, grad_gain_one, grad_up, grad_down, grad_gain_two, grad_gen, grad_bias,
-     gain_sums, share_qkv, share_out, share_up, share_down, *scratch) = refs[count + 2 :]
+     gain_one_sum, gain_two_sum, share_qkv, share_out, share_up, share_down, *scratch) = refs[count:]
     inside, (store, in_sem, copy_sem, gen_sem) = scratch[:count], scratch[count:]
     loads = [pltpu.make_async_copy(*pair, in_sem.at[at]) for at, pair in enumerate(zip(outside, inside))]
     for load in loads:
         load.start()
-    (code_low, columns, shares, waves, hyper_qkv, hyper_out, hyper_gains, hyper_up, hyper_down, bias_gen, code_grads, vectors,
-     *kept_refs) = inside
+    (code_low, columns, shares, waves, hyper_qkv, hyper_out, hyper_up, hyper_down, bias_gen, code_grads, vectors,
+     *kept_refs, hyper_gains, block_in, pixel_in) = inside
     width = bias_gen.shape[1]
-    copies = [
-        pltpu.make_async_copy(block_in, block_out, copy_sem.at[0]),
-        pltpu.make_async_copy(pixel_in, pixel_out, copy_sem.at[1]),
-    ]
-    for copy in copies:
-        copy.start()
     for load in loads[:2]:
         load.wait()
     code = code_low[...]
@@ -1558,11 +1618,19 @@
         gen_copies[-1].start()
     for load in loads[2:]:
         load.wait()
+    copies = [
+        pltpu.make_async_copy(block_in, block_out, copy_sem.at[0]),
+        pltpu.make_async_copy(pixel_in, pixel_out, copy_sem.at[1]),
+    ]
+    for copy in copies:
+        copy.start()
     share_qkv[...] = jnp.concatenate([shares[at * 24 : at * 24 + 24, :] for at in range(3)], axis=1)
     share_out[...] = shares[72:96, :]
     share_up[...] = jnp.concatenate([shares[at * 24 : at * 24 + 24, :] for at in range(4, 8)], axis=1)
     share_down[...] = shares[192:288, :]
-    gain_sums[...] = jnp.sum(vectors[...], axis=0)
+    sums = jnp.sum(vectors[...], axis=0)
+    gain_one_sum[...] = sums[0]
+    gain_two_sum[...] = sums[1]
     bias_grads = vectors[:, 2, :]
     grad_bias[...] = dot_tn(jnp.concatenate([code] * 3, axis=0), jnp.concatenate(split3(bias_grads), axis=0))
     grad_code = code_grads[...] + wide_nt(bias_grads, bias_gen[...])
@@ -1582,18 +1650,19 @@
     hbm = pl.BlockSpec(memory_space=pl.ANY)
     shape = lambda array: jax.ShapeDtypeStruct(array.shape, F32)
     line = jax.ShapeDtypeStruct((1, HW), F32)
-    operands = (code_low, columns, shares, waves, *hyper, bias_gen, code_grads, vectors, *kept)
+    weights_in = (hyper[0], hyper[1], hyper[4], hyper[5])
+    operands = (code_low, columns, shares, waves, *weights_in, bias_gen, code_grads, vectors, *kept, block_out, pixel_grad)
     return pl.pallas_call(
         finish_kernel,
         out_shape=[
             jax.ShapeDtypeStruct(block_out.shape, B16),
             jax.ShapeDtypeStruct(pixel_grad.shape, B16),
-            shape(hyper[0]), shape(hyper[1]), line, shape(hyper[3]), shape(hyper[4]), line,
-            shape(kernel_gen), shape(bias_gen), jax.ShapeDtypeStruct((8, width), F32),
+            shape(hyper[0]), shape(hyper[1]), line, shape(hyper[4]), shape(hyper[5]), line,
+            shape(kernel_gen), shape(bias_gen), *[jax.ShapeDtypeStruct((width,), F32)] * 2,
             *[shape(weight) for weight in weights],
         ],
-        in_specs=[hbm] * (2 + len(operands)),
-        out_specs=[hbm, hbm] + [vmem] * 6 + [hbm] + [vmem] * 6,
+        in_specs=[hbm] * len(operands),
+        out_specs=[hbm, hbm] + [vmem] * 6 + [hbm] + [vmem] * 7,
         scratch_shapes=[
             *[pltpu.VMEM(operand.shape, operand.dtype) for operand in operands],
             pltpu.VMEM((4, HW, width), F32),
@@ -1601,9 +1670,9 @@
             pltpu.SemaphoreType.DMA((2,)),
             pltpu.SemaphoreType.DMA((4,)),
         ],
-        compiler_params=pltpu.CompilerParams(vmem_limit_bytes=40 * 2**20),
+        compiler_params=pltpu.CompilerParams(vmem_limit_bytes=VMEM_BYTES),
         name="finish",
-    )(block_out, pixel_grad, *operands)
+    )(*operands)
 
 
 def body(
@@ -1821,24 +1890,23 @@
     mlp_down,
     out_grad,
 ):
-    waves = wave_embed(wavelengths, HW)
-    band = lax.axis_index("band")
-    count_row = band_counts[0]
-    active = (band < count_row) & (band_mask[0, :, 0] == 1)
-    band_weight = jnp.where(active, lax.rsqrt(count_row.astype(F32)), F32(0.0))
+    lane = jnp.arange(HW)
+    frequency = jnp.power(10000.0, -(lane % (HW // 2)).astype(F32) / (HW // 2))
+    angles = wavelengths.astype(F32)[:, None] * frequency[None, :]
+    waves = jnp.where(lane < HW // 2, jnp.sin(angles), jnp.cos(angles))
     weights = (attn_qkv, attn_out, mlp_up, mlp_down)
-    hyper_gains = jnp.stack([hyper_gain1, hyper_gain2]).astype(F32)
-    hyper = (hyper_qkv, hyper_out, hyper_gains, hyper_up, hyper_down)
+    hyper = (hyper_qkv, hyper_out, hyper_gain1, hyper_gain2, hyper_up, hyper_down)
     block_out, pixel_grad, shares, columns, code_low, code_grads, vectors, *kept = layer(
+        band_counts[0],
+        band_mask[0, :, 0],
         pixels[0, :, :, 0],
         kernel_gen,
         weights,
         waves,
         hyper,
         bias_gen,
-        jnp.broadcast_to(band_weight[:, None, None], (band_weight.shape[0], 8, 128)),
         out_grad[0, 0],
-        jnp.stack([norm_gain1, norm_gain2]).astype(F32),
+        (norm_gain1, norm_gain2),
     )
     outs = finish(
         waves,
@@ -1855,7 +1923,7 @@
         kernel_gen,
         weights,
     )
-    block_out, pixel_grad, *hyper_grads, grad_gen, grad_bias, gain_sums = outs[:11]
+    block_out, pixel_grad, *hyper_grads, grad_gen, grad_bias, gain_one, gain_two = outs[:12]
     hyper_grads[2], hyper_grads[5] = hyper_grads[2][0], hyper_grads[5][0]
     return (
         block_out[None, None],
@@ -1863,12 +1931,12 @@
         *hyper_grads,
         grad_gen,
         grad_bias,
-        gain_sums[0],
-        outs[11],
+        gain_one,
         outs[12],
-        gain_sums[1],
         outs[13],
+        gain_two,
         outs[14],
+        outs[15],
     )
 
 

time: 213 us -> 183 us (0.86)
  local copies, waits for them, and re-layouts: 16.3 us -> 0 us
  Pallas kernels: 191 us -> 179 us
  other arithmetic: 4.08 us -> 1.39 us
    unnamed x44 -> x0, local copies, waits for them, and re-layouts: 13.6 us -> none
    pallas_call x1, Pallas kernels: 182 us -> 170 us  [layer(): pl.pallas_call(layer_kernel, out_shape=[shape((tokens, width), B16), shap...]
where the time goes in v5:
time: 183 us; the launch traced here: 181 us
  Pallas kernels  179 us (98%)
    pallas_call x1, Pallas kernels, layer(): pl.pallas_call(layer_kernel, out_shape=[shape((tokens, width), B16), shap...  170 us
    pallas_call x1, Pallas kernels, finish(): pl.pallas_call(finish_kernel, out_shape=[jax.ShapeDtypeStruct(block_out.s...  9.18 us

profile of v5, /device:TPU:0, one launch (start us, length us, event | category | flops | bytes accessed | tf_op | source)
XLA Modules:
  0.0 181.0 jit_solution(4177766603630662461)
XLA Ops:
  0.6 0.7 convert_element_type.10
  1.3 0.7 fusion.refs_8_.refs_3_
  2.0 169.6 %layer.1 = (bf16[128,768]{1,0:T(8,128)(2,1)}, bf16[16,128,256]{2,1,0:T(8,128)(2,1)}, f32[288,768]{1,0:T(8,128)}, bf16[256,768]{1,0:T(8,128)(2,1)}, bf16[16,128]{...) custom-call(s32[16]{0:T(128)} %bitcast.12, ...), custom_call_target="tpu_custom_call" | custom-call | tf_op jit(solution)/shard_map/layer/pallas_call | solution.py:1515
  171.6 9.2 %finish.1 = (bf16[128,768]{1,0:T(8,128)(2,1)}, bf16[16,128,256]{2,1,0:T(8,128)(2,1)}, f32[128,384]{1,0:T(8,128)}, f32[128,128]{1,0:T(8,128)}, f32[1,128]{1,0:T(1...) custom-call(bf16[16,128]{1,0:T(8,128)(2,1)} %get-tuple-element.48.re, ...), custom_call_target="tpu_custom_call" | custom-call | tf_op jit(solution)/shard_map/finish/pallas_call | solution.py:1655
  (2 shorter events, 0.0 us)

commit v6 on v5

--- a/solution.py
+++ b/solution.py
@@ -98,17 +98,18 @@
         (),
         (),
         (),
-        (1, 2, 3, 30),
-        (54, 27),
-        (),
-        (11, 29, 57),
-        (),
-        (56,),
-        (13, 10, 5, 33, 60, 81, 85, 59, 39, 82, 86, 32, 22, 83, 84, 35, 17, 87, 95, 62, 45, 88, 96, 9, 47, 66, 93, 101, 65, 21, 94, 102, 38, 14, 41, 49, 72, 68, 24, 74, 71, 51, 18, 44, 76, 104, 107, 26, 106, 108, 78),
-        (53,),
-        (80,),
-        (),
-        (),
+        (1, 3, 2, 42, 41, 29, 11),
+        (),
+        (),
+        (53, 57, 61, 10, 13, 28),
+        (54,),
+        (55, 66, 72, 5, 58, 63, 48),
+        (56, 77, 83, 62, 22, 44, 67, 74, 35, 9, 14, 17, 73, 80, 82, 84, 50, 18, 89, 21, 91, 24, 31, 26, 34),
+        (86, 87, 37),
+        (39, 47),
+        (),
+        (),
+        (52,),
         (),
         (),
     ),
@@ -116,18 +117,19 @@
         (),
         (),
         (),
-        (0, 1, 2, 3),
-        (30, 54, 27),
-        (28, 7, 57),
-        (),
-        (29,),
-        (55, 11, 6),
-        (56,),
-        (58, 13, 10, 5, 31, 33, 60, 59, 81, 89, 36, 82, 32, 91, 39, 83, 35, 84, 19, 62, 63, 22, 87, 97, 65, 17, 88, 99, 38, 42, 98, 66, 93, 103, 100, 45, 94, 105, 104, 107, 47, 106, 108, 69, 49, 14, 72, 24, 74),
-        (),
-        (76,),
-        (),
-        (),
+        (0, 1, 3, 2),
+        (42, 29, 41, 7, 40),
+        (6, 11),
+        (),
+        (53,),
+        (54, 10, 13),
+        (55, 59, 5),
+        (56, 58, 64, 48, 62, 70, 45, 67, 75, 71, 27, 19, 68, 76, 14, 81, 73, 22, 88, 28, 17, 78, 82, 84, 31, 85, 89, 32, 91, 79, 44, 24),
+        (86, 87, 35),
+        (37,),
+        (),
+        (),
+        (50,),
         (),
         (),
     ),
@@ -135,17 +137,18 @@
         (),
         (),
         (),
-        (0, 1, 2, 3),
-        (30,),
-        (54, 27),
-        (),
-        (29, 7, 57),
-        (28,),
-        (56, 11, 6),
-        (55, 59, 13, 10, 4, 32, 33, 60, 58, 81, 39, 82, 31, 36, 83, 90, 34, 84, 92, 19, 87, 61, 22, 88, 64, 104, 15, 66, 106, 37, 93, 98, 45, 97, 94, 100, 99, 42, 63, 103, 107, 46, 105, 108, 72, 48, 12, 69, 23, 73),
-        (),
-        (75,),
-        (),
+        (0, 1, 3, 2),
+        (42, 29, 40, 7),
+        (41,),
+        (),
+        (53, 6, 11),
+        (54,),
+        (55, 10, 13),
+        (56, 58, 4, 45, 62, 60, 67, 48, 65, 70, 73, 28, 82, 75, 19, 89, 12, 81, 84, 22, 71, 88, 27, 76, 91, 15, 69, 30, 78, 35, 86, 85, 87, 79, 43, 23),
+        (32,),
+        (),
+        (36,),
+        (49,),
         (),
         (),
         (),
@@ -155,17 +158,18 @@
         (),
         (),
         (),
-        (0, 2, 3, 30, 54, 27),
-        (28, 7, 57),
-        (),
-        (),
-        (13, 6, 55),
-        (),
-        (4, 33, 60, 81, 58, 36, 82, 31, 19, 83, 85, 84, 86, 34, 15, 63, 61, 42, 87, 101, 8, 46, 88, 102, 93, 95, 64, 94, 96, 20, 37, 12, 40, 69, 48, 67, 73, 23, 70, 16, 50, 43, 75, 103, 107, 25, 105, 108, 77),
-        (52,),
-        (79,),
-        (),
-        (),
+        (0, 3, 2, 42, 40, 29, 7),
+        (6, 13, 27),
+        (),
+        (53,),
+        (54, 57, 61, 4, 45),
+        (55, 77, 83),
+        (56, 66, 72, 58, 19, 43, 62, 63, 32, 8, 12, 15, 67, 80, 81, 84, 49, 73, 74, 88, 20, 16, 91, 23, 30, 25, 33),
+        (85, 87, 36),
+        (38, 46),
+        (),
+        (),
+        (51,),
         (),
         (),
     ),
@@ -174,83 +178,73 @@
     (
         (),
         (),
-        (),
-        (),
-        (),
-        (),
-        (),
-        (),
-        (),
-        (),
-        (),
-        (81, 94, 0, 3, 1, 7, 2, 4, 8, 13, 29, 84, 11, 17, 30, 97, 12, 20, 31, 87, 100, 14, 23, 33, 82, 32, 37, 95, 22, 88, 36, 40, 101, 26, 42, 41),
-        (90, 103, 46, 43, 92, 49, 58, 105),
-        (59, 60, 61, 52, 62, 64, 65, 63, 68, 51, 53, 69, 73, 70, 55, 24, 57, 71, 72, 76),
-        (),
-        (28, 78),
-        (79,),
+        (0, 1, 2, 3),
+        (),
+        (4, 6),
+        (),
+        (5,),
+        (18, 21, 24, 27, 30, 33, 7, 70, 71, 11),
+        (83, 84, 39, 40, 41, 42, 43, 77, 44, 45, 46, 10, 14, 73, 90, 86, 47),
+        (79, 76, 92, 48, 89, 49, 53, 50, 16, 17, 81, 51, 94),
+        (54, 32, 34, 52, 57, 36, 59, 60, 58, 62, 61, 65),
+        (),
+        (38, 95, 96, 67, 68),
+        (),
     ),
     (
         (),
         (),
-        (),
-        (),
-        (),
-        (),
-        (),
-        (),
-        (),
-        (),
-        (),
-        (80, 81, 93, 94, 0, 1, 2, 4, 8, 29, 84, 11, 30, 5, 97, 12, 31, 9, 14, 33, 16, 15, 82, 37, 19, 95, 18, 85, 40, 21, 88, 41, 98, 25),
-        (101, 22, 90, 43, 34, 26, 58, 103, 38),
-        (59, 60, 45, 61, 44, 48, 62, 50, 47, 65, 63, 68, 69, 70, 24, 54, 51, 53, 71, 66, 55, 72, 74),
-        (),
-        (57, 75, 77, 28),
-        (78, 79),
+        (0, 1, 2, 3),
+        (),
+        (4,),
+        (),
+        (5,),
+        (8, 7),
+        (70, 71, 69, 83, 84, 82, 39, 40, 41, 42, 43, 44, 45, 46, 10, 19, 73, 77, 86, 74, 47, 22, 90, 13, 48, 25, 87),
+        (79, 92, 26, 50, 28, 29, 51, 31),
+        (49, 54, 35, 32, 34, 52, 57, 12, 36, 59, 15, 58, 60, 55, 61),
+        (16, 17, 38, 95),
+        (64, 63, 96, 66, 67, 68),
+        (),
     ),
     (
         (),
         (),
-        (),
-        (),
-        (),
-        (),
-        (),
-        (),
-        (),
-        (),
-        (),
-        (80, 81, 93, 94, 0, 1, 2, 4, 8, 29, 83, 11, 30, 96, 6, 12, 31, 10, 15, 14, 33, 22, 82, 18, 37, 95, 26, 21, 85, 40, 16, 88, 25, 41, 98, 19, 101, 43),
-        (89, 35, 102, 58, 39),
-        (59, 44, 60, 61, 47, 45, 62, 51, 48, 65, 63, 68, 69, 50, 53, 70, 24, 55, 54, 71, 67, 57, 78),
-        (),
-        (72, 74, 28, 77, 79, 75),
+        (0, 1, 2, 3),
+        (),
+        (4,),
+        (),
+        (5,),
+        (7,),
+        (69, 70, 71, 82, 83, 84, 39, 40, 41, 42, 43, 44, 45, 46, 10, 9, 74, 12, 72, 77, 47, 20, 85, 87, 48, 23, 90, 25),
+        (78, 50, 26, 28, 49, 51, 29, 31, 91, 54),
+        (32, 34, 35, 52, 57, 36, 58, 59, 16, 60, 13, 61, 56, 15, 17),
+        (63, 38, 95),
+        (67, 96, 64, 66, 68),
         (),
     ),
     (
         (),
         (),
-        (),
-        (),
-        (),
-        (),
-        (),
-        (),
-        (),
-        (),
-        (),
-        (80, 93, 0, 1, 2, 3, 4, 7, 8, 20, 29, 83, 11, 30, 23, 96, 12, 31, 86, 13, 99, 14, 33, 17, 82, 37, 32, 95, 21, 85, 40, 36, 25, 98, 41),
-        (89, 42, 102, 43, 46, 91, 58, 49, 104),
-        (59, 60, 61, 62, 52, 65, 63, 64, 68, 50, 53, 69, 76, 70, 24, 54, 57, 71, 72, 73),
-        (),
-        (28, 77, 79),
+        (0, 1, 2, 3),
+        (),
+        (4,),
+        (),
+        (5, 6),
+        (18, 21, 24, 27, 30, 33, 69, 71, 7, 14),
+        (82, 84, 39, 40, 41, 42, 74, 43, 44, 45, 46, 10, 72, 11, 87, 85, 47),
+        (78, 15, 17, 91, 48, 75, 49, 50, 88, 80, 51, 31, 34, 52, 53, 54, 35, 93),
+        (57, 58, 65, 59, 60, 38, 95, 61, 62, 96),
+        (),
+        (66, 68),
         (),
     ),
 )
-FIRST_PARTS = (0,)
-SUM_ORDERS = ('yxz', 'yzx', 'xzy')
-ORDERS = ("zxy", "xzy", "yzx")
+FIRST_PARTS = (0, 2)
+SUM_ORDERS = ('yxz', 'zy', 'yz')
+EMBED_ORDERS = ('xz', 'zx')
+IMAGE_ORDERS = ('zx', 'zx')
+ORDERS = ('zxy', 'zy', 'zy')
 
 
 def place(known_z=None):
@@ -461,7 +455,7 @@
         when(cond, self.pair(chunk, block, self.core).start)
 
     def rails(self, chunk):
-        return 16 if "y" in self.orders[chunk] else 8
+        return 4 * (2 if "x" in self.orders[chunk] else 1) * (2 if "y" in self.orders[chunk] else 1)
 
     def sent(self, chunk, z, over):
         order = self.orders[chunk]
@@ -519,8 +513,8 @@
     def sibling(self):
         return device(self.z, self.x, 1 - self.core, self.y)
 
-    def blocks(self):
-        return [(zz, fx, fy) for zz in (3, 0, 2, 1) for fx, fy in self.flips(0, 0)]
+    def blocks(self, chunk):
+        return [(zz, fx, fy) for zz in (3, 0, 2, 1) for fx, fy in self.flips(chunk, 0)]
 
     def places(self, chunk):
         order, keys = self.orders[chunk], []
@@ -650,7 +644,12 @@
     def events(self, chunks, start=0.0, pace=1.0):
         found = []
         for chunk in chunks:
-            times = {block: start for block in self.blocks()}
+            times = {block: start for block in self.blocks(chunk)}
+            found += [
+                (start, chunk, functools.partial(self.start, chunk, block))
+                for block in self.blocks(chunk)
+                if dict(x=block[1], y=block[2], z=0)[self.orders[chunk][0]]
+            ]
             for stage, dim in enumerate(self.orders[chunk]):
                 clock, later = 0.0, {}
                 if dim == "z":
@@ -783,7 +782,7 @@
             mixed = dot_nn(probs.astype(B16), value)
             self.mixed[:tokens, lanes] = jnp.where(where, mixed[:tokens], mixed[tokens:]).astype(B16)
 
-    def widen(self):
+    def middle(self):
         middle = self.residual[...] + dot_nn(self.own(self.mixed), self.weight(3))
         unit, inverse = unit_parts(middle)
         self.normed_two[: self.tokens] = (unit * self.gain_two[...]).astype(B16)
@@ -791,61 +790,74 @@
         self.inverse_two[...] = jnp.broadcast_to(inverse, self.inverse_two.shape)
         self.result[...] = middle
 
-        @pl.loop(0, 4)
+    def both_x(self, ref):
+        return ref[: 2 * self.tokens]
+
+    def down_rows(self, part):
+        return self.down[pl.ds(aligned(part * self.width), self.width), :]
+
+    def widen(self):
+        @pl.loop(0, 2)
         def _(part):
-            pre = dot_nn(self.own(self.normed_two), self.weight(4 + part))
+            pre = dot_nn(self.both_x(self.normed_two), self.weight(4 + part))
             self.pre_act[part] = pre
-            self.act[part, : self.tokens] = gelu_tanh(pre).astype(B16)
+            self.act[part, : 2 * self.tokens] = gelu_tanh(pre).astype(B16)
 
     def narrow(self):
-        @pl.loop(0, 4)
-        def _(part):
-            rows = pl.ds(aligned(part * self.width), self.width)
-            self.result[...] += dot_nn(self.act[part, : self.tokens], self.down[rows, :])
-
-        self.block_out[...] = self.result[...].astype(B16)
+        parts = [dot_nn(self.act[part, : 2 * self.tokens], self.down_rows(part)) for part in (0, 1)]
+        total = parts[0] + parts[1]
+        self.result[...] += total[: self.tokens]
+        self.result_x[...] = total[self.tokens :].astype(B16)
 
     def back_narrow(self):
         self.grad_normed[...] = jnp.zeros(self.grad_normed.shape, F32)
 
-        @pl.loop(0, 4)
+        @pl.loop(0, 2)
         def _(part):
-            rows = pl.ds(aligned(part * self.width), self.width)
-            grad_act = dot_nt(self.own(self.out_grad), self.down[rows, :])
+            grad_act = dot_nt(self.both_x(self.out_grad), self.down_rows(part))
             grad_pre = (grad_act * gelu_slope(self.pre_act[part])).astype(B16)
-            self.grad_pre[part, : self.tokens] = grad_pre
+            self.grad_pre[part, : 2 * self.tokens] = grad_pre
             self.grad_normed[...] += dot_nt(grad_pre, self.weight(4 + part))
 
-    def down_grad(self, part, core, store):
-        self.turned[...] = self.act[part].T
-        for x in (0, 1):
-            rows = self.turned[pl.ds(aligned((x * 2 + core) * 2 * PART), 2 * PART), :]
-            for at in range(0, self.width, 256):
-                cols = slice(at, at + 256)
-                store[(part * 4 + x * 2) * PART : (part * 4 + x * 2 + 2) * PART, cols] = dot_nn(
-                    rows, self.out_grad[:, cols]
-                ).astype(B16)
-
-    def turn_rail(self, which, ref, core):
-        self.turned[...] = ref[...].T
+        self.grad_x[...] = self.grad_normed[self.tokens :].astype(B16)
+
+    def turn(self, ref):
+        rows = ref.shape[0]
+        for at in range(0, self.width, 128):
+            self.turned[at : at + 128, :rows] = ref[:, at : at + 128].T
+
+    def down_grad(self, part, core, rail, store):
+        self.turn(self.act.at[part])
+        for z in (0, 1):
+            rail[z * 2 * PART : (z + 1) * 2 * PART, :] = self.turned[
+                pl.ds(aligned((z * 2 + core) * 2 * PART), 2 * PART), :
+            ]
+        for at in range(0, self.width, 256):
+            cols = slice(at, at + 256)
+            rows = slice(part * 4 * PART, (part + 1) * 4 * PART)
+            store[rows, cols] = dot_nn(rail[...], self.out_grad[:, cols]).astype(B16)
+
+    def turn_rail(self, target, ref, core):
+        rows = ref.shape[0]
+        self.turn(ref)
         for chip in range(8):
-            self.rail_rows[which, chip * CHUNK : (chip + 1) * CHUNK, :] = self.turned[
-                pl.ds(aligned((chip * 2 + core) * CHUNK), CHUNK), :
+            target[chip * CHUNK : (chip + 1) * CHUNK, :] = self.turned[
+                pl.ds(aligned((chip * 2 + core) * CHUNK), CHUNK), :rows
             ]
 
-    def pair_grad(self, first, second, first_grad, second_grad, store, offset):
+    def pair_grad(self, first, second, first_grad, second_grad, store, where):
         half = CHUNK // 2
         for at in range(0, self.width, 256):
             cols = slice(at, at + 256)
-            one = dot_nn(self.rail_rows[first], first_grad(cols))
-            two = dot_nn(self.rail_rows[second], second_grad(cols))
+            one = dot_nn(first[...], first_grad(cols))
+            two = dot_nn(second[...], second_grad(cols))
             for owner in range(16):
                 rows = slice(owner * half, owner * half + half)
                 piece = jnp.concatenate([one[rows], two[rows]], axis=0)
-                store[owner * PART + offset : owner * PART + offset + CHUNK, cols] = piece.astype(B16)
+                store[pl.ds(where(owner), CHUNK), cols] = piece.astype(B16)
 
     def back_wide(self):
-        grad_normed = self.grad_normed[...]
+        grad_normed = self.own(self.grad_normed) + self.grad_from_x[...].astype(F32)
         unit = self.unit_two[...]
         self.small[1:2, :] = jnp.sum(grad_normed * unit, axis=0, keepdims=True)
         scaled = grad_normed * self.gain_two[...]
@@ -883,13 +895,8 @@
             self.grad_joint[1, :tokens, lanes] = keys.astype(B16)
 
     def back_project(self):
-        self.grad_normed[...] = jnp.zeros(self.grad_normed.shape, F32)
-
-        @pl.loop(0, 3)
-        def _(part):
-            self.grad_normed[...] += dot_nt(self.grad_joint[part, : self.tokens], self.weight(part))
-
-        grad_normed = self.grad_normed[...]
+        parts = [dot_nt(self.grad_joint[part, : self.tokens], self.weight(part)) for part in range(3)]
+        grad_normed = parts[0] + parts[1] + parts[2]
         unit = self.unit_one[...]
         self.small[0:1, :] = jnp.sum(grad_normed * unit, axis=0, keepdims=True)
         scaled = grad_normed * self.gain_one[...]
@@ -1009,7 +1016,7 @@
     return grad_qkv, grad_out, grad_gain_one, grad_up, grad_down, grad_gain_two
 
 
-def spread(gathered, weights, part):
+def spread(gathered, weights):
     width = weights.shape[1]
     half = CHUNK // 2
 
@@ -1017,11 +1024,29 @@
     def _(two):
         for pair in (0, 1):
             one, other = (
-                gathered[part, pl.ds(aligned((two * 2 + k) * PART + pair * CHUNK), CHUNK), :].astype(F32)
+                gathered[pl.ds(aligned((two * 2 + k) * PART + pair * CHUNK), CHUNK), :].astype(F32)
                 for k in (0, 1)
             )
             for k, rows in ((0, slice(0, half)), (1, slice(half, CHUNK))):
-                target = pl.ds(aligned((4 * part + 2 * pair + k) * width + two * CHUNK), CHUNK)
+                target = pl.ds(aligned((2 * pair + k) * width + two * CHUNK), CHUNK)
+                weights[target, :] = jnp.concatenate([one[rows], other[rows]], 0).astype(B16)
+
+
+def spread_up(gathered, weights, x):
+    width = weights.shape[1]
+    half = CHUNK // 2
+
+    @pl.loop(0, 8)
+    def _(chip):
+        z, core = chip // 2, chip % 2
+        for far in (0, 1):
+            one, other = (
+                gathered[pl.ds(aligned((chip * 2 + k) * PART + far * CHUNK), CHUNK), :].astype(F32)
+                for k in (0, 1)
+            )
+            row = (z * 4 + (1 - x if far else x) * 2 + core) * CHUNK
+            for k, rows in ((0, slice(0, half)), (1, slice(half, CHUNK))):
+                target = pl.ds(aligned((4 + k) * width + row), CHUNK)
                 weights[target, :] = jnp.concatenate([one[rows], other[rows]], 0).astype(B16)
 
 
@@ -1037,19 +1062,21 @@
     return ref.at[pl.ds(aligned(index * 16), 16)]
 
 
-KEPT = ("joint", "soft", "mixed", "unit_one", "inverse_one", "inner", "unit_two", "inverse_two", "gains")
-SHARED = ("out_grad", "normed_one", "mixed", "normed_two", "act0", "act1", "act2", "act3")
-SHARED += ("pre0", "pre1", "pre2", "pre3", "grad_branch", "joint0", "joint1", "joint2")
+KEPT = 9
+SHARED = ("og", "n1", "mx", "n2", "a0", "a1")
+SHARED += ("p0", "p1", "gb", "j0", "j1", "j2")
+ACROSS = ("u", "og", "n2", "r", "g", "s")
 
 
 def layer_kernel(*refs):
     (counts, mask, pixels, kernel_gen, attn_qkv, attn_out, mlp_up, mlp_down, waves, hyper_qkv, hyper_out, hyper_one, hyper_two,
      hyper_up, hyper_down, bias_gen, out_grad_in, norm_one, norm_two,
      block_out, pixel_out, shares, kernel_grads, code_out, code_grads, vectors, *rest_refs) = refs
-    kept_refs, rest_refs = rest_refs[: len(KEPT)], rest_refs[len(KEPT) :]
-    (gathered, weights, spare, buf, joint, probs, pre_act, act, grad_pre, out_grad, mixed, normed_one, normed_two,
+    kept_refs, rest_refs = rest_refs[: KEPT], rest_refs[KEPT :]
+    (gathered_attn, gathered_up, gathered_down, weights, spare, buf, joint, probs, pre_act, act, grad_pre, out_grad, mixed, normed_one, normed_two,
      unit_one, unit_two, inverse_one, inverse_two, grad_normed, grad_middle, grad_branch, grad_mixed, grad_joint,
-     turned, rail_rows, residual, pixel_rows, turned_pixels, pair_pixels, mixing, kernels, pair_kernels, sending,
+     turned, rail_one, rail_mixed, rail_two, up_away, up_share, up_landed, result_x, result_from_x, grad_x, grad_from_x,
+     residual, pixel_rows, turned_pixels, pair_pixels, mixing, kernels, pair_kernels, sending,
      landed_grads, summed, small, small_partner, small_all, code_part, code_all, gains, band_scale, pair_scale,
      pix_sem, gen_sem, front_done, narrow_done, *sems) = rest_refs
     z, x, core, y = place()
@@ -1062,9 +1089,9 @@
     partner = (band, 1 - y)
     own_rows = pl.ds(aligned(band * 16), 16)
     gather_sems, grads_sems = sems[0:4], sems[4:8]
-    reduce_sems, embed_sems, share_sems, front_sems, kernel_sems, cols_sems, summed_sems, vec_half_sems, vec_sems, code_sems = (
-        sems[at : at + 2] for at in range(8, 28, 2)
-    )
+    (reduce_sems, embed_sems, share_sems, across_sems, front_sems, kernel_sems, cols_sems, summed_sems, vec_half_sems, vec_sems,
+     code_sems) = (sems[at : at + 2] for at in range(8, 30, 2))
+    gathered = (gathered_attn, gathered_up, gathered_down)
 
     def to_pair(index, source, target, pair=share_sems):
         return pltpu.make_async_remote_copy(
@@ -1079,11 +1106,33 @@
     def shared(name):
         index = SHARED.index(name)
         ref = dict(
-            out_grad=out_grad, normed_one=normed_one, mixed=mixed, normed_two=normed_two, grad_branch=grad_branch
+            og=out_grad, n1=normed_one, mx=mixed, n2=normed_two, gb=grad_branch
         ).get(name)
         if ref is None:
-            ref = dict(act=act, pre=grad_pre, joint=grad_joint)[name[:-1]].at[int(name[-1])]
-        return to_pair(index, ref.at[pl.ds(0, tokens)], ref.at[pl.ds(tokens, tokens)])
+            ref = dict(a=act, p=grad_pre, j=grad_joint)[name[0]].at[int(name[1])]
+        half = ref.shape[0] // 2
+        return to_pair(index, ref.at[pl.ds(0, half)], ref.at[pl.ds(half, half)])
+
+    own_block = aligned((z * 4 + core * 2 + y) * PART)
+
+    def across(name):
+        own, other = pl.ds(0, tokens), pl.ds(tokens, tokens)
+        source, target = dict(
+            u=(up_away, gathered_up.at[pl.ds(own_block + CHUNK, CHUNK)]),
+            og=(out_grad.at[own], out_grad.at[other]),
+            n2=(normed_two.at[own], normed_two.at[other]),
+            r=(result_x, result_from_x),
+            g=(grad_x, grad_from_x),
+            s=(up_share.at[pl.ds(CHUNK, CHUNK)], up_landed),
+        )[name]
+        return pltpu.make_async_remote_copy(
+            src_ref=source,
+            dst_ref=target,
+            send_sem=across_sems[0].at[ACROSS.index(name)],
+            recv_sem=across_sems[1].at[ACROSS.index(name)],
+            device_id=device(z, 1 - x, core, y),
+            device_id_type=MESH,
+        )
 
     def gen_copy(piece, target):
         return pltpu.make_async_copy(
@@ -1113,11 +1162,26 @@
         return weight[:, piece * width : (piece + 1) * width].astype(F32)
 
     pieces = [rows_of(attn_qkv, at) for at in range(3)] + [rows_of(attn_out, 0)]
-    pieces += [rows_of(mlp_up, at) for at in range(4)]
-    for at in range(4):
+    for at in (0, 1):
         rows = jnp.concatenate(pieces[2 * at : 2 * at + 2], axis=0).astype(B16)
-        gathered[at // 2, pl.ds(aligned(me * PART + at % 2 * CHUNK), CHUNK), :] = rows
-    gathered[2, pl.ds(aligned(me * PART), PART), :] = mlp_down[...]
+        gathered_attn[pl.ds(aligned(me * PART + at * CHUNK), CHUNK), :] = rows
+
+    def up_half(of_x):
+        group = 4 * PART
+        quarters = [
+            jnp.concatenate([mlp_up[:, at * group : (at + 1) * group] for at in (first, first + 2)], axis=1)
+            for first in (of_x, of_x + 4)
+        ]
+        return jnp.concatenate([quarter.astype(F32) for quarter in quarters], axis=0).astype(B16)
+
+    for of_x in (0, 1):
+
+        @pl.when(x == of_x)
+        def _(of_x=of_x):
+            gathered_up[pl.ds(own_block, CHUNK), :] = up_half(of_x)
+            up_away[...] = up_half(1 - of_x)
+
+    gathered_down[pl.ds(own_block, PART), :] = mlp_down[...]
     hyper_gains = [gain[...].astype(F32).reshape(1, HW) for gain in (hyper_one, hyper_two)]
     code, kept = hyper_forward(
         waves[...], hyper_qkv[...], hyper_out[...], hyper_gains[0], hyper_up[...], hyper_down[...], hyper_gains[1]
@@ -1129,8 +1193,11 @@
         ref[...] = value
 
     def weight_view(part, block, side):
-        where = slot(block[0], block[1], side, block[2])
-        return gathered.at[part, pl.ds(aligned(where * PART), PART)]
+        if part == 0:
+            where = slot(block[0], block[1], side, block[2])
+        else:
+            where = block[0] * 4 + side * 2 + block[2]
+        return gathered[part].at[pl.ds(aligned(where * PART), PART)]
 
     half = tokens // 2
 
@@ -1142,16 +1209,16 @@
 
     def gather_at(known_z=None):
         return Gather(
-            known_z, weight_view, ORDERS, lambda part, count: gathered.at[part, pl.ds(0, count * PART)], *gather_sems
+            known_z, weight_view, ORDERS, lambda part, count: gathered[part].at[pl.ds(0, count * PART)], *gather_sems
         )
 
     def embed_at(known_z=None):
         return Reduce(
             known_z,
             lambda chunk, block: spare.at[pl.ds(aligned(rail_row(block) + chunk * half), half)],
-            ("xz", "xz"),
+            EMBED_ORDERS,
             lambda chunk: residual.at[pl.ds(chunk * half, half)],
-            lambda chunk, where: buf.at[pl.ds((chunk * 9 + where) * half, half)],
+            lambda chunk, where: buf.at[pl.ds((chunk * 11 + where) * half, half)],
             lambda chunk, count: buf.at[pl.ds(0, count * half)],
             *embed_sems,
         )
@@ -1168,8 +1235,8 @@
     for chip in range(8):
         to_pair(0, pixel_rows.at[chip * 2 + 1 - core], pair_pixels.at[chip], front_sems).start()
     to_pair(1, band_scale, pair_scale, front_sems).start()
-    shared("out_grad").start()
-    plan.run()
+    plan.run()
+    across("u").start()
     for part in FIRST_PARTS:
         gather.start(part)
     plan.run()
@@ -1190,9 +1257,11 @@
     )
     spread_kernels.start()
     plan.run()
+    across("u").wait_recv()
     for part in range(3):
         if part not in FIRST_PARTS:
             gather.start(part)
+    across("og").start()
     plan.run()
     kernels[own_rows, :] = sending[own_rows, :]
     biases = dot_nn(code_out[...], bias_gen[...])
@@ -1227,11 +1296,9 @@
     for group in (3, 0, 2, 1):
         plan.run()
         term(group)
-        for chunk in (0, 1):
-            embed.start(chunk, (group, 1, 0))
     plan.run()
     gather.wait_pairs(0)
-    spread(gathered, weights, 0)
+    spread(gathered_attn, weights)
 
     names = dict(
         residual=residual, out_grad=out_grad, gain_one=gains.at[0:1], gain_two=gains.at[1:2], block_out=block_out,
@@ -1239,21 +1306,28 @@
         grad_pre=grad_pre, mixed=mixed, normed_one=normed_one, normed_two=normed_two, unit_one=unit_one,
         unit_two=unit_two, inverse_one=inverse_one, inverse_two=inverse_two, result=residual, grad_normed=grad_normed,
         grad_middle=grad_middle, grad_branch=grad_branch, grad_mixed=grad_mixed, grad_joint=grad_joint,
-        turned=turned, rail_rows=rail_rows, small=small,
-    )
-    block = Block(weights, gathered.at[2], names)
+        turned=turned, small=small, result_x=result_x, grad_x=grad_x, grad_from_x=grad_from_x,
+    )
+    block = Block(weights, gathered_down, names)
     plan.run()
     block.project()
-    shared("normed_one").start()
+    shared("n1").start()
     plan.run()
     block.attend()
-    shared("mixed").start()
+    shared("mx").start()
+    plan.run()
+    block.middle()
+    across("n2").start()
+    across("og").wait_recv()
+    shared("og").start()
     plan.run()
     gather.wait_pairs(1)
-    spread(gathered, weights, 1)
-    plan.run()
+    spread_up(gathered_up, weights, x)
+    plan.run()
+    across("n2").wait_recv()
+    shared("n2").start()
     block.widen()
-    for name in ("normed_two", "act0", "act1", "act2", "act3"):
+    for name in ("a0", "a1"):
         shared(name).start()
     plan.run()
     gather.wait_pairs(2)
@@ -1264,65 +1338,72 @@
     tell_near(front_done)
 
     def part_ref(part):
-        return spare if part == 2 else gathered.at[part]
+        return spare.at[pl.ds(8 * tokens, 8 * PART)] if part == 2 else gathered[part]
 
     def part_view(part, blk):
-        return part_ref(part).at[pl.ds(aligned((blk[0] * 4 + blk[1] * 2 + blk[2]) * PART), PART)]
+        where = blk[0] * 4 + blk[1] * 2 + blk[2] if part == 0 else blk[0] * 2 + blk[2]
+        return part_ref(part).at[pl.ds(aligned(where * PART), PART)]
 
     def reduce_at(known_z=None):
         return Reduce(
             known_z,
             part_view,
             SUM_ORDERS,
-            lambda part: shares.at[pl.ds(part * PART, PART)],
-            lambda part, where: buf.at[pl.ds((part * 19 + where) * PART, PART)],
+            lambda part: up_share if part == 1 else shares.at[pl.ds(part * PART, PART)],
+            lambda part, where: buf.at[pl.ds(((0, 19, 30)[part] + where) * PART, PART)],
             lambda part, count: part_ref(part).at[pl.ds(0, count * PART)],
             *reduce_sems,
         )
 
-    def send_terms(part, planes):
-        for zz in planes:
-            for flips in reduce.flips(part, 0):
-                reduce.start(part, (zz, *flips))
-
-    image_grads = gathered.at[2]
+    def up_send():
+        shares[pl.ds(aligned(PART + x * CHUNK), CHUNK), :] = up_share[:CHUNK]
+        across("s").start()
+
+    def up_take():
+        across("s").wait_recv()
+        shares[pl.ds(aligned(PART + (1 - x) * CHUNK), CHUNK), :] = up_landed[...]
+
+    image_grads = gathered_down
 
     def image_view(chunk, blk, side):
         return image_grads.at[pl.ds(aligned(image_row(blk, side) + chunk * half), half)]
 
     def grads_at(known_z=None):
         return Gather(
-            known_z, image_view, ("zx", "zx"), lambda chunk, count: image_grads.at[pl.ds(0, count * half)], *grads_sems
+            known_z, image_view, IMAGE_ORDERS, lambda chunk, count: image_grads.at[pl.ds(0, count * half)], *grads_sems
         )
 
     def tail_works(known_z):
         known, images = reduce_at(known_z), grads_at(known_z)
         works = [work for part in (2, 1, 0) for work in in_order(known.events((part,)))]
-        return works + [work for chunk in (0, 1) for work in in_order(images.events(chunk))]
+        works += [work for chunk in (0, 1) for work in in_order(images.events(chunk))]
+        return works + [up_send, up_take]
 
     reduce, grads = reduce_at(), grads_at()
     plan = Plan(TAIL_PLAN, [tail_works(known_z) for known_z in range(4)])
     hear_near(front_done)
-    shared("out_grad").wait_recv()
-    for part in (3, 0, 2, 1):
-        plan.run()
-        shared(f"act{part}").wait_recv()
-        block.down_grad(part, core, spare)
-        send_terms(2, (part,))
     plan.run()
     block.back_narrow()
-    for part in range(4):
-        shared(f"pre{part}").start()
+    for part in (0, 1):
+        shared(f"p{part}").start()
+    across("g").start()
+    plan.run()
+    for name in ("og", "a0", "a1"):
+        shared(name).wait_recv()
+    for part in (0, 1):
+        block.down_grad(part, core, rail_two, part_ref(2))
     plan.run()
     block.narrow()
+    across("r").start()
     tell_near(narrow_done)
     plan.run()
+    across("g").wait_recv()
     block.back_wide()
-    shared("grad_branch").start()
+    shared("gb").start()
     plan.run()
     block.back_attend()
     for part in range(3):
-        shared(f"joint{part}").start()
+        shared(f"j{part}").start()
     plan.run()
     block.back_project()
     hear_near(narrow_done)
@@ -1330,31 +1411,38 @@
     grads.start(0)
     grads.start(1)
     plan.run()
-    for name in ("normed_two", "pre0", "pre1", "pre2", "pre3"):
+    for name in ("n2", "p0", "p1"):
         shared(name).wait_recv()
-    block.turn_rail(0, normed_two, core)
-    for part in (0, 2):
-        block.pair_grad(
-            0, 0, lambda cols, part=part: grad_pre[part, :, cols],
-            lambda cols, part=part: grad_pre[part + 1, :, cols], part_ref(1), part // 2 * CHUNK,
-        )
-    send_terms(1, (3, 0, 2, 1))
-    plan.run()
-    for name in ("normed_one", "mixed", "grad_branch", "joint0", "joint1", "joint2"):
+    block.turn_rail(rail_two, normed_two, core)
+
+    def up_place(owner):
+        zz, xx, yy = owner // 4, owner // 2 % 2, owner % 2
+        return aligned((zz * 2 + yy) * PART + ((1 - x) if xx else x) * CHUNK)
+
+    block.pair_grad(
+        rail_two, rail_two, lambda cols: grad_pre[0, :, cols], lambda cols: grad_pre[1, :, cols], part_ref(1), up_place
+    )
+    plan.run()
+    for name in ("n1", "mx", "gb", "j0", "j1", "j2"):
         shared(name).wait_recv()
-    block.turn_rail(0, normed_one, core)
-    block.turn_rail(1, mixed, core)
-    block.pair_grad(0, 0, lambda cols: grad_joint[0, :, cols], lambda cols: grad_joint[1, :, cols], part_ref(0), 0)
+    block.turn_rail(rail_one, normed_one, core)
+    block.turn_rail(rail_mixed, mixed, core)
     block.pair_grad(
-        0, 1, lambda cols: grad_joint[2, :, cols], lambda cols: grad_branch[:, cols], part_ref(0), CHUNK
-    )
-    send_terms(0, (3, 0, 2, 1))
+        rail_one, rail_one, lambda cols: grad_joint[0, :, cols], lambda cols: grad_joint[1, :, cols], part_ref(0),
+        lambda owner: owner * PART,
+    )
+    block.pair_grad(
+        rail_one, rail_mixed, lambda cols: grad_joint[2, :, cols], lambda cols: grad_branch[:, cols], part_ref(0),
+        lambda owner: owner * PART + CHUNK,
+    )
     for name in SHARED:
         shared(name).wait_send()
+    for name in ("og", "n2", "g"):
+        across(name).wait_send()
     for piece in range(16):
         gen_copy(piece, weights).start()
 
-    kernel_total = pre_act.at[0:2]
+    kernel_total = pre_act.at[0]
     kernel_total[...] = jnp.zeros(kernel_total.shape, F32)
     small[2:3, :] = jnp.zeros((1, width), F32)
     near_side = z // 2
@@ -1367,18 +1455,19 @@
         def _(step, side=side):
             group = 2 * side + step
             for image in range(4):
+                half_rows = slice(image % 2 * tokens, (image % 2 + 1) * tokens)
                 rows = pl.ds(aligned((group * 4 + image) * tokens), tokens)
                 scaled = image_grads[rows, :].astype(F32) * band_scale[group * 4 + image][:1, :1]
                 small[2:3, :] += jnp.sum(scaled, axis=0, keepdims=True)
-                act[image, :tokens] = scaled.astype(B16)
-            scaled = act[:, :tokens].reshape(4 * tokens, width)
+                act[image // 2, half_rows] = scaled.astype(B16)
+            scaled = act[:, : 2 * tokens].reshape(4 * tokens, width)
             pixel_rows[pl.ds(group * 4, 4)] = dot_nt(scaled, kernels[...]).astype(B16).reshape(4, tokens, -1)
-            kernel_total[...] += dot_nn(turned_pixels[group], scaled).reshape(kernel_total.shape)
+            kernel_total[...] += dot_nn(turned_pixels[group], scaled)
 
     store_pixels = pltpu.make_async_copy(pixel_rows, pixel_out, pix_sem)
     store_pixels.start()
     spread_kernels.finish()
-    sending[...] = kernel_total[...].astype(B16).reshape(sending.shape)
+    sending[...] = kernel_total[...].astype(B16)
     owner = core == y
 
     def column_copy(target, plane):
@@ -1462,6 +1551,8 @@
     store_pixels.wait()
     store_columns.start()
     plan.run()
+    across("r").wait_recv()
+    block_out[...] = (residual[...] + result_from_x[...].astype(F32)).astype(B16)
     vector_spread.wait()
     vectors[...] = small_all[...]
     bulk = code_all.at[pl.ds(0, bands - 1)]
@@ -1475,6 +1566,8 @@
     plan.run()
     reduce.finish()
     grads.finish()
+    for name in ("u", "r", "s"):
+        across(name).wait_send()
     vec_half.wait_send()
     vector_spread.finish()
 
@@ -1509,6 +1602,7 @@
     shape = jax.ShapeDtypeStruct
     rows = lambda kind, *lead: pltpu.VMEM((*lead, tokens, width), kind)
     pair = lambda *lead: pltpu.VMEM((*lead, 2 * tokens, width), B16)
+    four = lambda *lead: pltpu.VMEM((*lead, 4 * tokens, width), B16)
     dma = pltpu.SemaphoreType.DMA
     code = (bands, HW)
     kept = [(bands, 3 * HW), (HHEADS * bands, bands), code, code, (bands, 1), (bands, hidden), code, (bands, 1), (2, HW)]
@@ -1527,30 +1621,41 @@
         in_specs=[smem] * 2 + [hbm] * 2 + [vmem] * 15,
         out_specs=[vmem, hbm, vmem, hbm] + [vmem] * 12,
         scratch_shapes=[
-            pltpu.VMEM((3, devices * PART, width), B16),
-            pltpu.VMEM((8 * width, width), B16),
+            pltpu.VMEM((devices * PART, width), B16),
+            pltpu.VMEM((devices // 2 * PART, width), B16),
+            pltpu.VMEM((images * tokens, width), B16),
+            pltpu.VMEM((6 * width, width), B16),
             pltpu.VMEM((16 * HW, width), B16),
-            pltpu.VMEM((3 * 19 * PART, width), B16),
+            pltpu.VMEM(((19 + 11 + 11) * PART, width), B16),
             rows(B16, 3),
             pltpu.VMEM((HEADS // 2, 2 * tokens, tokens), F32),
-            rows(F32, 4),
-            pair(4),
-            pair(4),
+            pltpu.VMEM((2, 2 * tokens, width), F32),
+            four(2),
+            four(2),
+            four(),
             pair(),
             pair(),
-            pair(),
-            pair(),
+            four(),
             rows(F32),
             rows(F32),
             pltpu.VMEM((tokens, 128), F32),
             pltpu.VMEM((tokens, 128), F32),
-            rows(F32),
+            pltpu.VMEM((2 * tokens, width), F32),
             rows(F32),
             pair(),
             rows(B16),
             pair(3),
-            pltpu.VMEM((width, 2 * tokens), B16),
-            pltpu.VMEM((2, width // 2, 2 * tokens), B16),
+            pltpu.VMEM((width, 4 * tokens), B16),
+            pltpu.VMEM((width // 2, 2 * tokens), B16),
+            pltpu.VMEM((width // 2, 2 * tokens), B16),
+            pltpu.VMEM((width // 2, 4 * tokens), B16),
+            pltpu.VMEM((CHUNK, width), B16),
+            pltpu.VMEM((PART, width), F32),
+            pltpu.VMEM((CHUNK, width), F32),
+            rows(B16),
+            rows(B16),
+            rows(B16),
+            rows(B16),
             rows(F32),
             pltpu.VMEM(pixels.shape, B16),
             pltpu.VMEM((4, pix, 4 * tokens), B16),
@@ -1576,8 +1681,9 @@
             *[dma((3, 3)), dma((3, 16)), dma((3, 2)), dma((3, 2))],
             *[dma((2, 3)), dma((2, 16)), dma((2, 2)), dma((2, 2))],
             *[dma((3, 3)), dma((3, 19))],
-            *[dma((2, 2)), dma((2, 9))],
+            *[dma((2, 2)), dma((2, 11))],
             *[dma((len(SHARED),))] * 2,
+            *[dma((len(ACROSS),))] * 2,
             *[dma((3,))] * 2,
             *[dma((1,))] * 12,
         ],
@@ -1589,7 +1695,7 @@
 
 
 def finish_kernel(*refs):
-    count = 13 + len(KEPT)
+    count = 13 + KEPT
     outside = refs[:count]
     (block_out, pixel_out, grad_qkv, grad_out, grad_gain_one, grad_up, grad_down, grad_gain_two, grad_gen, grad_bias,
      gain_one_sum, gain_two_sum, share_qkv, share_out, share_up, share_down, *scratch) = refs[count:]
@@ -1600,33 +1706,36 @@
     (code_low, columns, shares, waves, hyper_qkv, hyper_out, hyper_up, hyper_down, bias_gen, code_grads, vectors,
      *kept_refs, hyper_gains, block_in, pixel_in) = inside
     width = bias_gen.shape[1]
+    copies = [
+        pltpu.make_async_copy(block_in, block_out, copy_sem.at[0]),
+        pltpu.make_async_copy(pixel_in, pixel_out, copy_sem.at[1]),
+    ]
     for load in loads[:2]:
         load.wait()
     code = code_low[...]
     swapped = swap_rows(columns[...])
     gen_copies = []
     for piece in range(16):
-        slot_at = piece % store.shape[0]
-        if piece >= store.shape[0]:
-            gen_copies[piece - store.shape[0]].wait()
-        store[slot_at] = dot_tn(code, swapped[piece * 16 : (piece + 1) * 16])
+        store[piece] = dot_tn(code, swapped[piece * 16 : (piece + 1) * 16])
         gen_copies.append(
             pltpu.make_async_copy(
-                store.at[slot_at], grad_gen.at[:, pl.ds(piece * width, width)], gen_sem.at[slot_at]
+                store.at[piece], grad_gen.at[:, pl.ds(piece * width, width)], gen_sem.at[piece]
             )
         )
         gen_copies[-1].start()
     for load in loads[2:]:
         load.wait()
-    copies = [
-        pltpu.make_async_copy(block_in, block_out, copy_sem.at[0]),
-        pltpu.make_async_copy(pixel_in, pixel_out, copy_sem.at[1]),
-    ]
     for copy in copies:
         copy.start()
     share_qkv[...] = jnp.concatenate([shares[at * 24 : at * 24 + 24, :] for at in range(3)], axis=1)
     share_out[...] = shares[72:96, :]
-    share_up[...] = jnp.concatenate([shares[at * 24 : at * 24 + 24, :] for at in range(4, 8)], axis=1)
+    group = 4 * PART
+    up_pieces = []
+    for at in range(8):
+        z_of, x_of = at // 2, at % 2
+        row = PART + x_of * CHUNK + z_of // 2 * 24
+        up_pieces.append(shares[row : row + 24, z_of % 2 * group : (z_of % 2 + 1) * group])
+    share_up[...] = jnp.concatenate(up_pieces, axis=1)
     share_down[...] = shares[192:288, :]
     sums = jnp.sum(vectors[...], axis=0)
     gain_one_sum[...] = sums[0]
@@ -1640,7 +1749,7 @@
     )
     for ref, value in zip((grad_qkv, grad_out, grad_gain_one, grad_up, grad_down, grad_gain_two), grads):
         ref[...] = value
-    for copy in copies + gen_copies[-store.shape[0] :]:
+    for copy in copies + gen_copies:
         copy.wait()
 
 
@@ -1665,10 +1774,10 @@
         out_specs=[hbm, hbm] + [vmem] * 6 + [hbm] + [vmem] * 7,
         scratch_shapes=[
             *[pltpu.VMEM(operand.shape, operand.dtype) for operand in operands],
-            pltpu.VMEM((4, HW, width), F32),
+            pltpu.VMEM((16, HW, width), F32),
             pltpu.SemaphoreType.DMA((len(operands),)),
             pltpu.SemaphoreType.DMA((2,)),
-            pltpu.SemaphoreType.DMA((4,)),
+            pltpu.SemaphoreType.DMA((16,)),
         ],
         compiler_params=pltpu.CompilerParams(vmem_limit_bytes=VMEM_BYTES),
         name="finish",

time: 183 us -> 152 us (0.83)
  Pallas kernels: 179 us -> 150 us
    pallas_call x1, Pallas kernels: 170 us -> 143 us  [layer(): pl.pallas_call(layer_kernel, out_shape=[shape((tokens, width), B16), shap...]
    pallas_call x1, Pallas kernels: 9.18 us -> 6.81 us  [finish(): pl.pallas_call(finish_kernel, out_shape=[jax.ShapeDtypeStruct(block_out.s...]
where the time goes in v6:
time: 152 us
  Pallas kernels  150 us (99%)
    pallas_call x1, Pallas kernels, layer(): pl.pallas_call(layer_kernel, out_shape=[shape((tokens, width), B16), shap...  143 us
    pallas_call x1, Pallas kernels, finish(): pl.pallas_call(finish_kernel, out_shape=[jax.ShapeDtypeStruct(block_out.s...  6.81 us

profile of v6, /device:TPU:0, one launch (start us, length us, event | category | flops | bytes accessed | tf_op | source)
XLA Modules:
  0.0 151.7 jit_solution(7739778571765194623)
XLA Ops:
  0.6 0.7 convert_element_type.10
  1.3 0.7 fusion.refs_8_.refs_3_
  2.0 142.7 %layer.1 = (bf16[128,768]{1,0:T(8,128)(2,1)}, bf16[16,128,256]{2,1,0:T(8,128)(2,1)}, f32[288,768]{1,0:T(8,128)}, bf16[256,768]{1,0:T(8,128)(2,1)}, bf16[16,128]{...) custom-call(s32[16]{0:T(128)} %bitcast.12, ...), custom_call_target="tpu_custom_call" | custom-call | tf_op jit(solution)/shard_map/layer/pallas_call | solution.py:1609
  144.7 6.8 %finish.1 = (bf16[128,768]{1,0:T(8,128)(2,1)}, bf16[16,128,256]{2,1,0:T(8,128)(2,1)}, f32[128,384]{1,0:T(8,128)}, f32[128,128]{1,0:T(8,128)}, f32[1,128]{1,0:T(1...) custom-call(bf16[16,128]{1,0:T(8,128)(2,1)} %get-tuple-element.48.re, ...), custom_call_target="tpu_custom_call" | custom-call | tf_op jit(solution)/shard_map/finish/pallas_call | solution.py:1764
  (2 shorter events, 0.0 us)

commit v7 on v6

--- a/solution.py
+++ b/solution.py
@@ -7,6 +7,7 @@
 from jax.experimental import pallas as pl
 from jax.experimental.pallas import tpu as pltpu
 from jax.sharding import PartitionSpec as P
+import numpy as np
 
 HEADS = 12
 HEAD_DIM = 64
@@ -353,8 +354,13 @@
         self.pair_send, self.pair_recv = pair_send, pair_recv
         self.z, self.x, self.core, self.y = place(known_z)
 
-    def rail(self, block):
-        return block[0] * 4 + block[1] * 2 + block[2]
+    def place_of(self, chunk, block):
+        order = self.orders[chunk]
+        place = block[0]
+        for dim, at in (("x", block[1]), ("y", block[2])):
+            if dim in order:
+                place = place * 2 + at
+        return sum(self.rails(before) for before in range(chunk)) + place
 
     def sibling(self):
         return device(self.z, self.x, 1 - self.core, self.y)
@@ -379,7 +385,7 @@
                 src_ref=src,
                 dst_ref=src,
                 send_sem=self.send_sem.at[chunk, DIMS.index(dim)],
-                recv_sem=self.recv_sem.at[chunk, self.rail(block)],
+                recv_sem=self.recv_sem.at[self.place_of(chunk, block)],
                 device_id=target,
                 device_id_type=MESH,
             )
@@ -442,7 +448,7 @@
             src_ref=src,
             dst_ref=src,
             send_sem=self.send_sem.at[chunk, 0],
-            recv_sem=self.recv_sem.at[chunk, self.rail(block)],
+            recv_sem=self.recv_sem.at[self.place_of(chunk, block)],
             device_id=self.sibling(),
             device_id_type=MESH,
         )
@@ -485,7 +491,7 @@
             for dim in self.orders[chunk]:
                 send_sem = self.send_sem.at[chunk, DIMS.index(dim)]
                 for cond, z in ((ends, 0), (inner, 1)):
-                    copy = bulk_copy(self.bulk(chunk, self.sent(chunk, z, dim)), send_sem, self.recv_sem.at[chunk, 0])
+                    copy = bulk_copy(self.bulk(chunk, self.sent(chunk, z, dim)), send_sem, self.recv_sem.at[0])
                     when(cond, copy.wait_send)
             every = self.bulk(chunk, self.rails(chunk) // 2)
             for side in (0, 1):
@@ -499,6 +505,7 @@
         self.send_sem, self.recv_sem = send, recv
         self.z, self.x, self.core, self.y = place(known_z)
         self.index = [self.places(chunk) for chunk in range(len(orders))]
+        self.first = [sum(len(index) for index in self.index[:chunk]) for chunk in range(len(orders))]
 
     def coords(self, block):
         zz, flip_x, flip_y = block
@@ -543,7 +550,7 @@
             src_ref=self.own(chunk, block),
             dst_ref=self.buf(chunk, where),
             send_sem=self.send_sem.at[chunk, key[0]],
-            recv_sem=self.recv_sem.at[chunk, where],
+            recv_sem=self.recv_sem.at[self.first[chunk] + where],
             device_id=target,
             device_id_type=MESH,
         )
@@ -558,7 +565,7 @@
             src_ref=landed,
             dst_ref=landed,
             send_sem=self.send_sem.at[chunk, 0],
-            recv_sem=self.recv_sem.at[chunk, self.place_of(chunk, key)],
+            recv_sem=self.recv_sem.at[self.first[chunk] + self.place_of(chunk, key)],
             device_id=self.sibling(),
             device_id_type=MESH,
         ).wait_recv()
@@ -684,7 +691,7 @@
                 after = len(self.flips(chunk, stage + 1)) if stage + 1 < len(order) else 1
                 count = 3 * after if dim == "z" else after * (4 if "z" in order[stage + 1 :] else 1)
                 every = self.bulk(chunk, count)
-                bulk_copy(every, self.send_sem.at[chunk, stage], self.recv_sem.at[chunk, 0]).wait_send()
+                bulk_copy(every, self.send_sem.at[chunk, stage], self.recv_sem.at[0]).wait_send()
 
 
 class Exchange:
@@ -1062,14 +1069,14 @@
     return ref.at[pl.ds(aligned(index * 16), 16)]
 
 
-KEPT = 9
+KEPT = 10
 SHARED = ("og", "n1", "mx", "n2", "a0", "a1")
 SHARED += ("p0", "p1", "gb", "j0", "j1", "j2")
 ACROSS = ("u", "og", "n2", "r", "g", "s")
 
 
 def layer_kernel(*refs):
-    (counts, mask, pixels, kernel_gen, attn_qkv, attn_out, mlp_up, mlp_down, waves, hyper_qkv, hyper_out, hyper_one, hyper_two,
+    (counts, mask, wavelengths, pixels, kernel_gen, attn_qkv, attn_out, mlp_up, mlp_down, frequency, hyper_qkv, hyper_out, hyper_one, hyper_two,
      hyper_up, hyper_down, bias_gen, out_grad_in, norm_one, norm_two,
      block_out, pixel_out, shares, kernel_grads, code_out, code_grads, vectors, *rest_refs) = refs
     kept_refs, rest_refs = rest_refs[: KEPT], rest_refs[KEPT :]
@@ -1183,10 +1190,14 @@
 
     gathered_down[pl.ds(own_block, PART), :] = mlp_down[...]
     hyper_gains = [gain[...].astype(F32).reshape(1, HW) for gain in (hyper_one, hyper_two)]
+    lengths = [jnp.full((1, HW), wavelengths[at], jnp.int32) for at in range(bands)]
+    angles = jnp.concatenate(lengths, axis=0).astype(F32) * frequency[...]
+    lane = lax.broadcasted_iota(jnp.int32, angles.shape, 1)
+    waves = jnp.where(lane < HW // 2, jnp.sin(angles), jnp.cos(angles))
     code, kept = hyper_forward(
-        waves[...], hyper_qkv[...], hyper_out[...], hyper_gains[0], hyper_up[...], hyper_down[...], hyper_gains[1]
-    )
-    kept = (*kept, jnp.concatenate(hyper_gains, axis=0))
+        waves, hyper_qkv[...], hyper_out[...], hyper_gains[0], hyper_up[...], hyper_down[...], hyper_gains[1]
+    )
+    kept = (*kept, jnp.concatenate(hyper_gains, axis=0), waves)
     code_low = code.astype(B16)
     code_out[...] = code_low
     for ref, value in zip(kept_refs, kept):
@@ -1554,7 +1565,8 @@
     across("r").wait_recv()
     block_out[...] = (residual[...] + result_from_x[...].astype(F32)).astype(B16)
     vector_spread.wait()
-    vectors[...] = small_all[...]
+    store_vectors = pltpu.make_async_copy(small_all, vectors, gen_sem)
+    store_vectors.start()
     bulk = code_all.at[pl.ds(0, bands - 1)]
     pl.when(owner)(bulk_copy(bulk, code_sems[0].at[0], code_sems[1].at[0]).wait_recv)
     bulk = code_all.at[pl.ds(0, bands)]
@@ -1585,12 +1597,13 @@
         bulk_copy(sent, cols_sems[0].at[0], cols_sems[1].at[0]).wait_send()
 
     store_columns.wait()
+    store_vectors.wait()
 
 
 VMEM_BYTES = 63 * 2**20
 
 
-def layer(counts, mask, pixels, kernel_gen, weights, waves, hyper, bias_gen, out_grad, gains):
+def layer(counts, mask, wavelengths, pixels, kernel_gen, weights, frequency, hyper, bias_gen, out_grad, gains):
     width = bias_gen.shape[1]
     bands = lax.axis_size("band")
     devices = bands * lax.axis_size("dp")
@@ -1605,7 +1618,7 @@
     four = lambda *lead: pltpu.VMEM((*lead, 4 * tokens, width), B16)
     dma = pltpu.SemaphoreType.DMA
     code = (bands, HW)
-    kept = [(bands, 3 * HW), (HHEADS * bands, bands), code, code, (bands, 1), (bands, hidden), code, (bands, 1), (2, HW)]
+    kept = [(bands, 3 * HW), (HHEADS * bands, bands), code, code, (bands, 1), (bands, hidden), code, (bands, 1), (2, HW), code]
     return pl.pallas_call(
         layer_kernel,
         out_shape=[
@@ -1618,8 +1631,8 @@
             shape((bands, 8, width), F32),
             *[shape(dims, F32) for dims in kept],
         ],
-        in_specs=[smem] * 2 + [hbm] * 2 + [vmem] * 15,
-        out_specs=[vmem, hbm, vmem, hbm] + [vmem] * 12,
+        in_specs=[smem] * 3 + [hbm] * 2 + [vmem] * 15,
+        out_specs=[vmem, hbm, vmem, hbm, vmem, vmem, hbm] + [vmem] * KEPT,
         scratch_shapes=[
             pltpu.VMEM((devices * PART, width), B16),
             pltpu.VMEM((devices // 2 * PART, width), B16),
@@ -1678,10 +1691,10 @@
             dma,
             pltpu.SemaphoreType.REGULAR,
             pltpu.SemaphoreType.REGULAR,
-            *[dma((3, 3)), dma((3, 16)), dma((3, 2)), dma((3, 2))],
-            *[dma((2, 3)), dma((2, 16)), dma((2, 2)), dma((2, 2))],
-            *[dma((3, 3)), dma((3, 19))],
-            *[dma((2, 2)), dma((2, 11))],
+            *[dma((3, 3)), dma((32,)), dma((3, 2)), dma((3, 2))],
+            *[dma((2, 3)), dma((16,)), dma((2, 2)), dma((2, 2))],
+            *[dma((3, 3)), dma((37,))],
+            *[dma((2, 2)), dma((20,))],
             *[dma((len(SHARED),))] * 2,
             *[dma((len(ACROSS),))] * 2,
             *[dma((3,))] * 2,
@@ -1691,11 +1704,11 @@
             collective_id=0, has_side_effects=True, vmem_limit_bytes=VMEM_BYTES
         ),
         name="layer",
-    )(counts, mask, pixels, kernel_gen, *weights, waves, *hyper, bias_gen, out_grad, *gains)
+    )(counts, mask, wavelengths, pixels, kernel_gen, *weights, frequency, *hyper, bias_gen, out_grad, *gains)
 
 
 def finish_kernel(*refs):
-    count = 13 + KEPT
+    count = 12 + KEPT
     outside = refs[:count]
     (block_out, pixel_out, grad_qkv, grad_out, grad_gain_one, grad_up, grad_down, grad_gain_two, grad_gen, grad_bias,
      gain_one_sum, gain_two_sum, share_qkv, share_out, share_up, share_down, *scratch) = refs[count:]
@@ -1703,8 +1716,8 @@
     loads = [pltpu.make_async_copy(*pair, in_sem.at[at]) for at, pair in enumerate(zip(outside, inside))]
     for load in loads:
         load.start()
-    (code_low, columns, shares, waves, hyper_qkv, hyper_out, hyper_up, hyper_down, bias_gen, code_grads, vectors,
-     *kept_refs, hyper_gains, block_in, pixel_in) = inside
+    (code_low, columns, shares, hyper_qkv, hyper_out, hyper_up, hyper_down, bias_gen, code_grads, vectors,
+     *kept_refs, hyper_gains, waves, block_in, pixel_in) = inside
     width = bias_gen.shape[1]
     copies = [
         pltpu.make_async_copy(block_in, block_out, copy_sem.at[0]),
@@ -1753,14 +1766,14 @@
         copy.wait()
 
 
-def finish(waves, hyper, bias_gen, code_low, code_grads, vectors, columns, shares, block_out, pixel_grad, kept, kernel_gen, weights):
+def finish(hyper, bias_gen, code_low, code_grads, vectors, columns, shares, block_out, pixel_grad, kept, kernel_gen, weights):
     width = bias_gen.shape[1]
     vmem = pl.BlockSpec(memory_space=pltpu.VMEM)
     hbm = pl.BlockSpec(memory_space=pl.ANY)
     shape = lambda array: jax.ShapeDtypeStruct(array.shape, F32)
     line = jax.ShapeDtypeStruct((1, HW), F32)
     weights_in = (hyper[0], hyper[1], hyper[4], hyper[5])
-    operands = (code_low, columns, shares, waves, *weights_in, bias_gen, code_grads, vectors, *kept, block_out, pixel_grad)
+    operands = (code_low, columns, shares, *weights_in, bias_gen, code_grads, vectors, *kept, block_out, pixel_grad)
     return pl.pallas_call(
         finish_kernel,
         out_shape=[
@@ -1999,26 +2012,24 @@
     mlp_down,
     out_grad,
 ):
-    lane = jnp.arange(HW)
-    frequency = jnp.power(10000.0, -(lane % (HW // 2)).astype(F32) / (HW // 2))
-    angles = wavelengths.astype(F32)[:, None] * frequency[None, :]
-    waves = jnp.where(lane < HW // 2, jnp.sin(angles), jnp.cos(angles))
+    half = np.arange(HW) % (HW // 2)
+    frequency = jnp.power(10000.0, jnp.asarray(-half / (HW // 2), F32))[None]
     weights = (attn_qkv, attn_out, mlp_up, mlp_down)
     hyper = (hyper_qkv, hyper_out, hyper_gain1, hyper_gain2, hyper_up, hyper_down)
     block_out, pixel_grad, shares, columns, code_low, code_grads, vectors, *kept = layer(
         band_counts[0],
         band_mask[0, :, 0],
+        wavelengths,
         pixels[0, :, :, 0],
         kernel_gen,
         weights,
-        waves,
+        frequency,
         hyper,
         bias_gen,
         out_grad[0, 0],
         (norm_gain1, norm_gain2),
     )
     outs = finish(
-        waves,
         hyper,
         bias_gen,
         code_low,

time: 152 us -> 151 us (level)
  no operation moved by 1% of the time
where the time goes in v7:
time: 151 us; the launch traced here: 150 us
  Pallas kernels  149 us (99%)
    pallas_call x1, Pallas kernels, layer(): pl.pallas_call(layer_kernel, out_shape=[shape((tokens, width), B16), shap...  142 us
    pallas_call x1, Pallas kernels, finish(): pl.pallas_call(finish_kernel, out_shape=[jax.ShapeDtypeStruct(block_out.s...  6.81 us

profile of v7, /device:TPU:0, one launch (start us, length us, event | category | flops | bytes accessed | tf_op | source)
XLA Modules:
  0.0 149.8 jit_solution(2581433022501065927)
XLA Ops:
  0.7 142.2 %layer.1 = (bf16[128,768]{1,0:T(8,128)(2,1)}, bf16[16,128,256]{2,1,0:T(8,128)(2,1)}, f32[288,768]{1,0:T(8,128)}, bf16[256,768]{1,0:T(8,128)(2,1)}, bf16[16,128]{...) custom-call(s32[16]{0:T(128)} %bitcast.12, ...), custom_call_target="tpu_custom_call" | custom-call | tf_op jit(solution)/shard_map/layer/pallas_call | solution.py:1622
  142.9 6.8 %finish.1 = (bf16[128,768]{1,0:T(8,128)(2,1)}, bf16[16,128,256]{2,1,0:T(8,128)(2,1)}, f32[128,384]{1,0:T(8,128)}, f32[128,128]{1,0:T(8,128)}, f32[1,128]{1,0:T(1...) custom-call(bf16[16,128]{1,0:T(8,128)(2,1)} %get-tuple-element.49.re, ...), custom_call_target="tpu_custom_call" | custom-call | tf_op jit(solution)/shard_map/finish/pallas_call | solution.py:1777

commit v8 on v7

--- a/solution.py
+++ b/solution.py
@@ -184,10 +184,10 @@
         (4, 6),
         (),
         (5,),
-        (18, 21, 24, 27, 30, 33, 7, 70, 71, 11),
-        (83, 84, 39, 40, 41, 42, 43, 77, 44, 45, 46, 10, 14, 73, 90, 86, 47),
-        (79, 76, 92, 48, 89, 49, 53, 50, 16, 17, 81, 51, 94),
-        (54, 32, 34, 52, 57, 36, 59, 60, 58, 62, 61, 65),
+        (18, 21, 24, 70, 71, 27, 30, 33, 7, 83, 84, 11, 10, 14, 73, 77),
+        (90, 86, 39, 40, 41, 79, 42, 43, 44, 76, 45, 46),
+        (92, 89, 81, 47, 48, 94, 50),
+        (49, 53, 16, 17, 51, 32, 34, 52, 54, 57, 36, 58, 62, 59, 60, 61, 65),
         (),
         (38, 95, 96, 67, 68),
         (),
@@ -200,13 +200,13 @@
         (4,),
         (),
         (5,),
-        (8, 7),
-        (70, 71, 69, 83, 84, 82, 39, 40, 41, 42, 43, 44, 45, 46, 10, 19, 73, 77, 86, 74, 47, 22, 90, 13, 48, 25, 87),
-        (79, 92, 26, 50, 28, 29, 51, 31),
-        (49, 54, 35, 32, 34, 52, 57, 12, 36, 59, 15, 58, 60, 55, 61),
-        (16, 17, 38, 95),
-        (64, 63, 96, 66, 67, 68),
-        (),
+        (8, 7, 70, 71, 69),
+        (83, 84, 82, 77, 39, 40, 41, 73, 74, 42, 43, 44, 45, 86, 90, 46, 10, 19, 22, 87, 47, 25, 79),
+        (92, 48, 13, 28, 50, 26, 49, 31),
+        (51, 29, 35, 52, 54, 32, 34, 12, 57, 36, 15, 59, 58, 60, 61),
+        (55, 16, 17, 38, 95, 63),
+        (66, 96, 64),
+        (67, 68),
     ),
     (
         (),
@@ -217,11 +217,11 @@
         (),
         (5,),
         (7,),
-        (69, 70, 71, 82, 83, 84, 39, 40, 41, 42, 43, 44, 45, 46, 10, 9, 74, 12, 72, 77, 47, 20, 85, 87, 48, 23, 90, 25),
-        (78, 50, 26, 28, 49, 51, 29, 31, 91, 54),
-        (32, 34, 35, 52, 57, 36, 58, 59, 16, 60, 13, 61, 56, 15, 17),
-        (63, 38, 95),
-        (67, 96, 64, 66, 68),
+        (69, 70, 71, 82, 83, 84, 39, 40, 41, 42, 43, 74, 44, 45, 46, 10, 72, 77, 9, 12, 85, 87, 20, 47, 23, 90, 48),
+        (78, 91, 26, 25, 50, 29, 28, 51, 49),
+        (32, 31, 34, 54, 52, 36, 35, 57, 16, 59, 13, 60, 58, 61, 15, 17),
+        (38, 95, 56),
+        (67, 63, 64, 96, 66, 68),
         (),
     ),
     (
@@ -232,10 +232,10 @@
         (4,),
         (),
         (5, 6),
-        (18, 21, 24, 27, 30, 33, 69, 71, 7, 14),
-        (82, 84, 39, 40, 41, 42, 74, 43, 44, 45, 46, 10, 72, 11, 87, 85, 47),
-        (78, 15, 17, 91, 48, 75, 49, 50, 88, 80, 51, 31, 34, 52, 53, 54, 35, 93),
-        (57, 58, 65, 59, 60, 38, 95, 61, 62, 96),
+        (18, 21, 69, 71, 24, 27, 30, 33, 7, 82, 84, 14, 10, 11, 74),
+        (72, 87, 39, 85, 40, 41, 42, 43, 44, 45, 46),
+        (78, 75, 91, 47, 15, 17, 48, 80, 88, 50, 49, 51, 93, 31, 34),
+        (54, 52, 53, 35, 57, 59, 60, 58, 65, 38, 95, 61, 62, 96),
         (),
         (66, 68),
         (),

time: 151 us -> 150 us (level)
  no operation moved by 1% of the time
where the time goes in v8:
time: 150 us
  Pallas kernels  149 us (99%)
    pallas_call x1, Pallas kernels, layer(): pl.pallas_call(layer_kernel, out_shape=[shape((tokens, width), B16), shap...  142 us
    pallas_call x1, Pallas kernels, finish(): pl.pallas_call(finish_kernel, out_shape=[jax.ShapeDtypeStruct(block_out.s...  6.81 us

profile of v8, /device:TPU:0, one launch (start us, length us, event | category | flops | bytes accessed | tf_op | source)
XLA Modules:
  0.0 149.8 jit_solution(12616512091420508298)
XLA Ops:
  0.7 142.2 %layer.1 = (bf16[128,768]{1,0:T(8,128)(2,1)}, bf16[16,128,256]{2,1,0:T(8,128)(2,1)}, f32[288,768]{1,0:T(8,128)}, bf16[256,768]{1,0:T(8,128)(2,1)}, bf16[16,128]{...) custom-call(s32[16]{0:T(128)} %bitcast.12, ...), custom_call_target="tpu_custom_call" | custom-call | tf_op jit(solution)/shard_map/layer/pallas_call | solution.py:1622
  142.9 6.8 %finish.1 = (bf16[128,768]{1,0:T(8,128)(2,1)}, bf16[16,128,256]{2,1,0:T(8,128)(2,1)}, f32[128,384]{1,0:T(8,128)}, f32[128,128]{1,0:T(8,128)}, f32[1,128]{1,0:T(1...) custom-call(bf16[16,128]{1,0:T(8,128)(2,1)} %get-tuple-element.49.re, ...), custom_call_target="tpu_custom_call" | custom-call | tf_op jit(solution)/shard_map/finish/pallas_call | solution.py:1777
